TPU v7x, 256 devices: a whole 4x4x8 slice. The times are simulated.
256 devices in a mesh: dp: 32 (over y_lo, z, core), fsdp: 8 (over y_hi, x).
Axes of the slice: x: 4, y: 4 (y_hi: 2, y_lo: 2; y = y_hi * 2 + y_lo), z: 8, core: 2. Of those that a mesh axis runs over, the one named last changes fastest.
Arguments:
- activations: bfloat16 [4096, 8192], P('dp', 'fsdp'), may hold values from -6 to 6
- projector: bfloat16 [8192, 1024], P('fsdp'), may hold values from -0.0625 to 0.0625
- out_grad: bfloat16 [4096, 8, 3584], P('dp', 'fsdp'), may hold values from -0.1875 to 0.1875
- first_moment: float32 [8, 3584, 1024], P('fsdp', 'dp'), may hold values from -4 to 4
- second_moment: float32 [8, 3584, 1024], P('fsdp', 'dp'), may hold values from 0.002 to 0.05
Outputs:
- weight_update: bfloat16 [8, 3584, 8192], P(None, 'dp', 'fsdp')
- first_new: float32 [8, 3584, 1024], P('fsdp', 'dp')
- second_new: float32 [8, 3584, 1024], P('fsdp', 'dp')
All inputs are finite; a program needn't handle non-finite values.
Results may differ from a plain program's by a relative error of at most 0.0051.
Values may be sent and summed in bfloat16 or wider, within the bound.
No kernel may reach another device: no remote copies, remote signals or barrier semaphores. Data moves between devices by JAX's collectives and lax.ppermute only.
A program may use at most 128 MiB of HBM per device.

v0:
```python
import jax
import jax.numpy as jnp
from jax import lax
from jax.sharding import PartitionSpec as P

bias_first = 1.0 - 0.9**20
bias_second = 1.0 - 0.999**20
epsilon = 1e-08


def shards(activations, projector, out_grad, first_moment, second_moment):
    partial_value = jnp.dot(activations, projector, preferred_element_type=jnp.float32)
    projected = lax.psum(partial_value, "fsdp").astype(jnp.bfloat16)
    tok_rows = out_grad.shape[0]
    group_width = out_grad.shape[2]
    flat_grad = out_grad.reshape(tok_rows, group_width)
    owner_cols = first_moment.shape[1]
    rank_width = projector.shape[1]
    gradient = lax.psum_scatter(
        lax.dot_general(
            flat_grad, projected, (((0,), (0,)), ((), ())), preferred_element_type=jnp.float32
        ),
        "dp",
        scatter_dimension=0,
        tiled=True,
    )
    gradient = gradient.reshape(1, owner_cols, rank_width)
    first_new = 0.9 * first_moment + 0.1 * gradient
    second_new = 0.999 * second_moment + 0.001 * gradient * gradient
    direction = (first_new / bias_first / (jnp.sqrt(second_new / bias_second) + epsilon)).astype(
        jnp.bfloat16
    )
    product = lax.dot_general(
        lax.all_gather(direction, "fsdp", axis=0, tiled=True),
        projector,
        (((2,), (1,)), ((), ())),
        preferred_element_type=jnp.float32,
    )
    weight_update = product.astype(jnp.bfloat16)
    return (weight_update, first_new, second_new)


def solution(mesh):
    in_specs = (
        P("dp", "fsdp"),
        P("fsdp", None),
        P("dp", "fsdp", None),
        P("fsdp", "dp", None),
        P("fsdp", "dp", None),
    )
    out_specs = (P(None, "dp", "fsdp"), P("fsdp", "dp", None), P("fsdp", "dp", None))
    return jax.shard_map(shards, mesh=mesh, in_specs=in_specs, out_specs=out_specs, check_vma=False)
```

profile of v0, /device:TPU:64, one launch (start us, length us, event | category | flops | bytes accessed | tf_op | source)
XLA Modules:
  0.0 291.3 jit_solution(6581435398504558334)
XLA Ops:
  7.2 0.0 copy-start
  7.2 0.0 reduce-scatter.4.cloned.1.call-start
  7.2 1.5 copy-done
  8.8 1.4 fusion.10
  10.2 48.1 %all-reduce.1 = bf16[128,1024]{1,0:T(8,128)(2,1)S(1)} all-reduce(f32[128,1024]{1,0:T(8,128)S(1)} %fusion.10), channel_id=1, replica_groups=mesh['dp'=32,'fsdp'=8] {'fsdp'}, use_global_device_ids=true, to_apply=%region_0.0 | all-reduce | flops 131072 | bytes 786432 | tf_op jit(solution)/shard_map/psum | solution.py:13
  58.2 8.4 %convolution_bitcast_fusion = f32[3584,1024]{0,1:T(8,128)} fusion(bf16[128,1,3584]{2,0,1:T(8,128)(2,1)} %param.7, bf16[128,1024]{1,0:T(8,128)(2,1)S(1)} %all-reduce.1), kind=kOutput, calls=%fused_computation | convolution fusion | flops 939524096 | bytes 15859712 | tf_op jit(solution)/shard_map/dot_general | solution.py:20
  66.7 15.3 %copy.18 = f32[3584,1024]{1,0:T(8,128)} copy(f32[3584,1024]{0,1:T(8,128)} %convolution_bitcast_fusion) | data formatting | bytes 29360128
  82.0 0.0 copy-start.1
  82.0 0.0 copy-start.2
  82.0 0.0 reduce-scatter.4.cloned.1.call-update
  82.0 0.0 all-gather.2.cloned.1.call-start
  82.1 0.9 copy-done.1
  83.0 1.0 copy.13
  84.0 0.0 copy-done.2
  84.1 1.0 copy.14
  85.1 126.9 %reduce-scatter.4.cloned.1.call-done = f32[112,1024]{1,0:T(8,128)} async-done(((f32[3584,1024]{1,0:T(8,128)}), f32[112,1024]{1,0:T(8,128)}) %reduce-scatter.4.cloned.1.call-update) | async-done | bytes 458768
  212.0 2.0 copy.19
  214.0 1.7 divide_convert_fusion
  215.7 0.8 copy.15
  216.5 0.0 all-gather.2.cloned.1.call-update
  216.5 1.0 copy.16
  217.5 1.0 copy.17
  218.5 61.2 %all-gather.2.cloned.1.call-done = bf16[8,112,1024]{2,1,0:T(8,128)(2,1)} async-done(((bf16[1,112,1024]{2,1,0:T(8,128)(2,1)}), bf16[8,112,1024]{2,1,0:T(8,128)(2,1)}) %all-gather.2.cloned.1.call-update) | async-done | bytes 1835024 | tf_op jit(solution)/shard_map/all_gather | solution.py:34
  279.7 4.8 %fusion.2 = bf16[8,112,1024]{2,1,0:T(8,128)(2,1)} fusion(bf16[8,112,1024]{2,1,0:T(8,128)(2,1)} %all-gather.2.cloned.1.call-done, bf16[1024,1024]{1,0:T(8,128)(2,1)S(1)} %copy-done), kind=kOutput, calls=%fused_computation.3 | convolution fusion | flops 1879965696 | bytes 5767168 | tf_op jit(solution)/shard_map/dot_general | solution.py:33
Async XLA Ops:
  7.2 1.6 copy-start
  7.2 204.8 %reduce-scatter.4.cloned.1.call-start = ((), (), s32[]{:S(2)}) async-start(), calls=%async_computation.2 | async-start | bytes 15138816
  82.0 1.0 copy-start.1
  82.0 2.0 copy-start.2
  82.0 197.6 %all-gather.2.cloned.1.call-start = ((), (), s32[]{:S(2)}) async-start(), calls=%async_computation.1 | async-start | bytes 2064384 | tf_op jit(solution)/shard_map/all_gather | solution.py:34
Sparse Core Ops, SparseCore 0:
  82.2 129.7 reduce-scatter.3
  216.7 62.9 all-gather.1
where the time goes:
time: 292 us; the launch traced here: 291 us
  waiting for transfers between devices  188 us (64%)
  blocking collectives  48.1 us (16%)
  local copies, waits for them, and re-layouts  24.6 us (8%)
  matrix products  14.7 us (5%)
  between operations  14.1 us (5%)
    unnamed x3, waiting for transfers between devices  127 us
    all_gather x1, waiting for transfers between devices, shards(): lax.all_gather(direction, 'fsdp', axis=0, tiled=True)  61.2 us
    psum x1, blocking collectives, shards(): projected = lax.psum(partial_value, 'fsdp').astype(jnp.bfloat16)  48.1 us
    unnamed x12, local copies, waits for them, and re-layouts  23.8 us
    dot_general x1, matrix products, shards(): lax.dot_general(flat_grad, projected, (((0,), (0,)), ((), ())), preferred...  8.44 us
  transfers between devices with their start and end apart: 2, of which 2 were waited for; matrix products, arithmetic and copies ran while one was open for 1% of the time, Pallas kernels for 0%

commit v1 on v0

v1 whole, which is shorter than its diff:
```python
import jax
import jax.numpy as jnp
from jax import lax
from jax.sharding import Mesh, PartitionSpec as P

bias_first = 1.0 - 0.9**20
bias_second = 1.0 - 0.999**20
epsilon = 1e-08

YLO, ZH, ZL, CORE = 2, 4, 2, 2
DP = ("ylo", "zh", "zl", "core")


def swap(value, axis):
    return lax.ppermute(value, axis, [(0, 1), (1, 0)])


def shift(value, axis, size, step):
    return lax.ppermute(value, axis, [(i, (i + step) % size) for i in range(size)])


def half(value, axis, index):
    return lax.dynamic_index_in_dim(value, index, axis, keepdims=False)


def shards(activations, projector, out_grad, first_moment, second_moment):
    n_fsdp = lax.axis_size("fsdp")
    zh, zl, core, ylo = (lax.axis_index(a) for a in ("zh", "zl", "core", "ylo"))
    tokens, rank = activations.shape[0], projector.shape[1]
    cols = first_moment.shape[1]
    wide = jnp.float32
    narrow = jnp.bfloat16

    grads = out_grad.reshape(tokens, YLO, ZH, ZL * CORE * cols)
    kept = [half(grads, 2, zh)]
    for step in range(1, ZH):
        kept.append(shift(half(grads, 2, (zh + step) % ZH), "zh", ZH, step))
    grads = jnp.stack(kept)

    partial_value = jnp.dot(activations, projector, preferred_element_type=wide).astype(narrow)
    pieces = lax.all_to_all(partial_value.reshape(n_fsdp, tokens // n_fsdp, rank), "fsdp", 0, 0)
    piece = pieces.astype(wide).sum(0).astype(narrow)
    piece = jnp.stack([piece] + [shift(piece, "zh", ZH, step) for step in range(1, ZH)])
    projected = lax.all_to_all(jnp.broadcast_to(piece, (n_fsdp,) + piece.shape), "fsdp", 0, 0)

    grads = grads.reshape(ZH, n_fsdp, tokens // n_fsdp, YLO * ZL * CORE * cols)
    total = lax.dot_general(
        grads, projected, (((0, 1, 2), (1, 0, 2)), ((), ())), preferred_element_type=wide
    )
    total = total.reshape(YLO, ZL, CORE, cols, rank)
    total = half(total, 2, core) + swap(half(total, 2, 1 - core).astype(narrow), "core").astype(wide)
    left, right = total[..., : rank // 2], total[..., rank // 2 :]
    left_in = swap(half(left, 0, 1 - ylo).astype(narrow), "ylo")
    right_in = swap(half(right, 1, 1 - zl).astype(narrow), "zl")
    left = half(left, 0, ylo) + left_in.astype(wide)
    right = half(right, 1, zl) + right_in.astype(wide)
    left_in = swap(half(left, 0, 1 - zl).astype(narrow), "zl")
    right_in = swap(half(right, 0, 1 - ylo).astype(narrow), "ylo")
    left = half(left, 0, zl) + left_in.astype(wide)
    right = half(right, 0, ylo) + right_in.astype(wide)
    gradient = jnp.concatenate([left, right], axis=-1)[None]

    first_new = 0.9 * first_moment + 0.1 * gradient
    second_new = 0.999 * second_moment + 0.001 * gradient * gradient
    direction = (first_new / bias_first / (jnp.sqrt(second_new / bias_second) + epsilon)).astype(narrow)
    direction = lax.all_to_all(jnp.broadcast_to(direction, (n_fsdp, cols, rank)), "fsdp", 0, 0)
    weight_update = lax.dot_general(
        direction, projector, (((2,), (1,)), ((), ())), preferred_element_type=wide
    ).astype(narrow)
    return (weight_update, first_new, second_new)


def solution(mesh):
    fine = Mesh(
        mesh.devices.reshape(YLO, ZH, ZL, CORE, mesh.devices.shape[1]), DP + ("fsdp",)
    )
    in_specs = (
        P(DP, "fsdp"),
        P("fsdp", None),
        P(DP, "fsdp", None),
        P("fsdp", DP, None),
        P("fsdp", DP, None),
    )
    out_specs = (P(None, DP, "fsdp"), P("fsdp", DP, None), P("fsdp", DP, None))
    return jax.shard_map(shards, mesh=fine, in_specs=in_specs, out_specs=out_specs, check_vma=False)
```

time: 292 us -> 140 us (0.48)
  the two profiles are of different devices: /device:TPU:64 before, /device:TPU:32 now
where the time goes in v1:
time: 140 us; the launch traced here: 139 us
  blocking collectives  45.8 us (33%)
  starting transfers between devices  31.6 us (23%)
  local copies, waits for them, and re-layouts  26.1 us (19%)
  waiting for transfers between devices  20.7 us (15%)
  matrix products  7.17 us (5%)
  other arithmetic  6.71 us (5%)
    all_to_all x1, blocking collectives, shards(): lax.all_to_all(jnp.broadcast_to(direction, (n_fsdp, cols, rank)), 'fsdp',...  30.3 us
    ppermute x6, starting transfers between devices, shift(): lax.ppermute(value, axis, [(i, (i + step) % size) for i in range(size)])  18 us
    all_to_all x1, blocking collectives, shards(): lax.all_to_all(partial_value.reshape(n_fsdp, tokens // n_fsdp, rank), 'fs...  15.5 us
    ppermute x6, waiting for transfers between devices, shift(): lax.ppermute(value, axis, [(i, (i + step) % size) for i in range(size)])  11.2 us
    ppermute x5, starting transfers between devices, swap(): return lax.ppermute(value, axis, [(0, 1), (1, 0)])  10.1 us
    ppermute x5, waiting for transfers between devices, swap(): return lax.ppermute(value, axis, [(0, 1), (1, 0)])  9.53 us
    dot_general x1, local copies, waits for them, and re-layouts, shards(): lax.dot_general(grads, projected, (((0, 1, 2), (1, 0, 2)), ((), ())), pre...  6.54 us
    unnamed x11, local copies, waits for them, and re-layouts  6.51 us
  transfers between devices with their start and end apart: 12, of which 7 were waited for; matrix products, arithmetic and copies ran while one was open for 16% of the time, Pallas kernels for 0%

profile of v1, /device:TPU:32, one launch (start us, length us, event | category | flops | bytes accessed | tf_op | source)
XLA Modules:
  0.0 139.0 jit_solution(6512555461142686021)
XLA Ops:
  0.6 0.0 copy-start
  0.6 1.6 %copy-done = bf16[1024,1024]{1,0:T(8,128)(2,1)S(1)} copy-done((bf16[1024,1024]{1,0:T(8,128)(2,1)S(1)}, bf16[1024,1024]{1,0:T(8,128)(2,1)}, u32[]{:S(2)}) %copy-start) | copy-done | bytes 2097176
  2.2 1.4 %convolution_convert_fusion = bf16[128,1024]{1,0:T(8,128)(2,1)S(1)} fusion(bf16[128,1024]{1,0:T(8,128)(2,1)} %param.5, bf16[1024,1024]{1,0:T(8,128)(2,1)S(1)} %copy-done), kind=kOutput, calls=%fused_computation.6 | convolution fusion | flops 268566528 | bytes 2621440 | tf_op jit(solution)/shard_map/dot_general | solution.py:40
  3.6 15.5 %all_to_all.15 = bf16[8,16,1024]{2,1,0:T(8,128)(2,1)S(1)} all-to-all(bf16[8,16,1024]{2,1,0:T(8,128)(2,1)S(1)} %bitcast.67), channel_id=1, replica_groups=mesh['ylo'=2,'zh'=4,'zl'=2,'core'=2,'fsdp'=8] {'fsdp'}, dimensions={0} | all-to-all | bytes 524288 | tf_op jit(solution)/shard_map/all_to_all | solution.py:41
  19.2 3.3 %collective-permute-start.3 = (bf16[16,1024]{1,0:T(8,128)(2,1)S(1)}, bf16[16,1024]{1,0:T(8,128)(2,1)S(1)}, u32[]{:S(2)}, u32[]{:S(2)}) collective-permute-start(bf16[16,1024]{1,0:T(8,128)(2,1)S(1)} %reduce_sum.12), channel_id=1, source_target_pairs={{0,32},{32,64},{64,96},{96,0},{1,33},{33,65},{65,97},{97,1},{2,34}... | collective-permute-start | bytes 98312 | tf_op jit(solution)/shard_map/ppermute | solution.py:19
  22.5 4.5 %collective-permute-start.4 = (bf16[16,1024]{1,0:T(8,128)(2,1)S(1)}, bf16[16,1024]{1,0:T(8,128)(2,1)S(1)}, u32[]{:S(2)}, u32[]{:S(2)}) collective-permute-start(bf16[16,1024]{1,0:T(8,128)(2,1)S(1)} %reduce_sum.12), channel_id=1, source_target_pairs={{0,64},{32,96},{64,0},{96,32},{1,65},{33,97},{65,1},{97,33},{2,66}... | collective-permute-start | bytes 98312 | tf_op jit(solution)/shard_map/ppermute | solution.py:19
  27.0 2.7 %collective-permute-start.5 = (bf16[16,1024]{1,0:T(8,128)(2,1)S(1)}, bf16[16,1024]{1,0:T(8,128)(2,1)S(1)}, u32[]{:S(2)}, u32[]{:S(2)}) collective-permute-start(bf16[16,1024]{1,0:T(8,128)(2,1)S(1)} %reduce_sum.12), channel_id=1, source_target_pairs={{0,96},{32,0},{64,32},{96,64},{1,97},{33,1},{65,33},{97,65},{2,98}... | collective-permute-start | bytes 98312 | tf_op jit(solution)/shard_map/ppermute | solution.py:19
  29.7 0.0 collective-permute-done.3
  29.7 1.3 collective-permute-done.4
  31.0 0.9 collective-permute-done.5
  31.9 1.1 broadcast_in_dim.11
  33.0 3.6 %all-to-all-start.1 = ((bf16[8,4,16,1024]{3,2,1,0:T(8,128)(2,1)}), bf16[8,4,16,1024]{3,2,1,0:T(8,128)(2,1)S(1)}, u32[]{:S(2)}, u32[]{:S(2)}) async-start(bf16[8,4,16,1024]{3,2,1,0:T(8,128)(2,1)} %broadcast_in_dim.11), calls=%async_computation.1 | async-start | bytes 2097152 | tf_op jit(solution)/shard_map/all_to_all | solution.py:44
  36.6 2.2 %copy.14 = bf16[128,1,3584]{0,2,1:T(8,128)(2,1)} copy(bf16[128,1,3584]{2,0,1:T(8,128)(2,1)} %param.7) | data formatting | bytes 1835008 | tf_op args[2]
  38.8 2.2 %constant_dynamic-slice_fusion = (bf16[128,2,1,448]{0,3,2,1:T(8,128)(2,1)}, bf16[128,2,448]{0,2,1:T(8,128)(2,1)}, bf16[128,2,448]{0,2,1:T(8,128)(2,1)}, bf16[128,2,448]{0,2,1:T(8,128)(2,1)}) fusion(bf16[128,2,4,448]{0,3,2,1:T(8,128)(2,1)} %bitcast.66, s32[]{:T(128)S(6)} %select_n.54, s32[]{:T(128)S(6)} %select_n.60, s32[]{:T(128)S(6)} %select_n.58, ...), kind=kLoop, calls=%fused_computation.35 | loop fusion | bytes 1835024 | tf_op jit(solution)/shard_map/jit(dynamic_index_in_dim)/dynamic_slice | solution.py:23
  41.1 2.4 %collective-permute-start = (bf16[128,2,448]{0,2,1:T(8,128)(2,1)}, bf16[128,2,448]{0,2,1:T(8,128)(2,1)}, u32[]{:S(2)}, u32[]{:S(2)}) collective-permute-start(bf16[128,2,448]{0,2,1:T(8,128)(2,1)} %get-tuple-element.11), channel_id=1, source_target_pairs={{0,32},{32,64},{64,96},{96,0},{1,33},{33,65},{65,97},{97,1},{2,34}... | collective-permute-start | bytes 688136 | tf_op jit(solution)/shard_map/ppermute | solution.py:19
  43.5 3.8 %collective-permute-start.1 = (bf16[128,2,448]{0,2,1:T(8,128)(2,1)}, bf16[128,2,448]{0,2,1:T(8,128)(2,1)}, u32[]{:S(2)}, u32[]{:S(2)}) collective-permute-start(bf16[128,2,448]{0,2,1:T(8,128)(2,1)} %get-tuple-element.10), channel_id=1, source_target_pairs={{0,64},{32,96},{64,0},{96,32},{1,65},{33,97},{65,1},{97,33},{2,66}... | collective-permute-start | bytes 688136 | tf_op jit(solution)/shard_map/ppermute | solution.py:19
  47.3 1.2 collective-permute-start.2
  48.5 1.1 copy.15
  49.6 0.9 stack.30
  50.5 9.0 %collective-permute-done = bf16[128,2,448]{0,2,1:T(8,128)(2,1)} collective-permute-done((bf16[128,2,448]{0,2,1:T(8,128)(2,1)}, bf16[128,2,448]{0,2,1:T(8,128)(2,1)}, u32[]{:S(2)}, u32[]{:S(2)}) %collective-permute-start) | collective-permute-done | bytes 229408 | tf_op jit(solution)/shard_map/ppermute | solution.py:19
  59.6 1.1 copy.16
  60.7 0.9 stack.31
  61.6 0.0 collective-permute-done.1
  61.6 1.1 copy.17
  62.8 0.9 stack.32
  63.7 0.0 collective-permute-done.2
  63.7 1.1 copy.18
  64.8 0.9 stack.33
  65.7 2.4 %maximum_bitcast_fusion = bf16[896,4,8,16]{0,3,2,1:T(8,128)(2,1)} fusion(bf16[1,8,16,896]{3,2,1,0:T(8,128)(2,1)} %stack.33, bf16[1,8,16,896]{3,2,1,0:T(8,128)(2,1)} %stack.32, bf16[1,8,16,896]{3,2,1,0:T(8,128)(2,1)} %stack.31, bf16[1,8,16,896]{3,2,1,0:T(8,128)(2,1)} %stack.30), kind=kLoop, calls=%fused_computation.10 | loop fusion | flops 1376256 | bytes 1835008 | tf_op jit(solution)/shard_map/dot_general | solution.py:47
  68.1 6.5 %dot_general.14 = bf16[2,2,2,112,4,8,16]{3,2,1,0,6,5,4:T(2,128)(2,1)} reshape(bf16[896,4,8,16]{0,3,2,1:T(8,128)(2,1)} %maximum_bitcast_fusion) | data formatting | bytes 1835008 | tf_op jit(solution)/shard_map/dot_general | solution.py:47
  74.6 0.0 all-to-all-done.1
  74.6 2.4 %convolution_bitcast_fusion = f32[2,2,2,112,1024]{4,3,2,1,0:T(8,128)S(1)} fusion(bf16[2,2,2,112,4,8,16]{3,2,1,0,6,5,4:T(2,128)(2,1)} %dot_general.14, bf16[8,4,16,1024]{3,2,1,0:T(8,128)(2,1)S(1)} %all-to-all-done.1), kind=kOutput, calls=%fused_computation.2 | convolution fusion | flops 939524096 | bytes 5636096 | tf_op jit(solution)/shard_map/dot_general | solution.py:47
  77.0 0.0 copy-start.1
  77.0 1.8 %copy-done.1 = f32[2,2,2,112,1024]{4,3,2,1,0:T(8,128)} copy-done((f32[2,2,2,112,1024]{4,3,2,1,0:T(8,128)}, f32[2,2,2,112,1024]{4,3,2,1,0:T(8,128)S(1)}, u32[]{:S(2)}) %copy-start.1) | copy-done | bytes 3670040
  78.8 1.1 fusion.7
  79.9 0.0 collective-permute-start.6
  79.9 2.7 %collective-permute-done.6 = bf16[2,2,112,1024]{3,2,1,0:T(8,128)(2,1)S(1)} collective-permute-done((bf16[2,2,112,1024]{3,2,1,0:T(8,128)(2,1)}, bf16[2,2,112,1024]{3,2,1,0:T(8,128)(2,1)S(1)}, u32[]{:S(2)}, u32[]{:S(2)}) %collective-permute-start.6) | collective-permute-done | bytes 917536 | tf_op jit(solution)/shard_map/ppermute | solution.py:15
  82.5 1.8 %bitcast_add_fusion = f32[2,2,112,1024]{3,2,1,0:T(8,128)S(1)} fusion(bf16[2,2,112,1024]{3,2,1,0:T(8,128)(2,1)S(1)} %collective-permute-done.6, f32[2,2,2,112,1024]{4,3,2,1,0:T(8,128)} %copy-done.1, s32[]{:T(128)S(6)} %select_n.61), kind=kLoop, calls=%fused_computation.3 | loop fusion | flops 917504 | bytes 4587524 | tf_op jit(solution)/shard_map/add | solution.py:51
  84.3 0.2 fusion.17
  84.5 0.0 copy-start.2
  84.5 0.9 copy-done.2
  85.4 0.8 collective-permute-start.7
  86.2 0.0 copy-start.3
  86.2 0.0 copy-start.4
  86.2 4.3 %collective-permute-start.9 = (bf16[2,112,512]{2,1,0:T(8,128)(2,1)S(1)}, bf16[2,112,512]{2,1,0:T(8,128)(2,1)S(1)}, u32[]{:S(2)}, u32[]{:S(2)}) collective-permute-start(bf16[2,112,512]{2,1,0:T(8,128)(2,1)S(1)} %fusion.10), channel_id=1, source_target_pairs={{0,16},{16,0},{1,17},{17,1},{2,18},{18,2},{3,19},{19,3},{4,20},{20... | collective-permute-start | bytes 688136 | tf_op jit(solution)/shard_map/ppermute | solution.py:15
  90.5 2.8 %collective-permute-done.7 = bf16[2,112,512]{2,1,0:T(8,128)(2,1)} collective-permute-done((bf16[2,112,512]{2,1,0:T(8,128)(2,1)S(1)}, bf16[2,112,512]{2,1,0:T(8,128)(2,1)}, u32[]{:S(2)}, u32[]{:S(2)}) %collective-permute-start.7) | collective-permute-done | bytes 229408 | tf_op jit(solution)/shard_map/ppermute | solution.py:15
  93.3 1.2 bitcast_add_fusion.2
  94.5 4.3 %collective-permute-start.8 = (bf16[112,512]{1,0:T(8,128)(2,1)S(1)}, bf16[112,512]{1,0:T(8,128)(2,1)S(1)}, u32[]{:S(2)}, u32[]{:S(2)}) collective-permute-start(bf16[112,512]{1,0:T(8,128)(2,1)S(1)} %fusion.14), channel_id=1, source_target_pairs={{0,16},{16,0},{1,17},{17,1},{2,18},{18,2},{3,19},{19,3},{4,20},{20... | collective-permute-start | bytes 344072 | tf_op jit(solution)/shard_map/ppermute | solution.py:15
  98.8 0.0 collective-permute-done.9
  98.8 0.1 bitcast_add_fusion.1
  98.9 0.8 collective-permute-start.10
  99.7 1.9 %collective-permute-done.8 = bf16[112,512]{1,0:T(8,128)(2,1)S(1)} collective-permute-done((bf16[112,512]{1,0:T(8,128)(2,1)S(1)}, bf16[112,512]{1,0:T(8,128)(2,1)S(1)}, u32[]{:S(2)}, u32[]{:S(2)}) %collective-permute-start.8) | collective-permute-done | bytes 114720 | tf_op jit(solution)/shard_map/ppermute | solution.py:15
  101.6 2.2 %collective-permute-done.10 = bf16[112,512]{1,0:T(8,128)(2,1)S(1)} collective-permute-done((bf16[112,512]{1,0:T(8,128)(2,1)S(1)}, bf16[112,512]{1,0:T(8,128)(2,1)S(1)}, u32[]{:S(2)}, u32[]{:S(2)}) %collective-permute-start.10) | collective-permute-done | bytes 114720 | tf_op jit(solution)/shard_map/ppermute | solution.py:15
  103.8 0.0 copy-done.3
  103.8 0.0 copy-done.4
  103.8 1.2 fusion.13
  105.0 0.2 broadcast_in_dim.13
  105.3 30.3 %all_to_all.16 = bf16[8,112,1024]{2,1,0:T(8,128)(2,1)S(1)} all-to-all(bf16[8,112,1024]{2,1,0:T(8,128)(2,1)S(1)} %broadcast_in_dim.13), channel_id=1, replica_groups=mesh['ylo'=2,'zh'=4,'zl'=2,'core'=2,'fsdp'=8] {'fsdp'}, dimensions={0} | all-to-all | bytes 3670016 | tf_op jit(solution)/shard_map/all_to_all | solution.py:66
  135.6 3.4 %fusion.2 = bf16[8,112,1024]{2,1,0:T(8,128)(2,1)} fusion(bf16[8,112,1024]{2,1,0:T(8,128)(2,1)S(1)} %all_to_all.16, bf16[1024,1024]{1,0:T(8,128)(2,1)S(1)} %copy-done), kind=kOutput, calls=%fused_computation.5 | convolution fusion | flops 1879965696 | bytes 5767168 | tf_op jit(solution)/shard_map/dot_general | solution.py:67
  (8 shorter events, 0.2 us)
Async XLA Ops:
  0.6 1.6 %copy-start = (bf16[1024,1024]{1,0:T(8,128)(2,1)S(1)}, bf16[1024,1024]{1,0:T(8,128)(2,1)}, u32[]{:S(2)}) copy-start(bf16[1024,1024]{1,0:T(8,128)(2,1)} %param.6) | copy-start | bytes 6291460
  19.2 10.5 %collective-permute-start.3 = (bf16[16,1024]{1,0:T(8,128)(2,1)S(1)}, bf16[16,1024]{1,0:T(8,128)(2,1)S(1)}, u32[]{:S(2)}, u32[]{:S(2)}) collective-permute-start(bf16[16,1024]{1,0:T(8,128)(2,1)S(1)} %reduce_sum.12), channel_id=1, source_target_pairs={{0,32},{32,64},{64,96},{96,0},{1,33},{33,65},{65,97},{97,1},{2,34}... | collective-permute-start | bytes 98312 | tf_op jit(solution)/shard_map/ppermute | solution.py:19
  22.5 8.4 %collective-permute-start.4 = (bf16[16,1024]{1,0:T(8,128)(2,1)S(1)}, bf16[16,1024]{1,0:T(8,128)(2,1)S(1)}, u32[]{:S(2)}, u32[]{:S(2)}) collective-permute-start(bf16[16,1024]{1,0:T(8,128)(2,1)S(1)} %reduce_sum.12), channel_id=1, source_target_pairs={{0,64},{32,96},{64,0},{96,32},{1,65},{33,97},{65,1},{97,33},{2,66}... | collective-permute-start | bytes 98312 | tf_op jit(solution)/shard_map/ppermute | solution.py:19
  27.0 4.8 %collective-permute-start.5 = (bf16[16,1024]{1,0:T(8,128)(2,1)S(1)}, bf16[16,1024]{1,0:T(8,128)(2,1)S(1)}, u32[]{:S(2)}, u32[]{:S(2)}) collective-permute-start(bf16[16,1024]{1,0:T(8,128)(2,1)S(1)} %reduce_sum.12), channel_id=1, source_target_pairs={{0,96},{32,0},{64,32},{96,64},{1,97},{33,1},{65,33},{97,65},{2,98}... | collective-permute-start | bytes 98312 | tf_op jit(solution)/shard_map/ppermute | solution.py:19
  33.0 41.6 %all-to-all-start.1 = ((bf16[8,4,16,1024]{3,2,1,0:T(8,128)(2,1)}), bf16[8,4,16,1024]{3,2,1,0:T(8,128)(2,1)S(1)}, u32[]{:S(2)}, u32[]{:S(2)}) async-start(bf16[8,4,16,1024]{3,2,1,0:T(8,128)(2,1)} %broadcast_in_dim.11), calls=%async_computation.1 | async-start | bytes 2097152 | tf_op jit(solution)/shard_map/all_to_all | solution.py:44
  41.1 18.5 %collective-permute-start = (bf16[128,2,448]{0,2,1:T(8,128)(2,1)}, bf16[128,2,448]{0,2,1:T(8,128)(2,1)}, u32[]{:S(2)}, u32[]{:S(2)}) collective-permute-start(bf16[128,2,448]{0,2,1:T(8,128)(2,1)} %get-tuple-element.11), channel_id=1, source_target_pairs={{0,32},{32,64},{64,96},{96,0},{1,33},{33,65},{65,97},{97,1},{2,34}... | collective-permute-start | bytes 688136 | tf_op jit(solution)/shard_map/ppermute | solution.py:19
  43.5 18.1 %collective-permute-start.1 = (bf16[128,2,448]{0,2,1:T(8,128)(2,1)}, bf16[128,2,448]{0,2,1:T(8,128)(2,1)}, u32[]{:S(2)}, u32[]{:S(2)}) collective-permute-start(bf16[128,2,448]{0,2,1:T(8,128)(2,1)} %get-tuple-element.10), channel_id=1, source_target_pairs={{0,64},{32,96},{64,0},{96,32},{1,65},{33,97},{65,1},{97,33},{2,66}... | collective-permute-start | bytes 688136 | tf_op jit(solution)/shard_map/ppermute | solution.py:19
  47.3 16.4 %collective-permute-start.2 = (bf16[128,2,448]{0,2,1:T(8,128)(2,1)}, bf16[128,2,448]{0,2,1:T(8,128)(2,1)}, u32[]{:S(2)}, u32[]{:S(2)}) collective-permute-start(bf16[128,2,448]{0,2,1:T(8,128)(2,1)} %get-tuple-element.9), channel_id=1, source_target_pairs={{0,96},{32,0},{64,32},{96,64},{1,97},{33,1},{65,33},{97,65},{2,98}... | collective-permute-start | bytes 688136 | tf_op jit(solution)/shard_map/ppermute | solution.py:19
  77.0 1.8 %copy-start.1 = (f32[2,2,2,112,1024]{4,3,2,1,0:T(8,128)}, f32[2,2,2,112,1024]{4,3,2,1,0:T(8,128)S(1)}, u32[]{:S(2)}) copy-start(f32[2,2,2,112,1024]{4,3,2,1,0:T(8,128)S(1)} %convolution_bitcast_fusion) | copy-start | bytes 11010052
  79.9 2.7 %collective-permute-start.6 = (bf16[2,2,112,1024]{3,2,1,0:T(8,128)(2,1)}, bf16[2,2,112,1024]{3,2,1,0:T(8,128)(2,1)S(1)}, u32[]{:S(2)}, u32[]{:S(2)}) collective-permute-start(bf16[2,2,112,1024]{3,2,1,0:T(8,128)(2,1)} %fusion.7), channel_id=1, source_target_pairs={{0,8},{8,0},{1,9},{9,1},{2,10},{10,2},{3,11},{11,3},{4,12},{12,4},... | collective-permute-start | bytes 2752520 | tf_op jit(solution)/shard_map/ppermute | solution.py:15
  84.5 0.9 copy-start.2
  85.4 7.8 %collective-permute-start.7 = (bf16[2,112,512]{2,1,0:T(8,128)(2,1)S(1)}, bf16[2,112,512]{2,1,0:T(8,128)(2,1)}, u32[]{:S(2)}, u32[]{:S(2)}) collective-permute-start(bf16[2,112,512]{2,1,0:T(8,128)(2,1)S(1)} %fusion.9), channel_id=1, source_target_pairs={{0,128},{128,0},{1,129},{129,1},{2,130},{130,2},{3,131},{131,3},{4... | collective-permute-start | bytes 688136 | tf_op jit(solution)/shard_map/ppermute | solution.py:15
  86.2 17.6 %copy-start.3 = (f32[1,112,1024]{2,1,0:T(8,128)S(1)}, f32[1,112,1024]{2,1,0:T(8,128)}, u32[]{:S(2)}) copy-start(f32[1,112,1024]{2,1,0:T(8,128)} %param.8) | copy-start | bytes 1376260
  86.2 17.6 %copy-start.4 = (f32[1,112,1024]{2,1,0:T(8,128)S(1)}, f32[1,112,1024]{2,1,0:T(8,128)}, u32[]{:S(2)}) copy-start(f32[1,112,1024]{2,1,0:T(8,128)} %param.9) | copy-start | bytes 1376260
  86.2 12.6 %collective-permute-start.9 = (bf16[2,112,512]{2,1,0:T(8,128)(2,1)S(1)}, bf16[2,112,512]{2,1,0:T(8,128)(2,1)S(1)}, u32[]{:S(2)}, u32[]{:S(2)}) collective-permute-start(bf16[2,112,512]{2,1,0:T(8,128)(2,1)S(1)} %fusion.10), channel_id=1, source_target_pairs={{0,16},{16,0},{1,17},{17,1},{2,18},{18,2},{3,19},{19,3},{4,20},{20... | collective-permute-start | bytes 688136 | tf_op jit(solution)/shard_map/ppermute | solution.py:15
  94.5 7.0 %collective-permute-start.8 = (bf16[112,512]{1,0:T(8,128)(2,1)S(1)}, bf16[112,512]{1,0:T(8,128)(2,1)S(1)}, u32[]{:S(2)}, u32[]{:S(2)}) collective-permute-start(bf16[112,512]{1,0:T(8,128)(2,1)S(1)} %fusion.14), channel_id=1, source_target_pairs={{0,16},{16,0},{1,17},{17,1},{2,18},{18,2},{3,19},{19,3},{4,20},{20... | collective-permute-start | bytes 344072 | tf_op jit(solution)/shard_map/ppermute | solution.py:15
  98.9 4.9 %collective-permute-start.10 = (bf16[112,512]{1,0:T(8,128)(2,1)S(1)}, bf16[112,512]{1,0:T(8,128)(2,1)S(1)}, u32[]{:S(2)}, u32[]{:S(2)}) collective-permute-start(bf16[112,512]{1,0:T(8,128)(2,1)S(1)} %fusion.15), channel_id=1, source_target_pairs={{0,128},{128,0},{1,129},{129,1},{2,130},{130,2},{3,131},{131,3},{4... | collective-permute-start | bytes 344072 | tf_op jit(solution)/shard_map/ppermute | solution.py:15

commit v2 on v1

v2 whole, which is shorter than its diff:
```python
import functools

import jax
import jax.numpy as jnp
from jax import lax
from jax.experimental import pallas as pl
from jax.experimental.pallas import tpu as pltpu
from jax.sharding import Mesh, PartitionSpec as P

bias_first = 1.0 - 0.9**20
bias_second = 1.0 - 0.999**20
epsilon = 1e-08

YLO, ZH, ZL, CORE = 2, 4, 2, 2
DP = ("ylo", "zh", "zl", "core")
wide, narrow = jnp.float32, jnp.bfloat16
VMEM = pl.BlockSpec(memory_space=pltpu.VMEM)
SMEM = pl.BlockSpec(memory_space=pltpu.SMEM)


def swap(value, axis):
    return lax.ppermute(value, axis, [(0, 1), (1, 0)])


def shift(value, axis, size, step):
    return lax.ppermute(value, axis, [(i, (i + step) % size) for i in range(size)])


def local(body, outs, count, **kwargs):
    return pl.pallas_call(
        body,
        out_shape=[jax.ShapeDtypeStruct(shape, dtype) for shape, dtype in outs],
        in_specs=[SMEM] + [VMEM] * count,
        out_specs=[VMEM] * len(outs),
        compiler_params=pltpu.CompilerParams(vmem_limit_bytes=40 * 2**20),
        **kwargs,
    )


def turn_kernel(zh_ref, grads_ref, *refs):
    outs, turned = refs[:ZH], refs[ZH]
    turned[...] = grads_ref[...].T
    block = outs[0].shape[1]
    for step in range(ZH):
        owner = lax.rem(zh_ref[0] + step, ZH)
        for y in range(YLO):
            start = pl.multiple_of((y * ZH + owner) * block, 16)
            outs[step][y] = turned[pl.ds(start, block), :]


def rows_of_core(place_ref, core, grads, rows, sems):
    copies = []
    for step in range(ZH):
        for part in range(YLO * ZL):
            y = lax.rem(place_ref[0] + part % 2, YLO)
            z = lax.rem(place_ref[1] + part // 2, ZL)
            copies.append(
                pltpu.make_async_copy(
                    grads[step].at[y, z, core], rows.at[step, part], sems.at[step, part]
                )
            )
    for copy in copies:
        copy.start()
    return copies


def product(projected_ref, rows, copies):
    parts, cols, tokens = rows.shape[1:]
    acc = None
    for step in range(ZH):
        for copy in copies[step * parts : (step + 1) * parts]:
            copy.wait()
        part = jnp.dot(
            rows[step].reshape(parts * cols, tokens),
            projected_ref[:, step].reshape(tokens, projected_ref.shape[-1]),
            preferred_element_type=wide,
        )
        acc = part if acc is None else acc + part
    return acc.reshape(parts, cols, -1)


def send_kernel(place_ref, projected_ref, *refs):
    grads, (out_ref, rows, sems) = refs[:ZH], refs[ZH:]
    copies = rows_of_core(place_ref, 1 - place_ref[2], grads, rows, sems)
    out_ref[...] = product(projected_ref, rows, copies).astype(narrow)


def keep_kernel(place_ref, projected_ref, *refs):
    grads, (came_ref, own_ref, *sent_refs, rows, sems) = refs[:ZH], refs[ZH:]
    copies = rows_of_core(place_ref, place_ref[2], grads, rows, sems)
    total = product(projected_ref, rows, copies) + came_ref[...].astype(wide)
    own_ref[...] = total[0]
    for part, ref in enumerate(sent_refs):
        ref[...] = total[part + 1].astype(narrow)


def gradient_call(body, outs, tokens, cols, extra):
    parts = YLO * ZL
    return pl.pallas_call(
        body,
        out_shape=[jax.ShapeDtypeStruct(shape, dtype) for shape, dtype in outs],
        in_specs=[SMEM, VMEM] + [pl.BlockSpec(memory_space=pl.ANY)] * ZH + [VMEM] * extra,
        out_specs=[VMEM] * len(outs),
        scratch_shapes=[
            pltpu.VMEM((ZH, parts, cols, tokens), narrow),
            pltpu.SemaphoreType.DMA((ZH, parts)),
        ],
        compiler_params=pltpu.CompilerParams(vmem_limit_bytes=40 * 2**20),
    )


def shards(activations, projector, out_grad, first_moment, second_moment):
    n_fsdp = lax.axis_size("fsdp")
    zh, zl, core, ylo = (lax.axis_index(a) for a in ("zh", "zl", "core", "ylo"))
    tokens, rank = activations.shape[0], projector.shape[1]
    cols = first_moment.shape[1]
    block = ZL * CORE * cols

    partial_value = jnp.dot(activations, projector, preferred_element_type=wide).astype(narrow)
    partial_value, out_grad = lax.optimization_barrier((partial_value, out_grad))
    pieces = lax.all_to_all(partial_value.reshape(n_fsdp, tokens // n_fsdp, rank), "fsdp", 0, 0)

    grads = local(
        turn_kernel,
        [((YLO, block, tokens), narrow)] * ZH,
        1,
        scratch_shapes=[pltpu.VMEM((YLO * ZH * block, tokens), narrow)],
    )(zh[None], out_grad.reshape(tokens, YLO * ZH * block))
    near = [shift(grads[step], "zh", ZH, step) for step in (1, 3)]
    far = shift(grads[2], "zh", ZH, 2)

    piece = pieces.astype(wide).sum(0).astype(narrow)
    piece = jnp.stack([piece] + [shift(piece, "zh", ZH, step) for step in range(1, ZH)])
    piece, near = lax.optimization_barrier((piece, near))
    projected = lax.all_to_all(jnp.broadcast_to(piece, (n_fsdp,) + piece.shape), "fsdp", 0, 0)

    grads = [g.reshape(YLO, ZL, CORE, cols, tokens) for g in (grads[0], near[0], far, near[1])]
    place = jnp.stack([ylo, zl, core])
    one = (cols, rank)
    (sent,) = gradient_call(send_kernel, [((YLO * ZL,) + one, narrow)], tokens, cols, 0)(
        place, projected, *grads
    )
    came = swap(sent, "core")
    own, over_y, over_z, over_both = gradient_call(
        keep_kernel, [(one, wide)] + [(one, narrow)] * 3, tokens, cols, 1
    )(place, projected, *grads, came)
    over_both = lax.ppermute(over_both, ("ylo", "zl"), [(i, 3 - i) for i in range(4)])
    over_y, over_z = swap(over_y, "ylo"), swap(over_z, "zl")
    gradient = own + over_y.astype(wide) + over_z.astype(wide) + over_both.astype(wide)
    gradient = gradient[None]

    first_new = 0.9 * first_moment + 0.1 * gradient
    second_new = 0.999 * second_moment + 0.001 * gradient * gradient
    direction = (first_new / bias_first / (jnp.sqrt(second_new / bias_second) + epsilon)).astype(narrow)
    direction = lax.all_to_all(jnp.broadcast_to(direction, (n_fsdp, cols, rank)), "fsdp", 0, 0)
    weight_update = lax.dot_general(
        direction, projector, (((2,), (1,)), ((), ())), preferred_element_type=wide
    ).astype(narrow)
    return (weight_update, first_new, second_new)


def solution(mesh):
    fine = Mesh(
        mesh.devices.reshape(YLO, ZH, ZL, CORE, mesh.devices.shape[1]), DP + ("fsdp",)
    )
    in_specs = (
        P(DP, "fsdp"),
        P("fsdp", None),
        P(DP, "fsdp", None),
        P("fsdp", DP, None),
        P("fsdp", DP, None),
    )
    out_specs = (P(None, DP, "fsdp"), P("fsdp", DP, None), P("fsdp", DP, None))
    return jax.shard_map(shards, mesh=fine, in_specs=in_specs, out_specs=out_specs, check_vma=False)
```

time: 140 us -> 117 us (0.84)
  the two profiles are of different devices: /device:TPU:32 before, /device:TPU:64 now
where the time goes in v2:
time: 117 us
  starting transfers between devices  33.4 us (29%)
  waiting for transfers between devices  32.7 us (28%)
  blocking collectives  30.3 us (26%)
  Pallas kernels  6.01 us (5%)
  local copies, waits for them, and re-layouts  5.51 us (5%)
  matrix products  5.48 us (5%)
  other arithmetic  2.38 us (2%)
    all_to_all x1, blocking collectives, shards(): lax.all_to_all(jnp.broadcast_to(direction, (n_fsdp, cols, rank)), 'fsdp',...  30.3 us
    ppermute x6, starting transfers between devices, shift(): lax.ppermute(value, axis, [(i, (i + step) % size) for i in range(size)])  16.3 us
    ppermute x6, waiting for transfers between devices, shift(): lax.ppermute(value, axis, [(i, (i + step) % size) for i in range(size)])  16.2 us
    ppermute x3, waiting for transfers between devices, swap(): return lax.ppermute(value, axis, [(0, 1), (1, 0)])  8.13 us
    all_to_all x1, starting transfers between devices, shards(): lax.all_to_all(partial_value.reshape(n_fsdp, tokens // n_fsdp, rank), 'fs...  6.93 us
    all_to_all x1, starting transfers between devices, shards(): lax.all_to_all(jnp.broadcast_to(piece, (n_fsdp,) + piece.shape), 'fsdp',...  6.57 us
    ppermute x1, waiting for transfers between devices, shards(): lax.ppermute(over_both, ('ylo', 'zl'), [(i, 3 - i) for i in range(4)])  4.58 us
    unnamed x18, local copies, waits for them, and re-layouts  4.16 us
  transfers between devices with their start and end apart: 12, of which 8 were waited for; matrix products, arithmetic and copies ran while one was open for 1% of the time, Pallas kernels for 1%

profile of v2, /device:TPU:64, one launch (start us, length us, event | category | flops | bytes accessed | tf_op | source)
XLA Modules:
  0.0 116.6 jit_solution(14795645428309240671)
XLA Ops:
  0.6 0.0 copy-start
  0.6 0.0 copy-start.5
  0.7 1.6 %copy-done = bf16[1024,1024]{1,0:T(8,128)(2,1)S(1)} copy-done((bf16[1024,1024]{1,0:T(8,128)(2,1)S(1)}, bf16[1024,1024]{1,0:T(8,128)(2,1)}, u32[]{:S(2)}) %copy-start) | copy-done | bytes 2097176
  2.2 2.1 %convolution_convert_fusion = bf16[128,1024]{1,0:T(8,128)(2,1)} fusion(bf16[128,1024]{1,0:T(8,128)(2,1)} %param.5, bf16[1024,1024]{1,0:T(8,128)(2,1)S(1)} %copy-done), kind=kOutput, calls=%fused_computation.3 | convolution fusion | flops 268566528 | bytes 2621440 | tf_op jit(solution)/shard_map/dot_general | solution.py:119
  4.3 6.9 %all-to-all-start = ((bf16[8,16,1024]{2,1,0:T(8,128)(2,1)}), bf16[8,16,1024]{2,1,0:T(8,128)(2,1)}, u32[]{:S(2)}, u32[]{:S(2)}) async-start(bf16[8,16,1024]{2,1,0:T(8,128)(2,1)} %bitcast.3), calls=%async_computation | async-start | bytes 524288 | tf_op jit(solution)/shard_map/all_to_all | solution.py:121
  11.3 0.0 copy-done.5
  11.3 1.1 shard_map.76
  12.4 0.0 copy-start.6
  12.4 0.7 copy-done.6
  13.1 4.5 %collective-permute-start.3 = (bf16[2,448,128]{2,1,0:T(8,128)(2,1)}, bf16[2,448,128]{2,1,0:T(8,128)(2,1)S(1)}, u32[]{:S(2)}, u32[]{:S(2)}) collective-permute-start(bf16[2,448,128]{2,1,0:T(8,128)(2,1)} %get-tuple-element.18), channel_id=1, source_target_pairs={{0,32},{32,64},{64,96},{96,0},{1,33},{33,65},{65,97},{97,1},{2,34}... | collective-permute-start | bytes 688136 | tf_op jit(solution)/shard_map/ppermute | solution.py:26
  17.5 0.0 collective-permute-start.4
  17.5 2.6 %all-to-all-done = bf16[8,16,1024]{2,1,0:T(8,128)(2,1)} async-done(((bf16[8,16,1024]{2,1,0:T(8,128)(2,1)}), bf16[8,16,1024]{2,1,0:T(8,128)(2,1)}, u32[]{:S(2)}, u32[]{:S(2)}) %all-to-all-start) | async-done | bytes 262176 | tf_op jit(solution)/shard_map/all_to_all | solution.py:121
  20.2 1.0 reduce_sum.12
  21.1 0.1 collective-permute-start.2
  21.2 6.8 %collective-permute-start.1 = (bf16[16,1024]{1,0:T(8,128)(2,1)S(1)}, bf16[16,1024]{1,0:T(8,128)(2,1)S(1)}, u32[]{:S(2)}, u32[]{:S(2)}) collective-permute-start(bf16[16,1024]{1,0:T(8,128)(2,1)S(1)} %reduce_sum.12), channel_id=1, source_target_pairs={{0,64},{32,96},{64,0},{96,32},{1,65},{33,97},{65,1},{97,33},{2,66}... | collective-permute-start | bytes 98312 | tf_op jit(solution)/shard_map/ppermute | solution.py:26
  28.1 2.7 %collective-permute-start = (bf16[16,1024]{1,0:T(8,128)(2,1)S(1)}, bf16[16,1024]{1,0:T(8,128)(2,1)S(1)}, u32[]{:S(2)}, u32[]{:S(2)}) collective-permute-start(bf16[16,1024]{1,0:T(8,128)(2,1)S(1)} %reduce_sum.12), channel_id=1, source_target_pairs={{0,32},{32,64},{64,96},{96,0},{1,33},{33,65},{65,97},{97,1},{2,34}... | collective-permute-start | bytes 98312 | tf_op jit(solution)/shard_map/ppermute | solution.py:26
  30.8 3.4 %collective-permute-done.2 = bf16[16,1024]{1,0:T(8,128)(2,1)S(1)} collective-permute-done((bf16[16,1024]{1,0:T(8,128)(2,1)S(1)}, bf16[16,1024]{1,0:T(8,128)(2,1)S(1)}, u32[]{:S(2)}, u32[]{:S(2)}) %collective-permute-start.2) | collective-permute-done | bytes 32800 | tf_op jit(solution)/shard_map/ppermute | solution.py:26
  34.2 0.0 collective-permute-done.1
  34.2 0.0 collective-permute-done
  34.2 0.0 collective-permute-done.3
  34.2 0.0 copy-start.1
  34.2 0.0 collective-permute-done.4
  34.2 0.0 copy-start.3
  34.2 1.1 broadcast_in_dim.15
  35.4 0.0 copy-done.1
  35.4 0.0 copy-done.3
  35.4 6.6 %all-to-all-start.1 = ((bf16[8,4,16,1024]{3,2,1,0:T(8,128)(2,1)}), bf16[8,4,16,1024]{3,2,1,0:T(8,128)(2,1)S(1)}, u32[]{:S(2)}, u32[]{:S(2)}) async-start(bf16[8,4,16,1024]{3,2,1,0:T(8,128)(2,1)} %broadcast_in_dim.15), calls=%async_computation.1 | async-start | bytes 2097152 | tf_op jit(solution)/shard_map/all_to_all | solution.py:135
  41.9 2.2 %collective-permute-start.5 = (bf16[2,448,128]{2,1,0:T(8,128)(2,1)}, bf16[2,448,128]{2,1,0:T(8,128)(2,1)}, u32[]{:S(2)}, u32[]{:S(2)}) collective-permute-start(bf16[2,448,128]{2,1,0:T(8,128)(2,1)} %copy-done.6), channel_id=1, source_target_pairs={{0,64},{32,96},{64,0},{96,32},{1,65},{33,97},{65,1},{97,33},{2,66}... | collective-permute-start | bytes 688136 | tf_op jit(solution)/shard_map/ppermute | solution.py:26
  44.1 0.1 pad_add_fusion.place_ref
  44.2 12.7 %collective-permute-done.5 = bf16[2,448,128]{2,1,0:T(8,128)(2,1)} collective-permute-done((bf16[2,448,128]{2,1,0:T(8,128)(2,1)}, bf16[2,448,128]{2,1,0:T(8,128)(2,1)}, u32[]{:S(2)}, u32[]{:S(2)}) %collective-permute-start.5) | collective-permute-done | bytes 229408 | tf_op jit(solution)/shard_map/ppermute | solution.py:26
  57.0 1.2 %all-to-all-done.1.projected_ref = bf16[8,4,16,1024]{3,2,1,0:T(8,128)(2,1)S(1)} async-done(((bf16[8,4,16,1024]{3,2,1,0:T(8,128)(2,1)}), bf16[8,4,16,1024]{3,2,1,0:T(8,128)(2,1)S(1)}, u32[]{:S(2)}, u32[]{:S(2)}) %all-to-all-start.1) | async-done | bytes 1048608 | tf_op jit(solution)/shard_map/all_to_all | solution.py:135
  58.2 0.0 copy-start.2
  58.2 0.9 copy-done.2
  59.1 0.0 copy-start.4
  59.1 0.9 copy-done.4
  60.1 2.4 %shard_map.77 = bf16[4,112,1024]{2,1,0:T(8,128)(2,1)S(1)} custom-call(s32[3]{0:T(128)S(1)} %pad_add_fusion.place_ref, bf16[8,4,16,1024]{3,2,1,0:T(8,128)(2,1)S(1)} %all-to-all-done.1.projected_ref, bf16[2,2,2,112,128]{4,3,2,1,0:T(8,128)(2,1)S(1)} %bitcast.32, bf16[2,2,2,112,128]{4,3,2,1,0:T(8,128)(2,1)S(1)} %bitcast.34, ...), custom_call_target="tpu_custom_call" | custom-call | tf_op jit(solution)/shard_map/pallas_call | solution.py:140
  62.5 0.0 copy-start.7
  62.5 0.0 copy-start.8
  62.6 0.1 collective-permute-start.6
  62.7 2.5 %collective-permute-done.6.refs_4_ = bf16[4,112,1024]{2,1,0:T(8,128)(2,1)S(1)} collective-permute-done((bf16[4,112,1024]{2,1,0:T(8,128)(2,1)S(1)}, bf16[4,112,1024]{2,1,0:T(8,128)(2,1)S(1)}, u32[]{:S(2)}, u32[]{:S(2)}) %collective-permute-start.6) | collective-permute-done | bytes 917536 | tf_op jit(solution)/shard_map/ppermute | solution.py:22
  65.1 2.5 %shard_map.78 = (f32[112,1024]{1,0:T(8,128)S(1)}, bf16[112,1024]{1,0:T(8,128)(2,1)S(1)}, bf16[112,1024]{1,0:T(8,128)(2,1)S(1)}, bf16[112,1024]{1,0:T(8,128)(2,1)S(1)}) custom-call(s32[3]{0:T(128)S(1)} %pad_add_fusion.place_ref, bf16[8,4,16,1024]{3,2,1,0:T(8,128)(2,1)S(1)} %all-to-all-done.1.projected_ref, bf16[2,2,2,112,128]{4,3,2,1,0:T(8,128)(2,1)S(1)} %bitcast.33, ...), custom_call_target="tpu_custom_call" | custom-call | tf_op jit(solution)/shard_map/pallas_call | solution.py:144
  67.6 0.8 collective-permute-start.7
  68.3 0.0 collective-permute-start.8
  68.3 2.8 %collective-permute-start.9 = (bf16[112,1024]{1,0:T(8,128)(2,1)S(1)}, bf16[112,1024]{1,0:T(8,128)(2,1)S(1)}, u32[]{:S(2)}, u32[]{:S(2)}) collective-permute-start(bf16[112,1024]{1,0:T(8,128)(2,1)S(1)} %get-tuple-element.28), channel_id=1, source_target_pairs={{0,144},{16,128},{128,16},{144,0},{1,145},{17,129},{129,17},{145,1... | collective-permute-start | bytes 688136 | tf_op jit(solution)/shard_map/ppermute | solution.py:147
  71.2 4.2 %collective-permute-done.7 = bf16[112,1024]{1,0:T(8,128)(2,1)S(1)} collective-permute-done((bf16[112,1024]{1,0:T(8,128)(2,1)S(1)}, bf16[112,1024]{1,0:T(8,128)(2,1)S(1)}, u32[]{:S(2)}, u32[]{:S(2)}) %collective-permute-start.7) | collective-permute-done | bytes 229408 | tf_op jit(solution)/shard_map/ppermute | solution.py:22
  75.3 1.5 %collective-permute-done.8 = bf16[112,1024]{1,0:T(8,128)(2,1)S(1)} collective-permute-done((bf16[112,1024]{1,0:T(8,128)(2,1)S(1)}, bf16[112,1024]{1,0:T(8,128)(2,1)S(1)}, u32[]{:S(2)}, u32[]{:S(2)}) %collective-permute-start.8) | collective-permute-done | bytes 229408 | tf_op jit(solution)/shard_map/ppermute | solution.py:22
  76.8 4.6 %collective-permute-done.9 = bf16[112,1024]{1,0:T(8,128)(2,1)S(1)} collective-permute-done((bf16[112,1024]{1,0:T(8,128)(2,1)S(1)}, bf16[112,1024]{1,0:T(8,128)(2,1)S(1)}, u32[]{:S(2)}, u32[]{:S(2)}) %collective-permute-start.9) | collective-permute-done | bytes 229408 | tf_op jit(solution)/shard_map/ppermute | solution.py:147
  81.4 0.0 copy-done.7
  81.4 0.0 copy-done.8
  81.4 1.3 %fusion.7 = (bf16[112,1024]{1,0:T(8,128)(2,1)S(1)}, f32[1,112,1024]{2,1,0:T(8,128)}, f32[1,112,1024]{2,1,0:T(8,128)}) fusion(bf16[112,1024]{1,0:T(8,128)(2,1)S(1)} %collective-permute-done.9, bf16[112,1024]{1,0:T(8,128)(2,1)S(1)} %collective-permute-done.8, f32[112,1024]{1,0:T(8,128)S(1)} %get-tuple-element.25, ...), kind=kLoop, calls=%fused_computation.10 | loop fusion | flops 2064384 | bytes 3211264 | tf_op jit(solution)/shard_map/broadcast_in_dim | solution.py:155
  82.7 0.2 broadcast_in_dim.17
  82.9 30.3 %all_to_all.15 = bf16[8,112,1024]{2,1,0:T(8,128)(2,1)S(1)} all-to-all(bf16[8,112,1024]{2,1,0:T(8,128)(2,1)S(1)} %broadcast_in_dim.17), channel_id=1, replica_groups=mesh['ylo'=2,'zh'=4,'zl'=2,'core'=2,'fsdp'=8] {'fsdp'}, dimensions={0} | all-to-all | bytes 3670016 | tf_op jit(solution)/shard_map/all_to_all | solution.py:155
  113.2 3.4 %fusion.2 = bf16[8,112,1024]{2,1,0:T(8,128)(2,1)} fusion(bf16[8,112,1024]{2,1,0:T(8,128)(2,1)S(1)} %all_to_all.15, bf16[1024,1024]{1,0:T(8,128)(2,1)S(1)} %copy-done), kind=kOutput, calls=%fused_computation.2 | convolution fusion | flops 1879965696 | bytes 5767168 | tf_op jit(solution)/shard_map/dot_general | solution.py:156
  (1 shorter events, 0.0 us)
Async XLA Ops:
  0.6 1.6 %copy-start = (bf16[1024,1024]{1,0:T(8,128)(2,1)S(1)}, bf16[1024,1024]{1,0:T(8,128)(2,1)}, u32[]{:S(2)}) copy-start(bf16[1024,1024]{1,0:T(8,128)(2,1)} %param.6) | copy-start | bytes 6291460
  0.6 10.6 %copy-start.5 = (bf16[128,1,3584]{2,0,1:T(8,128)(2,1)S(1)}, bf16[128,1,3584]{2,0,1:T(8,128)(2,1)}, u32[]{:S(2)}) copy-start(bf16[128,1,3584]{2,0,1:T(8,128)(2,1)} %param.7) | copy-start | bytes 2752516
  4.3 15.8 %all-to-all-start = ((bf16[8,16,1024]{2,1,0:T(8,128)(2,1)}), bf16[8,16,1024]{2,1,0:T(8,128)(2,1)}, u32[]{:S(2)}, u32[]{:S(2)}) async-start(bf16[8,16,1024]{2,1,0:T(8,128)(2,1)} %bitcast.3), calls=%async_computation | async-start | bytes 524288 | tf_op jit(solution)/shard_map/all_to_all | solution.py:121
  12.4 0.7 copy-start.6
  13.1 21.1 %collective-permute-start.3 = (bf16[2,448,128]{2,1,0:T(8,128)(2,1)}, bf16[2,448,128]{2,1,0:T(8,128)(2,1)S(1)}, u32[]{:S(2)}, u32[]{:S(2)}) collective-permute-start(bf16[2,448,128]{2,1,0:T(8,128)(2,1)} %get-tuple-element.18), channel_id=1, source_target_pairs={{0,32},{32,64},{64,96},{96,0},{1,33},{33,65},{65,97},{97,1},{2,34}... | collective-permute-start | bytes 688136 | tf_op jit(solution)/shard_map/ppermute | solution.py:26
  17.5 16.7 %collective-permute-start.4 = (bf16[2,448,128]{2,1,0:T(8,128)(2,1)S(1)}, bf16[2,448,128]{2,1,0:T(8,128)(2,1)S(1)}, u32[]{:S(2)}, u32[]{:S(2)}) collective-permute-start(bf16[2,448,128]{2,1,0:T(8,128)(2,1)S(1)} %get-tuple-element.19), channel_id=1, source_target_pairs={{0,96},{32,0},{64,32},{96,64},{1,97},{33,1},{65,33},{97,65},{2,98}... | collective-permute-start | bytes 688136 | tf_op jit(solution)/shard_map/ppermute | solution.py:26
  21.1 13.0 %collective-permute-start.2 = (bf16[16,1024]{1,0:T(8,128)(2,1)S(1)}, bf16[16,1024]{1,0:T(8,128)(2,1)S(1)}, u32[]{:S(2)}, u32[]{:S(2)}) collective-permute-start(bf16[16,1024]{1,0:T(8,128)(2,1)S(1)} %reduce_sum.12), channel_id=1, source_target_pairs={{0,96},{32,0},{64,32},{96,64},{1,97},{33,1},{65,33},{97,65},{2,98}... | collective-permute-start | bytes 98312 | tf_op jit(solution)/shard_map/ppermute | solution.py:26
  21.2 12.9 %collective-permute-start.1 = (bf16[16,1024]{1,0:T(8,128)(2,1)S(1)}, bf16[16,1024]{1,0:T(8,128)(2,1)S(1)}, u32[]{:S(2)}, u32[]{:S(2)}) collective-permute-start(bf16[16,1024]{1,0:T(8,128)(2,1)S(1)} %reduce_sum.12), channel_id=1, source_target_pairs={{0,64},{32,96},{64,0},{96,32},{1,65},{33,97},{65,1},{97,33},{2,66}... | collective-permute-start | bytes 98312 | tf_op jit(solution)/shard_map/ppermute | solution.py:26
  28.1 6.1 %collective-permute-start = (bf16[16,1024]{1,0:T(8,128)(2,1)S(1)}, bf16[16,1024]{1,0:T(8,128)(2,1)S(1)}, u32[]{:S(2)}, u32[]{:S(2)}) collective-permute-start(bf16[16,1024]{1,0:T(8,128)(2,1)S(1)} %reduce_sum.12), channel_id=1, source_target_pairs={{0,32},{32,64},{64,96},{96,0},{1,33},{33,65},{65,97},{97,1},{2,34}... | collective-permute-start | bytes 98312 | tf_op jit(solution)/shard_map/ppermute | solution.py:26
  34.2 1.2 %copy-start.1 = (bf16[2,448,128]{2,1,0:T(8,128)(2,1)}, bf16[2,448,128]{2,1,0:T(8,128)(2,1)S(1)}, u32[]{:S(2)}) copy-start(bf16[2,448,128]{2,1,0:T(8,128)(2,1)S(1)} %collective-permute-done.3) | copy-start | bytes 688132
  34.2 1.1 copy-start.3
  35.4 22.8 %all-to-all-start.1 = ((bf16[8,4,16,1024]{3,2,1,0:T(8,128)(2,1)}), bf16[8,4,16,1024]{3,2,1,0:T(8,128)(2,1)S(1)}, u32[]{:S(2)}, u32[]{:S(2)}) async-start(bf16[8,4,16,1024]{3,2,1,0:T(8,128)(2,1)} %broadcast_in_dim.15), calls=%async_computation.1 | async-start | bytes 2097152 | tf_op jit(solution)/shard_map/all_to_all | solution.py:135
  41.9 15.0 %collective-permute-start.5 = (bf16[2,448,128]{2,1,0:T(8,128)(2,1)}, bf16[2,448,128]{2,1,0:T(8,128)(2,1)}, u32[]{:S(2)}, u32[]{:S(2)}) collective-permute-start(bf16[2,448,128]{2,1,0:T(8,128)(2,1)} %copy-done.6), channel_id=1, source_target_pairs={{0,64},{32,96},{64,0},{96,32},{1,65},{33,97},{65,1},{97,33},{2,66}... | collective-permute-start | bytes 688136 | tf_op jit(solution)/shard_map/ppermute | solution.py:26
  58.2 0.9 copy-start.2
  59.1 0.9 copy-start.4
  62.5 18.9 %copy-start.7 = (f32[1,112,1024]{2,1,0:T(8,128)S(1)}, f32[1,112,1024]{2,1,0:T(8,128)}, u32[]{:S(2)}) copy-start(f32[1,112,1024]{2,1,0:T(8,128)} %param.8) | copy-start | bytes 1376260
  62.5 18.9 %copy-start.8 = (f32[1,112,1024]{2,1,0:T(8,128)S(1)}, f32[1,112,1024]{2,1,0:T(8,128)}, u32[]{:S(2)}) copy-start(f32[1,112,1024]{2,1,0:T(8,128)} %param.9) | copy-start | bytes 1376260
  62.6 2.6 %collective-permute-start.6 = (bf16[4,112,1024]{2,1,0:T(8,128)(2,1)S(1)}, bf16[4,112,1024]{2,1,0:T(8,128)(2,1)S(1)}, u32[]{:S(2)}, u32[]{:S(2)}) collective-permute-start(bf16[4,112,1024]{2,1,0:T(8,128)(2,1)S(1)} %shard_map.77), channel_id=1, source_target_pairs={{0,8},{8,0},{1,9},{9,1},{2,10},{10,2},{3,11},{11,3},{4,12},{12,4},... | collective-permute-start | bytes 2752520 | tf_op jit(solution)/shard_map/ppermute | solution.py:22
  67.6 7.7 %collective-permute-start.7 = (bf16[112,1024]{1,0:T(8,128)(2,1)S(1)}, bf16[112,1024]{1,0:T(8,128)(2,1)S(1)}, u32[]{:S(2)}, u32[]{:S(2)}) collective-permute-start(bf16[112,1024]{1,0:T(8,128)(2,1)S(1)} %get-tuple-element.26), channel_id=1, source_target_pairs={{0,128},{128,0},{1,129},{129,1},{2,130},{130,2},{3,131},{131,3},{4... | collective-permute-start | bytes 688136 | tf_op jit(solution)/shard_map/ppermute | solution.py:22
  68.3 8.5 %collective-permute-start.8 = (bf16[112,1024]{1,0:T(8,128)(2,1)S(1)}, bf16[112,1024]{1,0:T(8,128)(2,1)S(1)}, u32[]{:S(2)}, u32[]{:S(2)}) collective-permute-start(bf16[112,1024]{1,0:T(8,128)(2,1)S(1)} %get-tuple-element.27), channel_id=1, source_target_pairs={{0,16},{16,0},{1,17},{17,1},{2,18},{18,2},{3,19},{19,3},{4,20},{20... | collective-permute-start | bytes 688136 | tf_op jit(solution)/shard_map/ppermute | solution.py:22
  68.3 13.1 %collective-permute-start.9 = (bf16[112,1024]{1,0:T(8,128)(2,1)S(1)}, bf16[112,1024]{1,0:T(8,128)(2,1)S(1)}, u32[]{:S(2)}, u32[]{:S(2)}) collective-permute-start(bf16[112,1024]{1,0:T(8,128)(2,1)S(1)} %get-tuple-element.28), channel_id=1, source_target_pairs={{0,144},{16,128},{128,16},{144,0},{1,145},{17,129},{129,17},{145,1... | collective-permute-start | bytes 688136 | tf_op jit(solution)/shard_map/ppermute | solution.py:147

commit v3 on v2

v3 whole, which is shorter than its diff:
```python
import functools

import jax
import jax.numpy as jnp
from jax import lax
from jax.experimental import pallas as pl
from jax.experimental.pallas import tpu as pltpu
from jax.sharding import Mesh, PartitionSpec as P

bias_first = 1.0 - 0.9**20
bias_second = 1.0 - 0.999**20
epsilon = 1e-08

YLO, ZH, ZL, CORE = 2, 4, 2, 2
DP = ("ylo", "zh", "zl", "core")
YHI, X = 2, 4
FSDP = ("yhi", "x")
wide, narrow = jnp.float32, jnp.bfloat16
VMEM = pl.BlockSpec(memory_space=pltpu.VMEM)
SMEM = pl.BlockSpec(memory_space=pltpu.SMEM)


def swap(value, axis):
    return lax.ppermute(value, axis, [(0, 1), (1, 0)])


def shift(value, axis, size, step):
    return lax.ppermute(value, axis, [(i, (i + step) % size) for i in range(size)])


def local(body, outs, count, **kwargs):
    return pl.pallas_call(
        body,
        out_shape=[jax.ShapeDtypeStruct(shape, dtype) for shape, dtype in outs],
        in_specs=[SMEM] + [VMEM] * count,
        out_specs=[VMEM] * len(outs),
        compiler_params=pltpu.CompilerParams(vmem_limit_bytes=16 * 2**20),
        **kwargs,
    )


def turn_kernel(zh_ref, grads_ref, *refs):
    outs, turned = refs[:ZH], refs[ZH]
    turned[...] = grads_ref[...].T
    block = outs[0].shape[1]
    for step in range(ZH):
        owner = lax.rem(zh_ref[0] + step, ZH)
        for y in range(YLO):
            start = pl.multiple_of((y * ZH + owner) * block, 16)
            outs[step][y] = turned[pl.ds(start, block), :]


def product(place_ref, core, pieces, grads, whole):
    cols, tokens = grads[0].shape[3:]
    for j, piece in enumerate(pieces):
        whole[:, pl.ds(place_ref[3 + j], 1)] = piece[...][:, None]
    rows = []
    for part in range(YLO * ZL):
        y = lax.rem(place_ref[0] + part % 2, YLO)
        z = lax.rem(place_ref[1] + part // 2, ZL)
        rows.append(jnp.concatenate([grads[step][y, z, core] for step in range(ZH)], axis=1))
    total = jnp.dot(
        jnp.concatenate(rows, axis=0),
        whole[...].reshape(ZH * tokens, whole.shape[-1]),
        preferred_element_type=wide,
    )
    return total.reshape(YLO * ZL, cols, -1)


def send_kernel(place_ref, *refs):
    pieces, grads, (out_ref, whole) = refs[:8], refs[8 : 8 + ZH], refs[8 + ZH :]
    out_ref[...] = product(place_ref, 1 - place_ref[2], pieces, grads, whole).astype(narrow)


def keep_kernel(place_ref, *refs):
    pieces, grads, rest = refs[:8], refs[8 : 8 + ZH], refs[8 + ZH :]
    came_ref, own_ref, *sent_refs, whole = rest
    total = product(place_ref, place_ref[2], pieces, grads, whole) + came_ref[...].astype(wide)
    own_ref[...] = total[0]
    for part, ref in enumerate(sent_refs):
        ref[...] = total[part + 1].astype(narrow)


def gradient_call(body, outs, tokens, rank, extra):
    n_fsdp = YHI * X
    return pl.pallas_call(
        body,
        out_shape=[jax.ShapeDtypeStruct(shape, dtype) for shape, dtype in outs],
        in_specs=[SMEM] + [VMEM] * (n_fsdp + ZH + extra),
        out_specs=[VMEM] * len(outs),
        scratch_shapes=[pltpu.VMEM((ZH, n_fsdp, tokens // n_fsdp, rank), narrow)],
        compiler_params=pltpu.CompilerParams(vmem_limit_bytes=16 * 2**20),
    )


def adam_kernel(own_ref, over_y_ref, over_z_ref, over_both_ref, first_ref, second_ref, *outs):
    gradient = own_ref[...] + over_y_ref[...].astype(wide)
    gradient = gradient + over_z_ref[...].astype(wide) + over_both_ref[...].astype(wide)
    first_new = 0.9 * first_ref[0] + 0.1 * gradient
    second_new = 0.999 * second_ref[0] + 0.001 * gradient * gradient
    root = jnp.sqrt(second_new / bias_second) + epsilon
    outs[0][...] = (first_new / bias_first / root).astype(narrow)
    outs[1][0] = first_new
    outs[2][0] = second_new


def back_kernel(count, first, place_ref, projector_ref, *refs):
    blocks = refs[:count]
    out_ref, held, sems = refs[-3:]
    stacked = jnp.concatenate([block[...] for block in blocks], axis=0)
    held[...] = lax.dot_general(
        stacked, projector_ref[...], (((1,), (1,)), ((), ())), preferred_element_type=wide
    ).astype(narrow).reshape(held.shape)
    copies = [
        pltpu.make_async_copy(held.at[j], out_ref.at[place_ref[3 + first + j]], sems.at[j])
        for j in range(count)
    ]
    for copy in copies:
        copy.start()
    for copy in copies:
        copy.wait()


def back(place, projector, blocks, first, out):
    count = len(blocks)
    cols = blocks[0].shape[0]
    width = projector.shape[0]
    before = [] if out is None else [out]
    return pl.pallas_call(
        functools.partial(back_kernel, count, first),
        out_shape=jax.ShapeDtypeStruct((YHI * X, cols, width), narrow),
        in_specs=[SMEM] + [VMEM] * (1 + count) + [pl.BlockSpec(memory_space=pl.ANY)] * len(before),
        out_specs=pl.BlockSpec(memory_space=pl.ANY),
        input_output_aliases={} if out is None else {2 + count: 0},
        scratch_shapes=[
            pltpu.VMEM((count, cols, width), narrow),
            pltpu.SemaphoreType.DMA((count,)),
        ],
        compiler_params=pltpu.CompilerParams(vmem_limit_bytes=16 * 2**20),
    )(place, projector, *blocks, *before)


def gathered(value, other=None):
    other = swap(value, "yhi") if other is None else other
    steps = (1, 3, 2)
    return (
        [value, other]
        + [shift(value, "x", X, step) for step in steps]
        + [shift(other, "x", X, step) for step in steps]
    )


def gathered_from(yhi, x):
    mine, other = yhi * X, (1 - yhi) * X
    steps = [(x + X - step) % X for step in (1, 3, 2)]
    return [mine + x, other + x] + [mine + s for s in steps] + [other + s for s in steps]


def shards(activations, projector, out_grad, first_moment, second_moment):
    n_fsdp = YHI * X
    zh, zl, core, ylo, yhi, x = (
        lax.axis_index(a) for a in ("zh", "zl", "core", "ylo", "yhi", "x")
    )
    tokens, rank = activations.shape[0], projector.shape[1]
    cols = first_moment.shape[1]
    block = ZL * CORE * cols

    partial_value = jnp.dot(activations, projector, preferred_element_type=wide).astype(narrow)
    partial_value, out_grad = lax.optimization_barrier((partial_value, out_grad))
    pieces = lax.all_to_all(partial_value.reshape(n_fsdp, tokens // n_fsdp, rank), FSDP, 0, 0)

    grads = local(
        turn_kernel,
        [((YLO, block, tokens), narrow)] * ZH,
        1,
        scratch_shapes=[pltpu.VMEM((YLO * ZH * block, tokens), narrow)],
    )(zh[None], out_grad.reshape(tokens, YLO * ZH * block))
    near = [shift(grads[step], "zh", ZH, step) for step in (1, 3)]

    piece = pieces.astype(wide).sum(0).astype(narrow)
    piece = jnp.stack([piece] + [shift(piece, "zh", ZH, step) for step in range(1, ZH)])
    piece, near = lax.optimization_barrier((piece, near))
    other, late = lax.optimization_barrier((swap(piece, "yhi"), grads[2]))
    far = shift(late, "zh", ZH, 2)
    projected = gathered(piece, other)

    grads = [g.reshape(YLO, ZL, CORE, cols, tokens) for g in (grads[0], near[0], far, near[1])]
    place = jnp.stack([ylo, zl, core] + gathered_from(yhi, x))
    one = (cols, rank)
    (sent,) = gradient_call(send_kernel, [((YLO * ZL,) + one, narrow)], tokens, rank, 0)(
        place, *projected, *grads
    )
    came = swap(sent, "core")
    own, over_y, over_z, over_both = gradient_call(
        keep_kernel, [(one, wide)] + [(one, narrow)] * 3, tokens, rank, 1
    )(place, *projected, *grads, came)
    over_both = lax.ppermute(over_both, ("ylo", "zl"), [(i, 3 - i) for i in range(4)])
    over_y, over_z = swap(over_y, "ylo"), swap(over_z, "zl")
    moment = jax.ShapeDtypeStruct((1,) + one, wide)
    direction, first_new, second_new = pl.pallas_call(
        adam_kernel,
        out_shape=[jax.ShapeDtypeStruct(one, narrow), moment, moment],
        in_specs=[VMEM] * 6,
        out_specs=[VMEM] * 3,
        compiler_params=pltpu.CompilerParams(vmem_limit_bytes=16 * 2**20),
    )(own, over_y, over_z, over_both, first_moment, second_moment)
    directions = gathered(direction)
    weight_update = back(place, projector, directions[:5], 0, None)
    weight_update = back(place, projector, directions[5:], 5, weight_update)
    return (weight_update, first_new, second_new)


def solution(mesh):
    fine = Mesh(
        mesh.devices.reshape(YLO, ZH, ZL, CORE, YHI, X), DP + FSDP
    )
    in_specs = (
        P(DP, FSDP),
        P(FSDP, None),
        P(DP, FSDP, None),
        P(FSDP, DP, None),
        P(FSDP, DP, None),
    )
    out_specs = (P(None, DP, FSDP), P(FSDP, DP, None), P(FSDP, DP, None))
    return jax.shard_map(shards, mesh=fine, in_specs=in_specs, out_specs=out_specs, check_vma=False)
```

time: 117 us -> 103 us (0.88)
  blocking collectives: 30.3 us -> 0 us
  starting transfers between devices: 33.4 us -> 51.2 us
  local copies, waits for them, and re-layouts: 5.51 us -> 1.04 us
  waiting for transfers between devices: 32.7 us -> 36.4 us
  Pallas kernels: 6.01 us -> 9.39 us
  matrix products: 5.48 us -> 2.74 us
  other arithmetic: 2.38 us -> 0.06 us
    all_to_all x1 -> x0, blocking collectives: 30.3 us -> none  [shards(): lax.all_to_all(jnp.broadcast_to(direction, (n_fsdp, cols, rank)), 'fsdp',...]
    ppermute x6 -> x18, starting transfers between devices: 16.3 us -> 35.4 us  [shift(): lax.ppermute(value, axis, [(i, (i + step) % size) for i in range(size)])]
    all_to_all x2 -> x1, starting transfers between devices: 13.5 us -> 6.93 us  [shards(): lax.all_to_all(partial_value.reshape(n_fsdp, tokens // n_fsdp, rank), FSD...]
    ppermute x3 -> x5, starting transfers between devices: 0.86 us -> 6.85 us  [swap(): return lax.ppermute(value, axis, [(0, 1), (1, 0)])]
    pallas_call x2 -> x5, Pallas kernels: 4.9 us -> 8.96 us  [the longest x2 5.28 us: back(): pl.pallas_call(functools.partial(back_kernel, count, first), out_shape=ja...]
    dot_general x1 -> x0, matrix products: 3.38 us -> none  [shards(): lax.dot_general(direction, projector, (((2,), (1,)), ((), ())), preferred...]
    unnamed x18 -> x10, local copies, waits for them, and re-layouts: 4.16 us -> 0.96 us
    ppermute x6 -> x18, waiting for transfers between devices: 16.2 us -> 19.2 us  [shift(): lax.ppermute(value, axis, [(i, (i + step) % size) for i in range(size)])]
  transfers between devices with their start and end apart: 12 -> 25, of which waited for: 8 -> 15; matrix products, arithmetic and copies ran while one was open for 1% -> 0% of each run, Pallas kernels for 1% -> 3%
where the time goes in v3:
time: 103 us; the launch traced here: 102 us
  starting transfers between devices  51.2 us (50%)
  waiting for transfers between devices  36.4 us (35%)
  Pallas kernels  9.39 us (9%)
  matrix products  2.74 us (3%)
  local copies, waits for them, and re-layouts  1.04 us (1%)
    ppermute x18, starting transfers between devices, shift(): lax.ppermute(value, axis, [(i, (i + step) % size) for i in range(size)])  35.4 us
    ppermute x18, waiting for transfers between devices, shift(): lax.ppermute(value, axis, [(i, (i + step) % size) for i in range(size)])  19.2 us
    ppermute x5, waiting for transfers between devices, swap(): return lax.ppermute(value, axis, [(0, 1), (1, 0)])  8.84 us
    all_to_all x1, starting transfers between devices, shards(): lax.all_to_all(partial_value.reshape(n_fsdp, tokens // n_fsdp, rank), FSD...  6.93 us
    ppermute x5, starting transfers between devices, swap(): return lax.ppermute(value, axis, [(0, 1), (1, 0)])  6.85 us
    pallas_call x2, Pallas kernels, back(): pl.pallas_call(functools.partial(back_kernel, count, first), out_shape=ja...  5.28 us
    ppermute x1, waiting for transfers between devices, shards(): lax.ppermute(over_both, ('ylo', 'zl'), [(i, 3 - i) for i in range(4)])  4.58 us
    all_to_all x1, waiting for transfers between devices, shards(): lax.all_to_all(partial_value.reshape(n_fsdp, tokens // n_fsdp, rank), FSD...  3.79 us
  transfers between devices with their start and end apart: 25, of which 15 were waited for; matrix products, arithmetic and copies ran while one was open for 0% of the time, Pallas kernels for 3%

profile of v3, /device:TPU:64, one launch (start us, length us, event | category | flops | bytes accessed | tf_op | source)
XLA Modules:
  0.0 101.8 jit_solution(3469133074357275475)
XLA Ops:
  0.6 0.0 copy-start
  0.6 0.0 copy-start.2
  0.7 0.9 copy-done
  1.6 2.7 %convolution_convert_fusion = bf16[128,1024]{1,0:T(8,128)(2,1)} fusion(bf16[128,1024]{1,0:T(8,128)(2,1)S(1)} %copy-done, bf16[1024,1024]{1,0:T(8,128)(2,1)} %projector_ref.3), kind=kOutput, calls=%fused_computation | convolution fusion | flops 268566528 | bytes 2621440 | tf_op jit(solution)/shard_map/dot_general | solution.py:168
  4.3 6.9 %all-to-all-start = ((bf16[8,16,1024]{2,1,0:T(8,128)(2,1)}), bf16[8,16,1024]{2,1,0:T(8,128)(2,1)S(1)}, u32[]{:S(2)}, u32[]{:S(2)}) async-start(bf16[8,16,1024]{2,1,0:T(8,128)(2,1)} %bitcast.11), calls=%async_computation | async-start | bytes 524288 | tf_op jit(solution)/shard_map/all_to_all | solution.py:170
  11.3 0.4 shard_map.76
  11.7 4.6 %collective-permute-start.3 = (bf16[2,448,128]{2,1,0:T(8,128)(2,1)S(1)}, bf16[2,448,128]{2,1,0:T(8,128)(2,1)S(1)}, u32[]{:S(2)}, u32[]{:S(2)}) collective-permute-start(bf16[2,448,128]{2,1,0:T(8,128)(2,1)S(1)} %get-tuple-element.23), channel_id=1, source_target_pairs={{0,32},{32,64},{64,96},{96,0},{1,33},{33,65},{65,97},{97,1},{2,34}... | collective-permute-start | bytes 688136 | tf_op jit(solution)/shard_map/ppermute | solution.py:28
  16.3 0.0 collective-permute-start.4
  16.3 3.8 %all-to-all-done = bf16[8,16,1024]{2,1,0:T(8,128)(2,1)S(1)} async-done(((bf16[8,16,1024]{2,1,0:T(8,128)(2,1)}), bf16[8,16,1024]{2,1,0:T(8,128)(2,1)S(1)}, u32[]{:S(2)}, u32[]{:S(2)}) %all-to-all-start) | async-done | bytes 262176 | tf_op jit(solution)/shard_map/all_to_all | solution.py:170
  20.1 0.1 collective-permute-start.2
  20.2 6.8 %collective-permute-start.1 = (bf16[16,1024]{1,0:T(8,128)(2,1)S(1)}, bf16[16,1024]{1,0:T(8,128)(2,1)S(1)}, u32[]{:S(2)}, u32[]{:S(2)}) collective-permute-start(bf16[16,1024]{1,0:T(8,128)(2,1)S(1)} %reduce_sum.12), channel_id=1, source_target_pairs={{0,64},{32,96},{64,0},{96,32},{1,65},{33,97},{65,1},{97,33},{2,66}... | collective-permute-start | bytes 98312 | tf_op jit(solution)/shard_map/ppermute | solution.py:28
  27.0 2.7 %collective-permute-start = (bf16[16,1024]{1,0:T(8,128)(2,1)S(1)}, bf16[16,1024]{1,0:T(8,128)(2,1)S(1)}, u32[]{:S(2)}, u32[]{:S(2)}) collective-permute-start(bf16[16,1024]{1,0:T(8,128)(2,1)S(1)} %reduce_sum.12), channel_id=1, source_target_pairs={{0,32},{32,64},{64,96},{96,0},{1,33},{33,65},{65,97},{97,1},{2,34}... | collective-permute-start | bytes 98312 | tf_op jit(solution)/shard_map/ppermute | solution.py:28
  29.7 3.2 %collective-permute-done.2 = bf16[16,1024]{1,0:T(8,128)(2,1)S(1)} collective-permute-done((bf16[16,1024]{1,0:T(8,128)(2,1)S(1)}, bf16[16,1024]{1,0:T(8,128)(2,1)S(1)}, u32[]{:S(2)}, u32[]{:S(2)}) %collective-permute-start.2) | collective-permute-done | bytes 32800 | tf_op jit(solution)/shard_map/ppermute | solution.py:28
  32.9 0.0 collective-permute-done.1
  32.9 0.0 collective-permute-done
  32.9 0.0 collective-permute-done.3
  32.9 0.0 collective-permute-done.4
  32.9 2.9 %collective-permute-start.5 = (bf16[4,16,1024]{2,1,0:T(8,128)(2,1)S(1)}, bf16[4,16,1024]{2,1,0:T(8,128)(2,1)S(1)}, u32[]{:S(2)}, u32[]{:S(2)}) collective-permute-start(bf16[4,16,1024]{2,1,0:T(8,128)(2,1)S(1)} %pad_maximum_fusion.refs_0_), channel_id=1, source_target_pairs={{0,4},{4,0},{1,5},{5,1},{2,6},{6,2},{3,7},{7,3},{8,12},{12,8},{9,1... | collective-permute-start | bytes 393224 | tf_op jit(solution)/shard_map/ppermute | solution.py:24
  35.8 2.9 %collective-permute-start.8 = (bf16[4,16,1024]{2,1,0:T(8,128)(2,1)S(1)}, bf16[4,16,1024]{2,1,0:T(8,128)(2,1)S(1)}, u32[]{:S(2)}, u32[]{:S(2)}) collective-permute-start(bf16[4,16,1024]{2,1,0:T(8,128)(2,1)S(1)} %pad_maximum_fusion.refs_0_), channel_id=1, source_target_pairs={{0,2},{1,3},{2,0},{3,1},{4,6},{5,7},{6,4},{7,5},{8,10},{9,11},{10,... | collective-permute-start | bytes 393224 | tf_op jit(solution)/shard_map/ppermute | solution.py:28
  38.8 1.2 %collective-permute-start.7 = (bf16[4,16,1024]{2,1,0:T(8,128)(2,1)S(1)}, bf16[4,16,1024]{2,1,0:T(8,128)(2,1)S(1)}, u32[]{:S(2)}, u32[]{:S(2)}) collective-permute-start(bf16[4,16,1024]{2,1,0:T(8,128)(2,1)S(1)} %pad_maximum_fusion.refs_0_), channel_id=1, source_target_pairs={{0,3},{1,0},{2,1},{3,2},{4,7},{5,4},{6,5},{7,6},{8,11},{9,8},{10,9... | collective-permute-start | bytes 393224 | tf_op jit(solution)/shard_map/ppermute | solution.py:28
  40.0 0.0 collective-permute-done.5.refs_1_
  40.0 2.1 %collective-permute-start.12 = (bf16[2,448,128]{2,1,0:T(8,128)(2,1)S(1)}, bf16[2,448,128]{2,1,0:T(8,128)(2,1)S(1)}, u32[]{:S(2)}, u32[]{:S(2)}) collective-permute-start(bf16[2,448,128]{2,1,0:T(8,128)(2,1)S(1)} %get-tuple-element.30), channel_id=1, source_target_pairs={{0,64},{32,96},{64,0},{96,32},{1,65},{33,97},{65,1},{97,33},{2,66}... | collective-permute-start | bytes 688136 | tf_op jit(solution)/shard_map/ppermute | solution.py:28
  42.0 0.9 collective-permute-start.6
  42.9 2.4 %collective-permute-start.11 = (bf16[4,16,1024]{2,1,0:T(8,128)(2,1)S(1)}, bf16[4,16,1024]{2,1,0:T(8,128)(2,1)S(1)}, u32[]{:S(2)}, u32[]{:S(2)}) collective-permute-start(bf16[4,16,1024]{2,1,0:T(8,128)(2,1)S(1)} %collective-permute-done.5.refs_1_), channel_id=1, source_target_pairs={{0,2},{1,3},{2,0},{3,1},{4,6},{5,7},{6,4},{7,5},{8,10},{9,11},{10,... | collective-permute-start | bytes 393224 | tf_op jit(solution)/shard_map/ppermute | solution.py:28
  45.3 0.0 collective-permute-done.8.refs_4_
  45.3 1.7 %collective-permute-start.10 = (bf16[4,16,1024]{2,1,0:T(8,128)(2,1)S(1)}, bf16[4,16,1024]{2,1,0:T(8,128)(2,1)S(1)}, u32[]{:S(2)}, u32[]{:S(2)}) collective-permute-start(bf16[4,16,1024]{2,1,0:T(8,128)(2,1)S(1)} %collective-permute-done.5.refs_1_), channel_id=1, source_target_pairs={{0,3},{1,0},{2,1},{3,2},{4,7},{5,4},{6,5},{7,6},{8,11},{9,8},{10,9... | collective-permute-start | bytes 393224 | tf_op jit(solution)/shard_map/ppermute | solution.py:28
  47.0 0.0 collective-permute-done.7.refs_3_
  47.0 0.3 collective-permute-start.9
  47.3 0.1 stack.62.place_ref
  47.4 3.5 %collective-permute-done.6.refs_2_ = bf16[4,16,1024]{2,1,0:T(8,128)(2,1)S(1)} collective-permute-done((bf16[4,16,1024]{2,1,0:T(8,128)(2,1)S(1)}, bf16[4,16,1024]{2,1,0:T(8,128)(2,1)S(1)}, u32[]{:S(2)}, u32[]{:S(2)}) %collective-permute-start.6) | collective-permute-done | bytes 131104 | tf_op jit(solution)/shard_map/ppermute | solution.py:28
  50.9 0.0 collective-permute-done.11.refs_7_
  50.9 0.0 collective-permute-done.10.refs_6_
  50.9 2.3 %collective-permute-done.9.refs_5_ = bf16[4,16,1024]{2,1,0:T(8,128)(2,1)S(1)} collective-permute-done((bf16[4,16,1024]{2,1,0:T(8,128)(2,1)S(1)}, bf16[4,16,1024]{2,1,0:T(8,128)(2,1)S(1)}, u32[]{:S(2)}, u32[]{:S(2)}) %collective-permute-start.9) | collective-permute-done | bytes 131104 | tf_op jit(solution)/shard_map/ppermute | solution.py:28
  53.2 0.9 collective-permute-done.12
  54.0 1.3 %shard_map.77 = bf16[4,112,1024]{2,1,0:T(8,128)(2,1)S(1)} custom-call(s32[11]{0:T(128)S(1)} %stack.62.place_ref, bf16[4,16,1024]{2,1,0:T(8,128)(2,1)S(1)} %pad_maximum_fusion.refs_0_, bf16[4,16,1024]{2,1,0:T(8,128)(2,1)S(1)} %collective-permute-done.5.refs_1_, bf16[4,16,1024]{2,1,0:T(8,128)(2,1)S(1)} %collective-permute-done.6.refs_2_, ...), custom_call_target="tpu_custom_call" | custom-call | tf_op jit(solution)/shard_map/pallas_call | solution.py:190
  55.3 0.0 copy-start.3
  55.3 0.0 copy-start.1
  55.3 0.1 collective-permute-start.13
  55.4 2.5 %collective-permute-done.13.refs_12_ = bf16[4,112,1024]{2,1,0:T(8,128)(2,1)S(1)} collective-permute-done((bf16[4,112,1024]{2,1,0:T(8,128)(2,1)S(1)}, bf16[4,112,1024]{2,1,0:T(8,128)(2,1)S(1)}, u32[]{:S(2)}, u32[]{:S(2)}) %collective-permute-start.13) | collective-permute-done | bytes 917536 | tf_op jit(solution)/shard_map/ppermute | solution.py:24
  57.9 1.3 %shard_map.78 = (f32[112,1024]{1,0:T(8,128)S(1)}, bf16[112,1024]{1,0:T(8,128)(2,1)S(1)}, bf16[112,1024]{1,0:T(8,128)(2,1)S(1)}, bf16[112,1024]{1,0:T(8,128)(2,1)S(1)}) custom-call(s32[11]{0:T(128)S(1)} %stack.62.place_ref, bf16[4,16,1024]{2,1,0:T(8,128)(2,1)S(1)} %pad_maximum_fusion.refs_0_, bf16[4,16,1024]{2,1,0:T(8,128)(2,1)S(1)} %collective-permute-done.5.refs_1_, ...), custom_call_target="tpu_custom_call" | custom-call | tf_op jit(solution)/shard_map/pallas_call | solution.py:194
  59.2 0.8 collective-permute-start.14
  59.9 0.7 collective-permute-start.15
  60.7 2.1 %collective-permute-start.16 = (bf16[112,1024]{1,0:T(8,128)(2,1)S(1)}, bf16[112,1024]{1,0:T(8,128)(2,1)S(1)}, u32[]{:S(2)}, u32[]{:S(2)}) collective-permute-start(bf16[112,1024]{1,0:T(8,128)(2,1)S(1)} %get-tuple-element.35), channel_id=1, source_target_pairs={{0,144},{16,128},{128,16},{144,0},{1,145},{17,129},{129,17},{145,1... | collective-permute-start | bytes 688136 | tf_op jit(solution)/shard_map/ppermute | solution.py:197
  62.7 4.2 %collective-permute-done.14.over_y_ref = bf16[112,1024]{1,0:T(8,128)(2,1)S(1)} collective-permute-done((bf16[112,1024]{1,0:T(8,128)(2,1)S(1)}, bf16[112,1024]{1,0:T(8,128)(2,1)S(1)}, u32[]{:S(2)}, u32[]{:S(2)}) %collective-permute-start.14) | collective-permute-done | bytes 229408 | tf_op jit(solution)/shard_map/ppermute | solution.py:24
  66.9 1.5 %collective-permute-done.15.over_z_ref = bf16[112,1024]{1,0:T(8,128)(2,1)S(1)} collective-permute-done((bf16[112,1024]{1,0:T(8,128)(2,1)S(1)}, bf16[112,1024]{1,0:T(8,128)(2,1)S(1)}, u32[]{:S(2)}, u32[]{:S(2)}) %collective-permute-start.15) | collective-permute-done | bytes 229408 | tf_op jit(solution)/shard_map/ppermute | solution.py:24
  68.4 4.6 %collective-permute-done.16.over_both_ref = bf16[112,1024]{1,0:T(8,128)(2,1)S(1)} collective-permute-done((bf16[112,1024]{1,0:T(8,128)(2,1)S(1)}, bf16[112,1024]{1,0:T(8,128)(2,1)S(1)}, u32[]{:S(2)}, u32[]{:S(2)}) %collective-permute-start.16) | collective-permute-done | bytes 229408 | tf_op jit(solution)/shard_map/ppermute | solution.py:197
  73.0 0.0 copy-done.3
  73.0 1.2 %shard_map.79 = (bf16[112,1024]{1,0:T(8,128)(2,1)S(1)}, f32[1,112,1024]{2,1,0:T(8,128)}, f32[1,112,1024]{2,1,0:T(8,128)}) custom-call(f32[112,1024]{1,0:T(8,128)S(1)} %get-tuple-element.32.own_ref, bf16[112,1024]{1,0:T(8,128)(2,1)S(1)} %collective-permute-done.14.over_y_ref, bf16[112,1024]{1,0:T(8,128)(2,1)S(1)} %collective-permute-done.15.over_z_ref, ...), custom_call_target="tpu_custom_call" | custom-call | tf_op jit(solution)/shard_map/pallas_call | solution.py:200
  74.2 2.3 %collective-permute-start.17 = (bf16[112,1024]{1,0:T(8,128)(2,1)S(1)}, bf16[112,1024]{1,0:T(8,128)(2,1)S(1)}, u32[]{:S(2)}, u32[]{:S(2)}) collective-permute-start(bf16[112,1024]{1,0:T(8,128)(2,1)S(1)} %get-tuple-element.36.refs_0_), channel_id=1, source_target_pairs={{0,4},{4,0},{1,5},{5,1},{2,6},{6,2},{3,7},{7,3},{8,12},{12,8},{9,1... | collective-permute-start | bytes 688136 | tf_op jit(solution)/shard_map/ppermute | solution.py:24
  76.5 2.9 %collective-permute-start.23 = (bf16[112,1024]{1,0:T(8,128)(2,1)S(1)}, bf16[112,1024]{1,0:T(8,128)(2,1)S(1)}, u32[]{:S(2)}, u32[]{:S(2)}) collective-permute-start(bf16[112,1024]{1,0:T(8,128)(2,1)S(1)} %get-tuple-element.36.refs_0_), channel_id=1, source_target_pairs={{0,2},{1,3},{2,0},{3,1},{4,6},{5,7},{6,4},{7,5},{8,10},{9,11},{10,... | collective-permute-start | bytes 688136 | tf_op jit(solution)/shard_map/ppermute | solution.py:28
  79.4 1.2 %collective-permute-start.22 = (bf16[112,1024]{1,0:T(8,128)(2,1)S(1)}, bf16[112,1024]{1,0:T(8,128)(2,1)S(1)}, u32[]{:S(2)}, u32[]{:S(2)}) collective-permute-start(bf16[112,1024]{1,0:T(8,128)(2,1)S(1)} %get-tuple-element.36.refs_0_), channel_id=1, source_target_pairs={{0,3},{1,0},{2,1},{3,2},{4,7},{5,4},{6,5},{7,6},{8,11},{9,8},{10,9... | collective-permute-start | bytes 688136 | tf_op jit(solution)/shard_map/ppermute | solution.py:28
  80.6 0.9 collective-permute-start.21
  81.5 0.7 collective-permute-done.17.refs_1_
  82.2 2.0 %collective-permute-start.20 = (bf16[112,1024]{1,0:T(8,128)(2,1)S(1)}, bf16[112,1024]{1,0:T(8,128)(2,1)S(1)}, u32[]{:S(2)}, u32[]{:S(2)}) collective-permute-start(bf16[112,1024]{1,0:T(8,128)(2,1)S(1)} %collective-permute-done.17.refs_1_), channel_id=1, source_target_pairs={{0,2},{1,3},{2,0},{3,1},{4,6},{5,7},{6,4},{7,5},{8,10},{9,11},{10,... | collective-permute-start | bytes 688136 | tf_op jit(solution)/shard_map/ppermute | solution.py:28
  84.2 1.3 %collective-permute-start.19 = (bf16[112,1024]{1,0:T(8,128)(2,1)S(1)}, bf16[112,1024]{1,0:T(8,128)(2,1)S(1)}, u32[]{:S(2)}, u32[]{:S(2)}) collective-permute-start(bf16[112,1024]{1,0:T(8,128)(2,1)S(1)} %collective-permute-done.17.refs_1_), channel_id=1, source_target_pairs={{0,3},{1,0},{2,1},{3,2},{4,7},{5,4},{6,5},{7,6},{8,11},{9,8},{10,9... | collective-permute-start | bytes 688136 | tf_op jit(solution)/shard_map/ppermute | solution.py:28
  85.5 1.0 collective-permute-done.23.refs_4_
  86.6 1.4 %collective-permute-start.18 = (bf16[112,1024]{1,0:T(8,128)(2,1)S(1)}, bf16[112,1024]{1,0:T(8,128)(2,1)S(1)}, u32[]{:S(2)}, u32[]{:S(2)}) collective-permute-start(bf16[112,1024]{1,0:T(8,128)(2,1)S(1)} %collective-permute-done.17.refs_1_), channel_id=1, source_target_pairs={{0,1},{1,2},{2,3},{3,0},{4,5},{5,6},{6,7},{7,4},{8,9},{9,10},{10,1... | collective-permute-start | bytes 688136 | tf_op jit(solution)/shard_map/ppermute | solution.py:28
  88.0 3.5 %collective-permute-done.22.refs_3_ = bf16[112,1024]{1,0:T(8,128)(2,1)S(1)} collective-permute-done((bf16[112,1024]{1,0:T(8,128)(2,1)S(1)}, bf16[112,1024]{1,0:T(8,128)(2,1)S(1)}, u32[]{:S(2)}, u32[]{:S(2)}) %collective-permute-start.22) | collective-permute-done | bytes 229408 | tf_op jit(solution)/shard_map/ppermute | solution.py:28
  91.5 3.9 %collective-permute-done.21.refs_2_ = bf16[112,1024]{1,0:T(8,128)(2,1)S(1)} collective-permute-done((bf16[112,1024]{1,0:T(8,128)(2,1)S(1)}, bf16[112,1024]{1,0:T(8,128)(2,1)S(1)}, u32[]{:S(2)}, u32[]{:S(2)}) %collective-permute-start.21) | collective-permute-done | bytes 229408 | tf_op jit(solution)/shard_map/ppermute | solution.py:28
  95.3 3.0 %shard_map.80.refs_3_ = bf16[8,112,1024]{2,1,0:T(8,128)(2,1)} custom-call(s32[11]{0:T(128)S(1)} %stack.62.place_ref, bf16[1024,1024]{1,0:T(8,128)(2,1)S(1)} %copy-done.1, bf16[112,1024]{1,0:T(8,128)(2,1)S(1)} %get-tuple-element.36.refs_0_, bf16[112,1024]{1,0:T(8,128)(2,1)S(1)} %collective-permute-done.17.refs_1_, ...), custom_call_target="tpu_custom_call" | custom-call | tf_op jit(solution)/shard_map/pallas_call | solution.py:129
  98.3 0.0 collective-permute-done.20.refs_2_
  98.3 0.6 collective-permute-done.19.refs_1_
  99.0 0.3 collective-permute-done.18.refs_0_
  99.3 2.3 %shard_map.81 = bf16[8,112,1024]{2,1,0:T(8,128)(2,1)} custom-call(s32[11]{0:T(128)S(1)} %stack.62.place_ref, bf16[1024,1024]{1,0:T(8,128)(2,1)S(1)} %copy-done.1, bf16[112,1024]{1,0:T(8,128)(2,1)S(1)} %collective-permute-done.18.refs_0_, bf16[112,1024]{1,0:T(8,128)(2,1)S(1)} %collective-permute-done.19.refs_1_, ...), custom_call_target="tpu_custom_call", output_to_operand_aliasing={{}: (5, {})} | custom-call | tf_op jit(solution)/shard_map/pallas_call | solution.py:129
  (6 shorter events, 0.1 us)
Async XLA Ops:
  0.6 1.0 copy-start
  0.6 10.6 %copy-start.2 = (bf16[128,1,3584]{2,0,1:T(8,128)(2,1)S(1)}, bf16[128,1,3584]{2,0,1:T(8,128)(2,1)}, u32[]{:S(2)}) copy-start(bf16[128,1,3584]{2,0,1:T(8,128)(2,1)} %param.7) | copy-start | bytes 2752516
  4.3 15.7 %all-to-all-start = ((bf16[8,16,1024]{2,1,0:T(8,128)(2,1)}), bf16[8,16,1024]{2,1,0:T(8,128)(2,1)S(1)}, u32[]{:S(2)}, u32[]{:S(2)}) async-start(bf16[8,16,1024]{2,1,0:T(8,128)(2,1)} %bitcast.11), calls=%async_computation | async-start | bytes 524288 | tf_op jit(solution)/shard_map/all_to_all | solution.py:170
  11.7 21.2 %collective-permute-start.3 = (bf16[2,448,128]{2,1,0:T(8,128)(2,1)S(1)}, bf16[2,448,128]{2,1,0:T(8,128)(2,1)S(1)}, u32[]{:S(2)}, u32[]{:S(2)}) collective-permute-start(bf16[2,448,128]{2,1,0:T(8,128)(2,1)S(1)} %get-tuple-element.23), channel_id=1, source_target_pairs={{0,32},{32,64},{64,96},{96,0},{1,33},{33,65},{65,97},{97,1},{2,34}... | collective-permute-start | bytes 688136 | tf_op jit(solution)/shard_map/ppermute | solution.py:28
  16.3 16.7 %collective-permute-start.4 = (bf16[2,448,128]{2,1,0:T(8,128)(2,1)S(1)}, bf16[2,448,128]{2,1,0:T(8,128)(2,1)S(1)}, u32[]{:S(2)}, u32[]{:S(2)}) collective-permute-start(bf16[2,448,128]{2,1,0:T(8,128)(2,1)S(1)} %get-tuple-element.24), channel_id=1, source_target_pairs={{0,96},{32,0},{64,32},{96,64},{1,97},{33,1},{65,33},{97,65},{2,98}... | collective-permute-start | bytes 688136 | tf_op jit(solution)/shard_map/ppermute | solution.py:28
  20.1 12.8 %collective-permute-start.2 = (bf16[16,1024]{1,0:T(8,128)(2,1)S(1)}, bf16[16,1024]{1,0:T(8,128)(2,1)S(1)}, u32[]{:S(2)}, u32[]{:S(2)}) collective-permute-start(bf16[16,1024]{1,0:T(8,128)(2,1)S(1)} %reduce_sum.12), channel_id=1, source_target_pairs={{0,96},{32,0},{64,32},{96,64},{1,97},{33,1},{65,33},{97,65},{2,98}... | collective-permute-start | bytes 98312 | tf_op jit(solution)/shard_map/ppermute | solution.py:28
  20.2 12.7 %collective-permute-start.1 = (bf16[16,1024]{1,0:T(8,128)(2,1)S(1)}, bf16[16,1024]{1,0:T(8,128)(2,1)S(1)}, u32[]{:S(2)}, u32[]{:S(2)}) collective-permute-start(bf16[16,1024]{1,0:T(8,128)(2,1)S(1)} %reduce_sum.12), channel_id=1, source_target_pairs={{0,64},{32,96},{64,0},{96,32},{1,65},{33,97},{65,1},{97,33},{2,66}... | collective-permute-start | bytes 98312 | tf_op jit(solution)/shard_map/ppermute | solution.py:28
  27.0 5.9 %collective-permute-start = (bf16[16,1024]{1,0:T(8,128)(2,1)S(1)}, bf16[16,1024]{1,0:T(8,128)(2,1)S(1)}, u32[]{:S(2)}, u32[]{:S(2)}) collective-permute-start(bf16[16,1024]{1,0:T(8,128)(2,1)S(1)} %reduce_sum.12), channel_id=1, source_target_pairs={{0,32},{32,64},{64,96},{96,0},{1,33},{33,65},{65,97},{97,1},{2,34}... | collective-permute-start | bytes 98312 | tf_op jit(solution)/shard_map/ppermute | solution.py:28
  32.9 7.0 %collective-permute-start.5 = (bf16[4,16,1024]{2,1,0:T(8,128)(2,1)S(1)}, bf16[4,16,1024]{2,1,0:T(8,128)(2,1)S(1)}, u32[]{:S(2)}, u32[]{:S(2)}) collective-permute-start(bf16[4,16,1024]{2,1,0:T(8,128)(2,1)S(1)} %pad_maximum_fusion.refs_0_), channel_id=1, source_target_pairs={{0,4},{4,0},{1,5},{5,1},{2,6},{6,2},{3,7},{7,3},{8,12},{12,8},{9,1... | collective-permute-start | bytes 393224 | tf_op jit(solution)/shard_map/ppermute | solution.py:24
  35.8 9.4 %collective-permute-start.8 = (bf16[4,16,1024]{2,1,0:T(8,128)(2,1)S(1)}, bf16[4,16,1024]{2,1,0:T(8,128)(2,1)S(1)}, u32[]{:S(2)}, u32[]{:S(2)}) collective-permute-start(bf16[4,16,1024]{2,1,0:T(8,128)(2,1)S(1)} %pad_maximum_fusion.refs_0_), channel_id=1, source_target_pairs={{0,2},{1,3},{2,0},{3,1},{4,6},{5,7},{6,4},{7,5},{8,10},{9,11},{10,... | collective-permute-start | bytes 393224 | tf_op jit(solution)/shard_map/ppermute | solution.py:28
  38.8 8.2 %collective-permute-start.7 = (bf16[4,16,1024]{2,1,0:T(8,128)(2,1)S(1)}, bf16[4,16,1024]{2,1,0:T(8,128)(2,1)S(1)}, u32[]{:S(2)}, u32[]{:S(2)}) collective-permute-start(bf16[4,16,1024]{2,1,0:T(8,128)(2,1)S(1)} %pad_maximum_fusion.refs_0_), channel_id=1, source_target_pairs={{0,3},{1,0},{2,1},{3,2},{4,7},{5,4},{6,5},{7,6},{8,11},{9,8},{10,9... | collective-permute-start | bytes 393224 | tf_op jit(solution)/shard_map/ppermute | solution.py:28
  40.0 14.1 %collective-permute-start.12 = (bf16[2,448,128]{2,1,0:T(8,128)(2,1)S(1)}, bf16[2,448,128]{2,1,0:T(8,128)(2,1)S(1)}, u32[]{:S(2)}, u32[]{:S(2)}) collective-permute-start(bf16[2,448,128]{2,1,0:T(8,128)(2,1)S(1)} %get-tuple-element.30), channel_id=1, source_target_pairs={{0,64},{32,96},{64,0},{96,32},{1,65},{33,97},{65,1},{97,33},{2,66}... | collective-permute-start | bytes 688136 | tf_op jit(solution)/shard_map/ppermute | solution.py:28
  42.0 8.9 %collective-permute-start.6 = (bf16[4,16,1024]{2,1,0:T(8,128)(2,1)S(1)}, bf16[4,16,1024]{2,1,0:T(8,128)(2,1)S(1)}, u32[]{:S(2)}, u32[]{:S(2)}) collective-permute-start(bf16[4,16,1024]{2,1,0:T(8,128)(2,1)S(1)} %pad_maximum_fusion.refs_0_), channel_id=1, source_target_pairs={{0,1},{1,2},{2,3},{3,0},{4,5},{5,6},{6,7},{7,4},{8,9},{9,10},{10,1... | collective-permute-start | bytes 393224 | tf_op jit(solution)/shard_map/ppermute | solution.py:28
  42.9 8.0 %collective-permute-start.11 = (bf16[4,16,1024]{2,1,0:T(8,128)(2,1)S(1)}, bf16[4,16,1024]{2,1,0:T(8,128)(2,1)S(1)}, u32[]{:S(2)}, u32[]{:S(2)}) collective-permute-start(bf16[4,16,1024]{2,1,0:T(8,128)(2,1)S(1)} %collective-permute-done.5.refs_1_), channel_id=1, source_target_pairs={{0,2},{1,3},{2,0},{3,1},{4,6},{5,7},{6,4},{7,5},{8,10},{9,11},{10,... | collective-permute-start | bytes 393224 | tf_op jit(solution)/shard_map/ppermute | solution.py:28
  45.3 5.6 %collective-permute-start.10 = (bf16[4,16,1024]{2,1,0:T(8,128)(2,1)S(1)}, bf16[4,16,1024]{2,1,0:T(8,128)(2,1)S(1)}, u32[]{:S(2)}, u32[]{:S(2)}) collective-permute-start(bf16[4,16,1024]{2,1,0:T(8,128)(2,1)S(1)} %collective-permute-done.5.refs_1_), channel_id=1, source_target_pairs={{0,3},{1,0},{2,1},{3,2},{4,7},{5,4},{6,5},{7,6},{8,11},{9,8},{10,9... | collective-permute-start | bytes 393224 | tf_op jit(solution)/shard_map/ppermute | solution.py:28
  47.0 6.2 %collective-permute-start.9 = (bf16[4,16,1024]{2,1,0:T(8,128)(2,1)S(1)}, bf16[4,16,1024]{2,1,0:T(8,128)(2,1)S(1)}, u32[]{:S(2)}, u32[]{:S(2)}) collective-permute-start(bf16[4,16,1024]{2,1,0:T(8,128)(2,1)S(1)} %collective-permute-done.5.refs_1_), channel_id=1, source_target_pairs={{0,1},{1,2},{2,3},{3,0},{4,5},{5,6},{6,7},{7,4},{8,9},{9,10},{10,1... | collective-permute-start | bytes 393224 | tf_op jit(solution)/shard_map/ppermute | solution.py:28
  54.0 19.0 %copy-start.4 = (f32[1,112,1024]{2,1,0:T(8,128)S(1)}, f32[1,112,1024]{2,1,0:T(8,128)}, u32[]{:S(2)}) copy-start(f32[1,112,1024]{2,1,0:T(8,128)} %second_ref.1) | copy-start | bytes 1376260
  55.3 17.7 %copy-start.3 = (f32[1,112,1024]{2,1,0:T(8,128)S(1)}, f32[1,112,1024]{2,1,0:T(8,128)}, u32[]{:S(2)}) copy-start(f32[1,112,1024]{2,1,0:T(8,128)} %first_ref.1) | copy-start | bytes 1376260
  55.3 40.0 %copy-start.1 = (bf16[1024,1024]{1,0:T(8,128)(2,1)S(1)}, bf16[1024,1024]{1,0:T(8,128)(2,1)}, u32[]{:S(2)}) copy-start(bf16[1024,1024]{1,0:T(8,128)(2,1)} %projector_ref.3) | copy-start | bytes 6291460
  55.3 2.6 %collective-permute-start.13 = (bf16[4,112,1024]{2,1,0:T(8,128)(2,1)S(1)}, bf16[4,112,1024]{2,1,0:T(8,128)(2,1)S(1)}, u32[]{:S(2)}, u32[]{:S(2)}) collective-permute-start(bf16[4,112,1024]{2,1,0:T(8,128)(2,1)S(1)} %shard_map.77), channel_id=1, source_target_pairs={{0,8},{8,0},{1,9},{9,1},{2,10},{10,2},{3,11},{11,3},{4,12},{12,4},... | collective-permute-start | bytes 2752520 | tf_op jit(solution)/shard_map/ppermute | solution.py:24
  59.2 7.7 %collective-permute-start.14 = (bf16[112,1024]{1,0:T(8,128)(2,1)S(1)}, bf16[112,1024]{1,0:T(8,128)(2,1)S(1)}, u32[]{:S(2)}, u32[]{:S(2)}) collective-permute-start(bf16[112,1024]{1,0:T(8,128)(2,1)S(1)} %get-tuple-element.33), channel_id=1, source_target_pairs={{0,128},{128,0},{1,129},{129,1},{2,130},{130,2},{3,131},{131,3},{4... | collective-permute-start | bytes 688136 | tf_op jit(solution)/shard_map/ppermute | solution.py:24
  59.9 8.5 %collective-permute-start.15 = (bf16[112,1024]{1,0:T(8,128)(2,1)S(1)}, bf16[112,1024]{1,0:T(8,128)(2,1)S(1)}, u32[]{:S(2)}, u32[]{:S(2)}) collective-permute-start(bf16[112,1024]{1,0:T(8,128)(2,1)S(1)} %get-tuple-element.34), channel_id=1, source_target_pairs={{0,16},{16,0},{1,17},{17,1},{2,18},{18,2},{3,19},{19,3},{4,20},{20... | collective-permute-start | bytes 688136 | tf_op jit(solution)/shard_map/ppermute | solution.py:24
  60.7 12.3 %collective-permute-start.16 = (bf16[112,1024]{1,0:T(8,128)(2,1)S(1)}, bf16[112,1024]{1,0:T(8,128)(2,1)S(1)}, u32[]{:S(2)}, u32[]{:S(2)}) collective-permute-start(bf16[112,1024]{1,0:T(8,128)(2,1)S(1)} %get-tuple-element.35), channel_id=1, source_target_pairs={{0,144},{16,128},{128,16},{144,0},{1,145},{17,129},{129,17},{145,1... | collective-permute-start | bytes 688136 | tf_op jit(solution)/shard_map/ppermute | solution.py:197
  74.2 8.0 %collective-permute-start.17 = (bf16[112,1024]{1,0:T(8,128)(2,1)S(1)}, bf16[112,1024]{1,0:T(8,128)(2,1)S(1)}, u32[]{:S(2)}, u32[]{:S(2)}) collective-permute-start(bf16[112,1024]{1,0:T(8,128)(2,1)S(1)} %get-tuple-element.36.refs_0_), channel_id=1, source_target_pairs={{0,4},{4,0},{1,5},{5,1},{2,6},{6,2},{3,7},{7,3},{8,12},{12,8},{9,1... | collective-permute-start | bytes 688136 | tf_op jit(solution)/shard_map/ppermute | solution.py:24
  76.5 10.0 %collective-permute-start.23 = (bf16[112,1024]{1,0:T(8,128)(2,1)S(1)}, bf16[112,1024]{1,0:T(8,128)(2,1)S(1)}, u32[]{:S(2)}, u32[]{:S(2)}) collective-permute-start(bf16[112,1024]{1,0:T(8,128)(2,1)S(1)} %get-tuple-element.36.refs_0_), channel_id=1, source_target_pairs={{0,2},{1,3},{2,0},{3,1},{4,6},{5,7},{6,4},{7,5},{8,10},{9,11},{10,... | collective-permute-start | bytes 688136 | tf_op jit(solution)/shard_map/ppermute | solution.py:28
  79.4 12.0 %collective-permute-start.22 = (bf16[112,1024]{1,0:T(8,128)(2,1)S(1)}, bf16[112,1024]{1,0:T(8,128)(2,1)S(1)}, u32[]{:S(2)}, u32[]{:S(2)}) collective-permute-start(bf16[112,1024]{1,0:T(8,128)(2,1)S(1)} %get-tuple-element.36.refs_0_), channel_id=1, source_target_pairs={{0,3},{1,0},{2,1},{3,2},{4,7},{5,4},{6,5},{7,6},{8,11},{9,8},{10,9... | collective-permute-start | bytes 688136 | tf_op jit(solution)/shard_map/ppermute | solution.py:28
  80.6 14.7 %collective-permute-start.21 = (bf16[112,1024]{1,0:T(8,128)(2,1)S(1)}, bf16[112,1024]{1,0:T(8,128)(2,1)S(1)}, u32[]{:S(2)}, u32[]{:S(2)}) collective-permute-start(bf16[112,1024]{1,0:T(8,128)(2,1)S(1)} %get-tuple-element.36.refs_0_), channel_id=1, source_target_pairs={{0,1},{1,2},{2,3},{3,0},{4,5},{5,6},{6,7},{7,4},{8,9},{9,10},{10,1... | collective-permute-start | bytes 688136 | tf_op jit(solution)/shard_map/ppermute | solution.py:28
  82.2 16.1 %collective-permute-start.20 = (bf16[112,1024]{1,0:T(8,128)(2,1)S(1)}, bf16[112,1024]{1,0:T(8,128)(2,1)S(1)}, u32[]{:S(2)}, u32[]{:S(2)}) collective-permute-start(bf16[112,1024]{1,0:T(8,128)(2,1)S(1)} %collective-permute-done.17.refs_1_), channel_id=1, source_target_pairs={{0,2},{1,3},{2,0},{3,1},{4,6},{5,7},{6,4},{7,5},{8,10},{9,11},{10,... | collective-permute-start | bytes 688136 | tf_op jit(solution)/shard_map/ppermute | solution.py:28
  84.2 14.8 %collective-permute-start.19 = (bf16[112,1024]{1,0:T(8,128)(2,1)S(1)}, bf16[112,1024]{1,0:T(8,128)(2,1)S(1)}, u32[]{:S(2)}, u32[]{:S(2)}) collective-permute-start(bf16[112,1024]{1,0:T(8,128)(2,1)S(1)} %collective-permute-done.17.refs_1_), channel_id=1, source_target_pairs={{0,3},{1,0},{2,1},{3,2},{4,7},{5,4},{6,5},{7,6},{8,11},{9,8},{10,9... | collective-permute-start | bytes 688136 | tf_op jit(solution)/shard_map/ppermute | solution.py:28
  86.6 12.7 %collective-permute-start.18 = (bf16[112,1024]{1,0:T(8,128)(2,1)S(1)}, bf16[112,1024]{1,0:T(8,128)(2,1)S(1)}, u32[]{:S(2)}, u32[]{:S(2)}) collective-permute-start(bf16[112,1024]{1,0:T(8,128)(2,1)S(1)} %collective-permute-done.17.refs_1_), channel_id=1, source_target_pairs={{0,1},{1,2},{2,3},{3,0},{4,5},{5,6},{6,7},{7,4},{8,9},{9,10},{10,1... | collective-permute-start | bytes 688136 | tf_op jit(solution)/shard_map/ppermute | solution.py:28

commit v4 on v3

--- a/solution.py
+++ b/solution.py
@@ -93,7 +93,7 @@
     )
 
 
-def adam_kernel(own_ref, over_y_ref, over_z_ref, over_both_ref, first_ref, second_ref, *outs):
+def adam_kernel(own_ref, over_both_ref, over_z_ref, over_y_ref, first_ref, second_ref, *outs):
     gradient = own_ref[...] + over_y_ref[...].astype(wide)
     gradient = gradient + over_z_ref[...].astype(wide) + over_both_ref[...].astype(wide)
     first_new = 0.9 * first_ref[0] + 0.1 * gradient
@@ -142,12 +142,9 @@
 
 def gathered(value, other=None):
     other = swap(value, "yhi") if other is None else other
-    steps = (1, 3, 2)
-    return (
-        [value, other]
-        + [shift(value, "x", X, step) for step in steps]
-        + [shift(other, "x", X, step) for step in steps]
-    )
+    mine = [shift(value, "x", X, step) for step in (1, 3, 2)]
+    rest = [shift(other, "x", X, step) for step in (1, 3)] + [swap(mine[2], "yhi")]
+    return [value, other] + mine + rest
 
 
 def gathered_from(yhi, x):
@@ -194,8 +191,8 @@
     own, over_y, over_z, over_both = gradient_call(
         keep_kernel, [(one, wide)] + [(one, narrow)] * 3, tokens, rank, 1
     )(place, *projected, *grads, came)
+    over_y, over_z = swap(over_y, "ylo"), swap(over_z, "zl")
     over_both = lax.ppermute(over_both, ("ylo", "zl"), [(i, 3 - i) for i in range(4)])
-    over_y, over_z = swap(over_y, "ylo"), swap(over_z, "zl")
     moment = jax.ShapeDtypeStruct((1,) + one, wide)
     direction, first_new, second_new = pl.pallas_call(
         adam_kernel,
@@ -203,7 +200,7 @@
         in_specs=[VMEM] * 6,
         out_specs=[VMEM] * 3,
         compiler_params=pltpu.CompilerParams(vmem_limit_bytes=16 * 2**20),
-    )(own, over_y, over_z, over_both, first_moment, second_moment)
+    )(own, over_both, over_z, over_y, first_moment, second_moment)
     directions = gathered(direction)
     weight_update = back(place, projector, directions[:5], 0, None)
     weight_update = back(place, projector, directions[5:], 5, weight_update)

time: 103 us -> 98.8 us (0.959)
  waiting for transfers between devices: 36.4 us -> 32.4 us
    ppermute x5 -> x7, starting transfers between devices: 6.85 us -> 14 us  [swap(): return lax.ppermute(value, axis, [(0, 1), (1, 0)])]
    ppermute x18 -> x16, waiting for transfers between devices: 19.2 us -> 13.6 us  [shift(): lax.ppermute(value, axis, [(i, (i + step) % size) for i in range(size)])]
    ppermute x18 -> x16, starting transfers between devices: 35.4 us -> 30.1 us  [shift(): lax.ppermute(value, axis, [(i, (i + step) % size) for i in range(size)])]
    ppermute x1, waiting for transfers between devices: 4.58 us -> 5.9 us  [shards(): lax.ppermute(over_both, ('ylo', 'zl'), [(i, 3 - i) for i in range(4)])]
    ppermute x1, starting transfers between devices: 2.08 us -> 0.93 us  [shards(): lax.ppermute(over_both, ('ylo', 'zl'), [(i, 3 - i) for i in range(4)])]
    ppermute x5 -> x7, waiting for transfers between devices: 8.84 us -> 9.09 us  [swap(): return lax.ppermute(value, axis, [(0, 1), (1, 0)])]
  transfers between devices with their start and end apart: 25 -> 25, of which waited for: 15 -> 13; matrix products, arithmetic and copies ran while one was open for 0% -> 0% of each run, Pallas kernels for 3% -> 3%
where the time goes in v4:
time: 98.8 us; the launch traced here: 98.6 us
  starting transfers between devices  52 us (53%)
  waiting for transfers between devices  32.4 us (33%)
  Pallas kernels  9.39 us (10%)
  matrix products  2.74 us (3%)
  local copies, waits for them, and re-layouts  1.04 us (1%)
    ppermute x16, starting transfers between devices, shift(): lax.ppermute(value, axis, [(i, (i + step) % size) for i in range(size)])  30.1 us
    ppermute x7, starting transfers between devices, swap(): return lax.ppermute(value, axis, [(0, 1), (1, 0)])  14 us
    ppermute x16, waiting for transfers between devices, shift(): lax.ppermute(value, axis, [(i, (i + step) % size) for i in range(size)])  13.6 us
    ppermute x7, waiting for transfers between devices, swap(): return lax.ppermute(value, axis, [(0, 1), (1, 0)])  9.09 us
    all_to_all x1, starting transfers between devices, shards(): lax.all_to_all(partial_value.reshape(n_fsdp, tokens // n_fsdp, rank), FSD...  6.93 us
    ppermute x1, waiting for transfers between devices, shards(): lax.ppermute(over_both, ('ylo', 'zl'), [(i, 3 - i) for i in range(4)])  5.9 us
    pallas_call x2, Pallas kernels, back(): pl.pallas_call(functools.partial(back_kernel, count, first), out_shape=ja...  5.28 us
    all_to_all x1, waiting for transfers between devices, shards(): lax.all_to_all(partial_value.reshape(n_fsdp, tokens // n_fsdp, rank), FSD...  3.79 us
  transfers between devices with their start and end apart: 25, of which 13 were waited for; matrix products, arithmetic and copies ran while one was open for 0% of the time, Pallas kernels for 3%

profile of v4, /device:TPU:64, one launch (start us, length us, event | category | flops | bytes accessed | tf_op | source)
XLA Modules:
  0.0 98.6 jit_solution(6902258829053075113)
XLA Ops:
  0.6 0.0 copy-start
  0.6 0.0 copy-start.2
  0.7 0.9 copy-done
  1.6 2.7 %convolution_convert_fusion = bf16[128,1024]{1,0:T(8,128)(2,1)} fusion(bf16[128,1024]{1,0:T(8,128)(2,1)S(1)} %copy-done, bf16[1024,1024]{1,0:T(8,128)(2,1)} %projector_ref.3), kind=kOutput, calls=%fused_computation | convolution fusion | flops 268566528 | bytes 2621440 | tf_op jit(solution)/shard_map/dot_general | solution.py:165
  4.3 6.9 %all-to-all-start = ((bf16[8,16,1024]{2,1,0:T(8,128)(2,1)}), bf16[8,16,1024]{2,1,0:T(8,128)(2,1)S(1)}, u32[]{:S(2)}, u32[]{:S(2)}) async-start(bf16[8,16,1024]{2,1,0:T(8,128)(2,1)} %bitcast.11), calls=%async_computation | async-start | bytes 524288 | tf_op jit(solution)/shard_map/all_to_all | solution.py:167
  11.3 0.4 shard_map.76
  11.7 4.6 %collective-permute-start.3 = (bf16[2,448,128]{2,1,0:T(8,128)(2,1)S(1)}, bf16[2,448,128]{2,1,0:T(8,128)(2,1)S(1)}, u32[]{:S(2)}, u32[]{:S(2)}) collective-permute-start(bf16[2,448,128]{2,1,0:T(8,128)(2,1)S(1)} %get-tuple-element.23), channel_id=1, source_target_pairs={{0,32},{32,64},{64,96},{96,0},{1,33},{33,65},{65,97},{97,1},{2,34}... | collective-permute-start | bytes 688136 | tf_op jit(solution)/shard_map/ppermute | solution.py:28
  16.3 0.0 collective-permute-start.4
  16.3 3.8 %all-to-all-done = bf16[8,16,1024]{2,1,0:T(8,128)(2,1)S(1)} async-done(((bf16[8,16,1024]{2,1,0:T(8,128)(2,1)}), bf16[8,16,1024]{2,1,0:T(8,128)(2,1)S(1)}, u32[]{:S(2)}, u32[]{:S(2)}) %all-to-all-start) | async-done | bytes 262176 | tf_op jit(solution)/shard_map/all_to_all | solution.py:167
  20.1 0.1 collective-permute-start.2
  20.2 6.8 %collective-permute-start.1 = (bf16[16,1024]{1,0:T(8,128)(2,1)S(1)}, bf16[16,1024]{1,0:T(8,128)(2,1)S(1)}, u32[]{:S(2)}, u32[]{:S(2)}) collective-permute-start(bf16[16,1024]{1,0:T(8,128)(2,1)S(1)} %reduce_sum.12), channel_id=1, source_target_pairs={{0,64},{32,96},{64,0},{96,32},{1,65},{33,97},{65,1},{97,33},{2,66}... | collective-permute-start | bytes 98312 | tf_op jit(solution)/shard_map/ppermute | solution.py:28
  27.0 2.7 %collective-permute-start = (bf16[16,1024]{1,0:T(8,128)(2,1)S(1)}, bf16[16,1024]{1,0:T(8,128)(2,1)S(1)}, u32[]{:S(2)}, u32[]{:S(2)}) collective-permute-start(bf16[16,1024]{1,0:T(8,128)(2,1)S(1)} %reduce_sum.12), channel_id=1, source_target_pairs={{0,32},{32,64},{64,96},{96,0},{1,33},{33,65},{65,97},{97,1},{2,34}... | collective-permute-start | bytes 98312 | tf_op jit(solution)/shard_map/ppermute | solution.py:28
  29.7 3.2 %collective-permute-done.2 = bf16[16,1024]{1,0:T(8,128)(2,1)S(1)} collective-permute-done((bf16[16,1024]{1,0:T(8,128)(2,1)S(1)}, bf16[16,1024]{1,0:T(8,128)(2,1)S(1)}, u32[]{:S(2)}, u32[]{:S(2)}) %collective-permute-start.2) | collective-permute-done | bytes 32800 | tf_op jit(solution)/shard_map/ppermute | solution.py:28
  32.9 0.0 collective-permute-done.1
  32.9 0.0 collective-permute-done
  32.9 0.0 collective-permute-done.3
  32.9 0.0 collective-permute-done.4
  32.9 2.9 %collective-permute-start.5 = (bf16[4,16,1024]{2,1,0:T(8,128)(2,1)S(1)}, bf16[4,16,1024]{2,1,0:T(8,128)(2,1)S(1)}, u32[]{:S(2)}, u32[]{:S(2)}) collective-permute-start(bf16[4,16,1024]{2,1,0:T(8,128)(2,1)S(1)} %pad_maximum_fusion.refs_0_), channel_id=1, source_target_pairs={{0,4},{4,0},{1,5},{5,1},{2,6},{6,2},{3,7},{7,3},{8,12},{12,8},{9,1... | collective-permute-start | bytes 393224 | tf_op jit(solution)/shard_map/ppermute | solution.py:24
  35.8 2.9 %collective-permute-start.8 = (bf16[4,16,1024]{2,1,0:T(8,128)(2,1)S(1)}, bf16[4,16,1024]{2,1,0:T(8,128)(2,1)S(1)}, u32[]{:S(2)}, u32[]{:S(2)}) collective-permute-start(bf16[4,16,1024]{2,1,0:T(8,128)(2,1)S(1)} %pad_maximum_fusion.refs_0_), channel_id=1, source_target_pairs={{0,2},{1,3},{2,0},{3,1},{4,6},{5,7},{6,4},{7,5},{8,10},{9,11},{10,... | collective-permute-start | bytes 393224 | tf_op jit(solution)/shard_map/ppermute | solution.py:28
  38.8 1.2 %collective-permute-start.7 = (bf16[4,16,1024]{2,1,0:T(8,128)(2,1)S(1)}, bf16[4,16,1024]{2,1,0:T(8,128)(2,1)S(1)}, u32[]{:S(2)}, u32[]{:S(2)}) collective-permute-start(bf16[4,16,1024]{2,1,0:T(8,128)(2,1)S(1)} %pad_maximum_fusion.refs_0_), channel_id=1, source_target_pairs={{0,3},{1,0},{2,1},{3,2},{4,7},{5,4},{6,5},{7,6},{8,11},{9,8},{10,9... | collective-permute-start | bytes 393224 | tf_op jit(solution)/shard_map/ppermute | solution.py:28
  40.0 0.0 collective-permute-done.5.refs_1_
  40.0 2.1 %collective-permute-start.12 = (bf16[2,448,128]{2,1,0:T(8,128)(2,1)S(1)}, bf16[2,448,128]{2,1,0:T(8,128)(2,1)S(1)}, u32[]{:S(2)}, u32[]{:S(2)}) collective-permute-start(bf16[2,448,128]{2,1,0:T(8,128)(2,1)S(1)} %get-tuple-element.30), channel_id=1, source_target_pairs={{0,64},{32,96},{64,0},{96,32},{1,65},{33,97},{65,1},{97,33},{2,66}... | collective-permute-start | bytes 688136 | tf_op jit(solution)/shard_map/ppermute | solution.py:28
  42.0 0.9 collective-permute-start.6
  42.9 2.4 %collective-permute-start.10 = (bf16[4,16,1024]{2,1,0:T(8,128)(2,1)S(1)}, bf16[4,16,1024]{2,1,0:T(8,128)(2,1)S(1)}, u32[]{:S(2)}, u32[]{:S(2)}) collective-permute-start(bf16[4,16,1024]{2,1,0:T(8,128)(2,1)S(1)} %collective-permute-done.5.refs_1_), channel_id=1, source_target_pairs={{0,3},{1,0},{2,1},{3,2},{4,7},{5,4},{6,5},{7,6},{8,11},{9,8},{10,9... | collective-permute-start | bytes 393224 | tf_op jit(solution)/shard_map/ppermute | solution.py:28
  45.3 0.0 collective-permute-done.8.refs_4_
  45.3 2.3 %collective-permute-start.11 = (bf16[4,16,1024]{2,1,0:T(8,128)(2,1)S(1)}, bf16[4,16,1024]{2,1,0:T(8,128)(2,1)S(1)}, u32[]{:S(2)}, u32[]{:S(2)}) collective-permute-start(bf16[4,16,1024]{2,1,0:T(8,128)(2,1)S(1)} %collective-permute-done.8.refs_4_), channel_id=1, source_target_pairs={{0,4},{4,0},{1,5},{5,1},{2,6},{6,2},{3,7},{7,3},{8,12},{12,8},{9,1... | collective-permute-start | bytes 393224 | tf_op jit(solution)/shard_map/ppermute | solution.py:24
  47.6 0.0 collective-permute-done.7.refs_3_
  47.6 0.2 collective-permute-start.9
  47.9 0.1 stack.62.place_ref
  47.9 1.2 %collective-permute-done.6.refs_2_ = bf16[4,16,1024]{2,1,0:T(8,128)(2,1)S(1)} collective-permute-done((bf16[4,16,1024]{2,1,0:T(8,128)(2,1)S(1)}, bf16[4,16,1024]{2,1,0:T(8,128)(2,1)S(1)}, u32[]{:S(2)}, u32[]{:S(2)}) %collective-permute-start.6) | collective-permute-done | bytes 131104 | tf_op jit(solution)/shard_map/ppermute | solution.py:28
  49.2 2.6 %collective-permute-done.11.refs_7_ = bf16[4,16,1024]{2,1,0:T(8,128)(2,1)S(1)} collective-permute-done((bf16[4,16,1024]{2,1,0:T(8,128)(2,1)S(1)}, bf16[4,16,1024]{2,1,0:T(8,128)(2,1)S(1)}, u32[]{:S(2)}, u32[]{:S(2)}) %collective-permute-start.11) | collective-permute-done | bytes 131104 | tf_op jit(solution)/shard_map/ppermute | solution.py:24
  51.7 0.0 collective-permute-done.10.refs_6_
  51.7 2.0 %collective-permute-done.9.refs_5_ = bf16[4,16,1024]{2,1,0:T(8,128)(2,1)S(1)} collective-permute-done((bf16[4,16,1024]{2,1,0:T(8,128)(2,1)S(1)}, bf16[4,16,1024]{2,1,0:T(8,128)(2,1)S(1)}, u32[]{:S(2)}, u32[]{:S(2)}) %collective-permute-start.9) | collective-permute-done | bytes 131104 | tf_op jit(solution)/shard_map/ppermute | solution.py:28
  53.8 0.3 collective-permute-done.12
  54.0 1.3 %shard_map.77 = bf16[4,112,1024]{2,1,0:T(8,128)(2,1)S(1)} custom-call(s32[11]{0:T(128)S(1)} %stack.62.place_ref, bf16[4,16,1024]{2,1,0:T(8,128)(2,1)S(1)} %pad_maximum_fusion.refs_0_, bf16[4,16,1024]{2,1,0:T(8,128)(2,1)S(1)} %collective-permute-done.5.refs_1_, bf16[4,16,1024]{2,1,0:T(8,128)(2,1)S(1)} %collective-permute-done.6.refs_2_, ...), custom_call_target="tpu_custom_call" | custom-call | tf_op jit(solution)/shard_map/pallas_call | solution.py:187
  55.3 0.0 copy-start.3
  55.3 0.0 copy-start.1
  55.3 0.1 collective-permute-start.13
  55.4 2.5 %collective-permute-done.13.refs_12_ = bf16[4,112,1024]{2,1,0:T(8,128)(2,1)S(1)} collective-permute-done((bf16[4,112,1024]{2,1,0:T(8,128)(2,1)S(1)}, bf16[4,112,1024]{2,1,0:T(8,128)(2,1)S(1)}, u32[]{:S(2)}, u32[]{:S(2)}) %collective-permute-start.13) | collective-permute-done | bytes 917536 | tf_op jit(solution)/shard_map/ppermute | solution.py:24
  57.9 1.3 %shard_map.78 = (f32[112,1024]{1,0:T(8,128)S(1)}, bf16[112,1024]{1,0:T(8,128)(2,1)S(1)}, bf16[112,1024]{1,0:T(8,128)(2,1)S(1)}, bf16[112,1024]{1,0:T(8,128)(2,1)S(1)}) custom-call(s32[11]{0:T(128)S(1)} %stack.62.place_ref, bf16[4,16,1024]{2,1,0:T(8,128)(2,1)S(1)} %pad_maximum_fusion.refs_0_, bf16[4,16,1024]{2,1,0:T(8,128)(2,1)S(1)} %collective-permute-done.5.refs_1_, ...), custom_call_target="tpu_custom_call" | custom-call | tf_op jit(solution)/shard_map/pallas_call | solution.py:191
  59.2 0.9 collective-permute-start.14
  60.1 1.3 %collective-permute-start.15 = (bf16[112,1024]{1,0:T(8,128)(2,1)S(1)}, bf16[112,1024]{1,0:T(8,128)(2,1)S(1)}, u32[]{:S(2)}, u32[]{:S(2)}) collective-permute-start(bf16[112,1024]{1,0:T(8,128)(2,1)S(1)} %get-tuple-element.34), channel_id=1, source_target_pairs={{0,16},{16,0},{1,17},{17,1},{2,18},{18,2},{3,19},{19,3},{4,20},{20... | collective-permute-start | bytes 688136 | tf_op jit(solution)/shard_map/ppermute | solution.py:24
  61.4 1.3 %collective-permute-start.16 = (bf16[112,1024]{1,0:T(8,128)(2,1)S(1)}, bf16[112,1024]{1,0:T(8,128)(2,1)S(1)}, u32[]{:S(2)}, u32[]{:S(2)}) collective-permute-start(bf16[112,1024]{1,0:T(8,128)(2,1)S(1)} %get-tuple-element.35), channel_id=1, source_target_pairs={{0,128},{128,0},{1,129},{129,1},{2,130},{130,2},{3,131},{131,3},{4... | collective-permute-start | bytes 688136 | tf_op jit(solution)/shard_map/ppermute | solution.py:24
  62.7 5.9 %collective-permute-done.14.over_both_ref = bf16[112,1024]{1,0:T(8,128)(2,1)S(1)} collective-permute-done((bf16[112,1024]{1,0:T(8,128)(2,1)S(1)}, bf16[112,1024]{1,0:T(8,128)(2,1)S(1)}, u32[]{:S(2)}, u32[]{:S(2)}) %collective-permute-start.14) | collective-permute-done | bytes 229408 | tf_op jit(solution)/shard_map/ppermute | solution.py:195
  68.6 3.3 %collective-permute-done.15.over_z_ref = bf16[112,1024]{1,0:T(8,128)(2,1)S(1)} collective-permute-done((bf16[112,1024]{1,0:T(8,128)(2,1)S(1)}, bf16[112,1024]{1,0:T(8,128)(2,1)S(1)}, u32[]{:S(2)}, u32[]{:S(2)}) %collective-permute-start.15) | collective-permute-done | bytes 229408 | tf_op jit(solution)/shard_map/ppermute | solution.py:24
  72.0 0.7 collective-permute-done.16.over_y_ref
  72.7 0.0 copy-done.3
  72.7 1.2 %shard_map.79 = (bf16[112,1024]{1,0:T(8,128)(2,1)S(1)}, f32[1,112,1024]{2,1,0:T(8,128)}, f32[1,112,1024]{2,1,0:T(8,128)}) custom-call(f32[112,1024]{1,0:T(8,128)S(1)} %get-tuple-element.32.own_ref, bf16[112,1024]{1,0:T(8,128)(2,1)S(1)} %collective-permute-done.14.over_both_ref, bf16[112,1024]{1,0:T(8,128)(2,1)S(1)} %collective-permute-done.15.over_z_ref, ...), custom_call_target="tpu_custom_call" | custom-call | tf_op jit(solution)/shard_map/pallas_call | solution.py:197
  73.9 1.6 %collective-permute-start.20 = (bf16[112,1024]{1,0:T(8,128)(2,1)S(1)}, bf16[112,1024]{1,0:T(8,128)(2,1)S(1)}, u32[]{:S(2)}, u32[]{:S(2)}) collective-permute-start(bf16[112,1024]{1,0:T(8,128)(2,1)S(1)} %get-tuple-element.36.refs_0_), channel_id=1, source_target_pairs={{0,2},{1,3},{2,0},{3,1},{4,6},{5,7},{6,4},{7,5},{8,10},{9,11},{10,... | collective-permute-start | bytes 688136 | tf_op jit(solution)/shard_map/ppermute | solution.py:28
  75.5 3.7 %collective-permute-start.17 = (bf16[112,1024]{1,0:T(8,128)(2,1)S(1)}, bf16[112,1024]{1,0:T(8,128)(2,1)S(1)}, u32[]{:S(2)}, u32[]{:S(2)}) collective-permute-start(bf16[112,1024]{1,0:T(8,128)(2,1)S(1)} %get-tuple-element.36.refs_0_), channel_id=1, source_target_pairs={{0,4},{4,0},{1,5},{5,1},{2,6},{6,2},{3,7},{7,3},{8,12},{12,8},{9,1... | collective-permute-start | bytes 688136 | tf_op jit(solution)/shard_map/ppermute | solution.py:24
  79.2 1.2 %collective-permute-start.23 = (bf16[112,1024]{1,0:T(8,128)(2,1)S(1)}, bf16[112,1024]{1,0:T(8,128)(2,1)S(1)}, u32[]{:S(2)}, u32[]{:S(2)}) collective-permute-start(bf16[112,1024]{1,0:T(8,128)(2,1)S(1)} %get-tuple-element.36.refs_0_), channel_id=1, source_target_pairs={{0,3},{1,0},{2,1},{3,2},{4,7},{5,4},{6,5},{7,6},{8,11},{9,8},{10,9... | collective-permute-start | bytes 688136 | tf_op jit(solution)/shard_map/ppermute | solution.py:28
  80.3 0.9 collective-permute-start.22
  81.2 2.7 %collective-permute-done.20.refs_4_ = bf16[112,1024]{1,0:T(8,128)(2,1)S(1)} collective-permute-done((bf16[112,1024]{1,0:T(8,128)(2,1)S(1)}, bf16[112,1024]{1,0:T(8,128)(2,1)S(1)}, u32[]{:S(2)}, u32[]{:S(2)}) %collective-permute-start.20) | collective-permute-done | bytes 229408 | tf_op jit(solution)/shard_map/ppermute | solution.py:28
  83.9 2.3 %collective-permute-start.21 = (bf16[112,1024]{1,0:T(8,128)(2,1)S(1)}, bf16[112,1024]{1,0:T(8,128)(2,1)S(1)}, u32[]{:S(2)}, u32[]{:S(2)}) collective-permute-start(bf16[112,1024]{1,0:T(8,128)(2,1)S(1)} %collective-permute-done.20.refs_4_), channel_id=1, source_target_pairs={{0,4},{4,0},{1,5},{5,1},{2,6},{6,2},{3,7},{7,3},{8,12},{12,8},{9,1... | collective-permute-start | bytes 688136 | tf_op jit(solution)/shard_map/ppermute | solution.py:24
  86.2 0.0 collective-permute-done.17.refs_1_
  86.2 2.7 %collective-permute-start.19 = (bf16[112,1024]{1,0:T(8,128)(2,1)S(1)}, bf16[112,1024]{1,0:T(8,128)(2,1)S(1)}, u32[]{:S(2)}, u32[]{:S(2)}) collective-permute-start(bf16[112,1024]{1,0:T(8,128)(2,1)S(1)} %collective-permute-done.17.refs_1_), channel_id=1, source_target_pairs={{0,3},{1,0},{2,1},{3,2},{4,7},{5,4},{6,5},{7,6},{8,11},{9,8},{10,9... | collective-permute-start | bytes 688136 | tf_op jit(solution)/shard_map/ppermute | solution.py:28
  88.9 0.0 collective-permute-start.18
  88.9 0.0 collective-permute-done.23.refs_3_
  88.9 0.0 collective-permute-done.22.refs_2_
  88.9 3.0 %shard_map.80.refs_3_ = bf16[8,112,1024]{2,1,0:T(8,128)(2,1)} custom-call(s32[11]{0:T(128)S(1)} %stack.62.place_ref, bf16[1024,1024]{1,0:T(8,128)(2,1)S(1)} %copy-done.1, bf16[112,1024]{1,0:T(8,128)(2,1)S(1)} %get-tuple-element.36.refs_0_, bf16[112,1024]{1,0:T(8,128)(2,1)S(1)} %collective-permute-done.17.refs_1_, ...), custom_call_target="tpu_custom_call" | custom-call | tf_op jit(solution)/shard_map/pallas_call | solution.py:129
  91.9 0.0 collective-permute-done.21.refs_2_
  91.9 0.5 collective-permute-done.19.refs_1_
  92.4 3.7 %collective-permute-done.18.refs_0_ = bf16[112,1024]{1,0:T(8,128)(2,1)S(1)} collective-permute-done((bf16[112,1024]{1,0:T(8,128)(2,1)S(1)}, bf16[112,1024]{1,0:T(8,128)(2,1)S(1)}, u32[]{:S(2)}, u32[]{:S(2)}) %collective-permute-start.18) | collective-permute-done | bytes 229408 | tf_op jit(solution)/shard_map/ppermute | solution.py:28
  96.1 2.3 %shard_map.81 = bf16[8,112,1024]{2,1,0:T(8,128)(2,1)} custom-call(s32[11]{0:T(128)S(1)} %stack.62.place_ref, bf16[1024,1024]{1,0:T(8,128)(2,1)S(1)} %copy-done.1, bf16[112,1024]{1,0:T(8,128)(2,1)S(1)} %collective-permute-done.18.refs_0_, bf16[112,1024]{1,0:T(8,128)(2,1)S(1)} %collective-permute-done.19.refs_1_, ...), custom_call_target="tpu_custom_call", output_to_operand_aliasing={{}: (5, {})} | custom-call | tf_op jit(solution)/shard_map/pallas_call | solution.py:129
  (6 shorter events, 0.1 us)
Async XLA Ops:
  0.6 1.0 copy-start
  0.6 10.6 %copy-start.2 = (bf16[128,1,3584]{2,0,1:T(8,128)(2,1)S(1)}, bf16[128,1,3584]{2,0,1:T(8,128)(2,1)}, u32[]{:S(2)}) copy-start(bf16[128,1,3584]{2,0,1:T(8,128)(2,1)} %param.7) | copy-start | bytes 2752516
  4.3 15.7 %all-to-all-start = ((bf16[8,16,1024]{2,1,0:T(8,128)(2,1)}), bf16[8,16,1024]{2,1,0:T(8,128)(2,1)S(1)}, u32[]{:S(2)}, u32[]{:S(2)}) async-start(bf16[8,16,1024]{2,1,0:T(8,128)(2,1)} %bitcast.11), calls=%async_computation | async-start | bytes 524288 | tf_op jit(solution)/shard_map/all_to_all | solution.py:167
  11.7 21.2 %collective-permute-start.3 = (bf16[2,448,128]{2,1,0:T(8,128)(2,1)S(1)}, bf16[2,448,128]{2,1,0:T(8,128)(2,1)S(1)}, u32[]{:S(2)}, u32[]{:S(2)}) collective-permute-start(bf16[2,448,128]{2,1,0:T(8,128)(2,1)S(1)} %get-tuple-element.23), channel_id=1, source_target_pairs={{0,32},{32,64},{64,96},{96,0},{1,33},{33,65},{65,97},{97,1},{2,34}... | collective-permute-start | bytes 688136 | tf_op jit(solution)/shard_map/ppermute | solution.py:28
  16.3 16.7 %collective-permute-start.4 = (bf16[2,448,128]{2,1,0:T(8,128)(2,1)S(1)}, bf16[2,448,128]{2,1,0:T(8,128)(2,1)S(1)}, u32[]{:S(2)}, u32[]{:S(2)}) collective-permute-start(bf16[2,448,128]{2,1,0:T(8,128)(2,1)S(1)} %get-tuple-element.24), channel_id=1, source_target_pairs={{0,96},{32,0},{64,32},{96,64},{1,97},{33,1},{65,33},{97,65},{2,98}... | collective-permute-start | bytes 688136 | tf_op jit(solution)/shard_map/ppermute | solution.py:28
  20.1 12.8 %collective-permute-start.2 = (bf16[16,1024]{1,0:T(8,128)(2,1)S(1)}, bf16[16,1024]{1,0:T(8,128)(2,1)S(1)}, u32[]{:S(2)}, u32[]{:S(2)}) collective-permute-start(bf16[16,1024]{1,0:T(8,128)(2,1)S(1)} %reduce_sum.12), channel_id=1, source_target_pairs={{0,96},{32,0},{64,32},{96,64},{1,97},{33,1},{65,33},{97,65},{2,98}... | collective-permute-start | bytes 98312 | tf_op jit(solution)/shard_map/ppermute | solution.py:28
  20.2 12.7 %collective-permute-start.1 = (bf16[16,1024]{1,0:T(8,128)(2,1)S(1)}, bf16[16,1024]{1,0:T(8,128)(2,1)S(1)}, u32[]{:S(2)}, u32[]{:S(2)}) collective-permute-start(bf16[16,1024]{1,0:T(8,128)(2,1)S(1)} %reduce_sum.12), channel_id=1, source_target_pairs={{0,64},{32,96},{64,0},{96,32},{1,65},{33,97},{65,1},{97,33},{2,66}... | collective-permute-start | bytes 98312 | tf_op jit(solution)/shard_map/ppermute | solution.py:28
  27.0 5.9 %collective-permute-start = (bf16[16,1024]{1,0:T(8,128)(2,1)S(1)}, bf16[16,1024]{1,0:T(8,128)(2,1)S(1)}, u32[]{:S(2)}, u32[]{:S(2)}) collective-permute-start(bf16[16,1024]{1,0:T(8,128)(2,1)S(1)} %reduce_sum.12), channel_id=1, source_target_pairs={{0,32},{32,64},{64,96},{96,0},{1,33},{33,65},{65,97},{97,1},{2,34}... | collective-permute-start | bytes 98312 | tf_op jit(solution)/shard_map/ppermute | solution.py:28
  32.9 7.0 %collective-permute-start.5 = (bf16[4,16,1024]{2,1,0:T(8,128)(2,1)S(1)}, bf16[4,16,1024]{2,1,0:T(8,128)(2,1)S(1)}, u32[]{:S(2)}, u32[]{:S(2)}) collective-permute-start(bf16[4,16,1024]{2,1,0:T(8,128)(2,1)S(1)} %pad_maximum_fusion.refs_0_), channel_id=1, source_target_pairs={{0,4},{4,0},{1,5},{5,1},{2,6},{6,2},{3,7},{7,3},{8,12},{12,8},{9,1... | collective-permute-start | bytes 393224 | tf_op jit(solution)/shard_map/ppermute | solution.py:24
  35.8 9.4 %collective-permute-start.8 = (bf16[4,16,1024]{2,1,0:T(8,128)(2,1)S(1)}, bf16[4,16,1024]{2,1,0:T(8,128)(2,1)S(1)}, u32[]{:S(2)}, u32[]{:S(2)}) collective-permute-start(bf16[4,16,1024]{2,1,0:T(8,128)(2,1)S(1)} %pad_maximum_fusion.refs_0_), channel_id=1, source_target_pairs={{0,2},{1,3},{2,0},{3,1},{4,6},{5,7},{6,4},{7,5},{8,10},{9,11},{10,... | collective-permute-start | bytes 393224 | tf_op jit(solution)/shard_map/ppermute | solution.py:28
  38.8 8.8 %collective-permute-start.7 = (bf16[4,16,1024]{2,1,0:T(8,128)(2,1)S(1)}, bf16[4,16,1024]{2,1,0:T(8,128)(2,1)S(1)}, u32[]{:S(2)}, u32[]{:S(2)}) collective-permute-start(bf16[4,16,1024]{2,1,0:T(8,128)(2,1)S(1)} %pad_maximum_fusion.refs_0_), channel_id=1, source_target_pairs={{0,3},{1,0},{2,1},{3,2},{4,7},{5,4},{6,5},{7,6},{8,11},{9,8},{10,9... | collective-permute-start | bytes 393224 | tf_op jit(solution)/shard_map/ppermute | solution.py:28
  40.0 14.1 %collective-permute-start.12 = (bf16[2,448,128]{2,1,0:T(8,128)(2,1)S(1)}, bf16[2,448,128]{2,1,0:T(8,128)(2,1)S(1)}, u32[]{:S(2)}, u32[]{:S(2)}) collective-permute-start(bf16[2,448,128]{2,1,0:T(8,128)(2,1)S(1)} %get-tuple-element.30), channel_id=1, source_target_pairs={{0,64},{32,96},{64,0},{96,32},{1,65},{33,97},{65,1},{97,33},{2,66}... | collective-permute-start | bytes 688136 | tf_op jit(solution)/shard_map/ppermute | solution.py:28
  42.0 7.2 %collective-permute-start.6 = (bf16[4,16,1024]{2,1,0:T(8,128)(2,1)S(1)}, bf16[4,16,1024]{2,1,0:T(8,128)(2,1)S(1)}, u32[]{:S(2)}, u32[]{:S(2)}) collective-permute-start(bf16[4,16,1024]{2,1,0:T(8,128)(2,1)S(1)} %pad_maximum_fusion.refs_0_), channel_id=1, source_target_pairs={{0,1},{1,2},{2,3},{3,0},{4,5},{5,6},{6,7},{7,4},{8,9},{9,10},{10,1... | collective-permute-start | bytes 393224 | tf_op jit(solution)/shard_map/ppermute | solution.py:28
  42.9 8.9 %collective-permute-start.10 = (bf16[4,16,1024]{2,1,0:T(8,128)(2,1)S(1)}, bf16[4,16,1024]{2,1,0:T(8,128)(2,1)S(1)}, u32[]{:S(2)}, u32[]{:S(2)}) collective-permute-start(bf16[4,16,1024]{2,1,0:T(8,128)(2,1)S(1)} %collective-permute-done.5.refs_1_), channel_id=1, source_target_pairs={{0,3},{1,0},{2,1},{3,2},{4,7},{5,4},{6,5},{7,6},{8,11},{9,8},{10,9... | collective-permute-start | bytes 393224 | tf_op jit(solution)/shard_map/ppermute | solution.py:28
  45.3 6.5 %collective-permute-start.11 = (bf16[4,16,1024]{2,1,0:T(8,128)(2,1)S(1)}, bf16[4,16,1024]{2,1,0:T(8,128)(2,1)S(1)}, u32[]{:S(2)}, u32[]{:S(2)}) collective-permute-start(bf16[4,16,1024]{2,1,0:T(8,128)(2,1)S(1)} %collective-permute-done.8.refs_4_), channel_id=1, source_target_pairs={{0,4},{4,0},{1,5},{5,1},{2,6},{6,2},{3,7},{7,3},{8,12},{12,8},{9,1... | collective-permute-start | bytes 393224 | tf_op jit(solution)/shard_map/ppermute | solution.py:24
  47.6 6.2 %collective-permute-start.9 = (bf16[4,16,1024]{2,1,0:T(8,128)(2,1)S(1)}, bf16[4,16,1024]{2,1,0:T(8,128)(2,1)S(1)}, u32[]{:S(2)}, u32[]{:S(2)}) collective-permute-start(bf16[4,16,1024]{2,1,0:T(8,128)(2,1)S(1)} %collective-permute-done.5.refs_1_), channel_id=1, source_target_pairs={{0,1},{1,2},{2,3},{3,0},{4,5},{5,6},{6,7},{7,4},{8,9},{9,10},{10,1... | collective-permute-start | bytes 393224 | tf_op jit(solution)/shard_map/ppermute | solution.py:28
  54.0 18.7 %copy-start.4 = (f32[1,112,1024]{2,1,0:T(8,128)S(1)}, f32[1,112,1024]{2,1,0:T(8,128)}, u32[]{:S(2)}) copy-start(f32[1,112,1024]{2,1,0:T(8,128)} %second_ref.1) | copy-start | bytes 1376260
  55.3 17.4 %copy-start.3 = (f32[1,112,1024]{2,1,0:T(8,128)S(1)}, f32[1,112,1024]{2,1,0:T(8,128)}, u32[]{:S(2)}) copy-start(f32[1,112,1024]{2,1,0:T(8,128)} %first_ref.1) | copy-start | bytes 1376260
  55.3 33.6 %copy-start.1 = (bf16[1024,1024]{1,0:T(8,128)(2,1)S(1)}, bf16[1024,1024]{1,0:T(8,128)(2,1)}, u32[]{:S(2)}) copy-start(bf16[1024,1024]{1,0:T(8,128)(2,1)} %projector_ref.3) | copy-start | bytes 6291460
  55.3 2.6 %collective-permute-start.13 = (bf16[4,112,1024]{2,1,0:T(8,128)(2,1)S(1)}, bf16[4,112,1024]{2,1,0:T(8,128)(2,1)S(1)}, u32[]{:S(2)}, u32[]{:S(2)}) collective-permute-start(bf16[4,112,1024]{2,1,0:T(8,128)(2,1)S(1)} %shard_map.77), channel_id=1, source_target_pairs={{0,8},{8,0},{1,9},{9,1},{2,10},{10,2},{3,11},{11,3},{4,12},{12,4},... | collective-permute-start | bytes 2752520 | tf_op jit(solution)/shard_map/ppermute | solution.py:24
  59.2 9.5 %collective-permute-start.14 = (bf16[112,1024]{1,0:T(8,128)(2,1)S(1)}, bf16[112,1024]{1,0:T(8,128)(2,1)S(1)}, u32[]{:S(2)}, u32[]{:S(2)}) collective-permute-start(bf16[112,1024]{1,0:T(8,128)(2,1)S(1)} %get-tuple-element.33), channel_id=1, source_target_pairs={{0,144},{16,128},{128,16},{144,0},{1,145},{17,129},{129,17},{145,1... | collective-permute-start | bytes 688136 | tf_op jit(solution)/shard_map/ppermute | solution.py:195
  60.1 11.9 %collective-permute-start.15 = (bf16[112,1024]{1,0:T(8,128)(2,1)S(1)}, bf16[112,1024]{1,0:T(8,128)(2,1)S(1)}, u32[]{:S(2)}, u32[]{:S(2)}) collective-permute-start(bf16[112,1024]{1,0:T(8,128)(2,1)S(1)} %get-tuple-element.34), channel_id=1, source_target_pairs={{0,16},{16,0},{1,17},{17,1},{2,18},{18,2},{3,19},{19,3},{4,20},{20... | collective-permute-start | bytes 688136 | tf_op jit(solution)/shard_map/ppermute | solution.py:24
  61.4 11.3 %collective-permute-start.16 = (bf16[112,1024]{1,0:T(8,128)(2,1)S(1)}, bf16[112,1024]{1,0:T(8,128)(2,1)S(1)}, u32[]{:S(2)}, u32[]{:S(2)}) collective-permute-start(bf16[112,1024]{1,0:T(8,128)(2,1)S(1)} %get-tuple-element.35), channel_id=1, source_target_pairs={{0,128},{128,0},{1,129},{129,1},{2,130},{130,2},{3,131},{131,3},{4... | collective-permute-start | bytes 688136 | tf_op jit(solution)/shard_map/ppermute | solution.py:24
  73.9 10.0 %collective-permute-start.20 = (bf16[112,1024]{1,0:T(8,128)(2,1)S(1)}, bf16[112,1024]{1,0:T(8,128)(2,1)S(1)}, u32[]{:S(2)}, u32[]{:S(2)}) collective-permute-start(bf16[112,1024]{1,0:T(8,128)(2,1)S(1)} %get-tuple-element.36.refs_0_), channel_id=1, source_target_pairs={{0,2},{1,3},{2,0},{3,1},{4,6},{5,7},{6,4},{7,5},{8,10},{9,11},{10,... | collective-permute-start | bytes 688136 | tf_op jit(solution)/shard_map/ppermute | solution.py:28
  75.5 10.7 %collective-permute-start.17 = (bf16[112,1024]{1,0:T(8,128)(2,1)S(1)}, bf16[112,1024]{1,0:T(8,128)(2,1)S(1)}, u32[]{:S(2)}, u32[]{:S(2)}) collective-permute-start(bf16[112,1024]{1,0:T(8,128)(2,1)S(1)} %get-tuple-element.36.refs_0_), channel_id=1, source_target_pairs={{0,4},{4,0},{1,5},{5,1},{2,6},{6,2},{3,7},{7,3},{8,12},{12,8},{9,1... | collective-permute-start | bytes 688136 | tf_op jit(solution)/shard_map/ppermute | solution.py:24
  79.2 9.7 %collective-permute-start.23 = (bf16[112,1024]{1,0:T(8,128)(2,1)S(1)}, bf16[112,1024]{1,0:T(8,128)(2,1)S(1)}, u32[]{:S(2)}, u32[]{:S(2)}) collective-permute-start(bf16[112,1024]{1,0:T(8,128)(2,1)S(1)} %get-tuple-element.36.refs_0_), channel_id=1, source_target_pairs={{0,3},{1,0},{2,1},{3,2},{4,7},{5,4},{6,5},{7,6},{8,11},{9,8},{10,9... | collective-permute-start | bytes 688136 | tf_op jit(solution)/shard_map/ppermute | solution.py:28
  80.3 8.6 %collective-permute-start.22 = (bf16[112,1024]{1,0:T(8,128)(2,1)S(1)}, bf16[112,1024]{1,0:T(8,128)(2,1)S(1)}, u32[]{:S(2)}, u32[]{:S(2)}) collective-permute-start(bf16[112,1024]{1,0:T(8,128)(2,1)S(1)} %get-tuple-element.36.refs_0_), channel_id=1, source_target_pairs={{0,1},{1,2},{2,3},{3,0},{4,5},{5,6},{6,7},{7,4},{8,9},{9,10},{10,1... | collective-permute-start | bytes 688136 | tf_op jit(solution)/shard_map/ppermute | solution.py:28
  83.9 8.0 %collective-permute-start.21 = (bf16[112,1024]{1,0:T(8,128)(2,1)S(1)}, bf16[112,1024]{1,0:T(8,128)(2,1)S(1)}, u32[]{:S(2)}, u32[]{:S(2)}) collective-permute-start(bf16[112,1024]{1,0:T(8,128)(2,1)S(1)} %collective-permute-done.20.refs_4_), channel_id=1, source_target_pairs={{0,4},{4,0},{1,5},{5,1},{2,6},{6,2},{3,7},{7,3},{8,12},{12,8},{9,1... | collective-permute-start | bytes 688136 | tf_op jit(solution)/shard_map/ppermute | solution.py:24
  86.2 6.2 %collective-permute-start.19 = (bf16[112,1024]{1,0:T(8,128)(2,1)S(1)}, bf16[112,1024]{1,0:T(8,128)(2,1)S(1)}, u32[]{:S(2)}, u32[]{:S(2)}) collective-permute-start(bf16[112,1024]{1,0:T(8,128)(2,1)S(1)} %collective-permute-done.17.refs_1_), channel_id=1, source_target_pairs={{0,3},{1,0},{2,1},{3,2},{4,7},{5,4},{6,5},{7,6},{8,11},{9,8},{10,9... | collective-permute-start | bytes 688136 | tf_op jit(solution)/shard_map/ppermute | solution.py:28
  88.9 7.2 %collective-permute-start.18 = (bf16[112,1024]{1,0:T(8,128)(2,1)S(1)}, bf16[112,1024]{1,0:T(8,128)(2,1)S(1)}, u32[]{:S(2)}, u32[]{:S(2)}) collective-permute-start(bf16[112,1024]{1,0:T(8,128)(2,1)S(1)} %collective-permute-done.17.refs_1_), channel_id=1, source_target_pairs={{0,1},{1,2},{2,3},{3,0},{4,5},{5,6},{6,7},{7,4},{8,9},{9,10},{10,1... | collective-permute-start | bytes 688136 | tf_op jit(solution)/shard_map/ppermute | solution.py:28

commit v5 on v4

v5 whole, which is shorter than its diff:
```python
import functools

import jax
import jax.numpy as jnp
from jax import lax
from jax.experimental import pallas as pl
from jax.experimental.pallas import tpu as pltpu
from jax.sharding import Mesh, PartitionSpec as P

bias_first = 1.0 - 0.9**20
bias_second = 1.0 - 0.999**20
epsilon = 1e-08

YLO, ZH, ZL, CORE = 2, 4, 2, 2
PARTS = YLO * ZL
DP = ("ylo", "zh", "zl", "core")
YHI, X = 2, 4
FSDP = ("yhi", "x")
wide, narrow = jnp.float32, jnp.bfloat16
VMEM = pl.BlockSpec(memory_space=pltpu.VMEM)
SMEM = pl.BlockSpec(memory_space=pltpu.SMEM)


def swap(value, axis):
    return lax.ppermute(value, axis, [(0, 1), (1, 0)])


def shift(value, axis, size, step):
    return lax.ppermute(value, axis, [(i, (i + step) % size) for i in range(size)])


def exchanged(over_y, over_z, over_both):
    both = lax.ppermute(over_both, ("ylo", "zl"), [(i, 3 - i) for i in range(4)])
    return [swap(over_y, "ylo"), swap(over_z, "zl"), both]


def local(body, outs, count, **kwargs):
    return pl.pallas_call(
        body,
        out_shape=[jax.ShapeDtypeStruct(shape, dtype) for shape, dtype in outs],
        in_specs=[SMEM] + [VMEM] * count,
        out_specs=[VMEM] * len(outs),
        compiler_params=pltpu.CompilerParams(vmem_limit_bytes=16 * 2**20),
        **kwargs,
    )


def turn_kernel(place_ref, grads_ref, *refs):
    outs, turned = refs[:PARTS], refs[PARTS]
    turned[...] = grads_ref[...].T
    block = outs[0].shape[1]
    for part in range(PARTS):
        y = lax.rem(place_ref[0] + part % 2, YLO)
        z = lax.rem(place_ref[1] + part // 2, ZL)
        for h in range(ZH):
            start = pl.multiple_of(((y * ZH + h) * ZL + z) * block, 16)
            outs[part][h] = turned[pl.ds(start, block), :]


def product(place_ref, core, pieces, grads, whole):
    cols, tokens = grads[0].shape[2:]
    for j, piece in enumerate(pieces):
        whole[:, pl.ds(place_ref[4 + YHI * X + j], 1)] = piece[...][:, None]
    rows = []
    for step in range(ZH):
        h = lax.rem(place_ref[2] + step, ZH)
        rows.append(jnp.concatenate([part[h, core] for part in grads], axis=1))
    total = jnp.dot(
        jnp.concatenate(rows, axis=0),
        whole[...].reshape(PARTS * tokens, whole.shape[-1]),
        preferred_element_type=wide,
    )
    return total.reshape(ZH, cols, -1)


def send_kernel(place_ref, *refs):
    pieces, grads, (out_ref, whole) = refs[:X], refs[X : X + PARTS], refs[X + PARTS :]
    out_ref[...] = product(place_ref, 1 - place_ref[3], pieces, grads, whole).astype(narrow)


def keep_kernel(place_ref, *refs):
    pieces, grads, rest = refs[:X], refs[X : X + PARTS], refs[X + PARTS :]
    came_ref, own_ref, up_far_ref, down_far_ref, up_ref, down_ref, up_held_ref, down_held_ref, whole = rest
    total = product(place_ref, place_ref[3], pieces, grads, whole) + came_ref[...].astype(wide)
    lanes = total.shape[-1] // 2
    own_ref[...] = total[0]
    up_far_ref[...] = total[2, :, :lanes].astype(narrow)
    down_far_ref[...] = total[2, :, lanes:].astype(narrow)
    up_ref[...] = total[1, :, lanes:].astype(narrow)
    down_ref[...] = total[3, :, :lanes].astype(narrow)
    up_held_ref[...] = total[1, :, :lanes]
    down_held_ref[...] = total[3, :, lanes:]


def relay_kernel(up_held_ref, down_held_ref, up_ref, down_ref, up_out_ref, down_out_ref):
    up_out_ref[...] = (up_held_ref[...] + up_ref[...].astype(wide)).astype(narrow)
    down_out_ref[...] = (down_held_ref[...] + down_ref[...].astype(wide)).astype(narrow)


def gradient_call(body, outs, tokens, rank, extra):
    return pl.pallas_call(
        body,
        out_shape=[jax.ShapeDtypeStruct(shape, dtype) for shape, dtype in outs],
        in_specs=[SMEM] + [VMEM] * (X + PARTS + extra),
        out_specs=[VMEM] * len(outs),
        scratch_shapes=[pltpu.VMEM((PARTS, X, tokens // X, rank), narrow)],
        compiler_params=pltpu.CompilerParams(vmem_limit_bytes=16 * 2**20),
    )


def adam_kernel(own_ref, up_ref, down_ref, up_sum_ref, down_sum_ref, first_ref, second_ref, *outs):
    left = down_ref[...].astype(wide) + up_sum_ref[...].astype(wide)
    right = up_ref[...].astype(wide) + down_sum_ref[...].astype(wide)
    gradient = own_ref[...] + jnp.concatenate([left, right], axis=1)
    first_new = 0.9 * first_ref[0] + 0.1 * gradient
    second_new = 0.999 * second_ref[0] + 0.001 * gradient * gradient
    root = jnp.sqrt(second_new / bias_second) + epsilon
    outs[0][...] = (first_new / bias_first / root).astype(narrow)
    outs[1][0] = first_new
    outs[2][0] = second_new


def back_kernel(count, first, place_ref, projector_ref, *refs):
    blocks = refs[:count]
    out_ref, held, sems = refs[-3:]
    stacked = jnp.concatenate([block[...] for block in blocks], axis=0)
    held[...] = lax.dot_general(
        stacked, projector_ref[...], (((1,), (1,)), ((), ())), preferred_element_type=wide
    ).astype(narrow).reshape(held.shape)
    copies = [
        pltpu.make_async_copy(held.at[j], out_ref.at[place_ref[4 + first + j]], sems.at[j])
        for j in range(count)
    ]
    for copy in copies:
        copy.start()
    for copy in copies:
        copy.wait()


def back(place, projector, blocks, first, out):
    count = len(blocks)
    cols = blocks[0].shape[0]
    width = projector.shape[0]
    before = [] if out is None else [out]
    return pl.pallas_call(
        functools.partial(back_kernel, count, first),
        out_shape=jax.ShapeDtypeStruct((YHI * X, cols, width), narrow),
        in_specs=[SMEM] + [VMEM] * (1 + count) + [pl.BlockSpec(memory_space=pl.ANY)] * len(before),
        out_specs=pl.BlockSpec(memory_space=pl.ANY),
        input_output_aliases={} if out is None else {2 + count: 0},
        scratch_shapes=[
            pltpu.VMEM((count, cols, width), narrow),
            pltpu.SemaphoreType.DMA((count,)),
        ],
        compiler_params=pltpu.CompilerParams(vmem_limit_bytes=16 * 2**20),
    )(place, projector, *blocks, *before)


def gathered(value, other=None):
    other = swap(value, "yhi") if other is None else other
    mine = [shift(value, "x", X, step) for step in (1, 3, 2)]
    rest = [shift(other, "x", X, step) for step in (1, 3)] + [swap(mine[2], "yhi")]
    return [value, other] + mine + rest


def gathered_from(yhi, x):
    mine, other = yhi * X, (1 - yhi) * X
    steps = [(x + X - step) % X for step in (1, 3, 2)]
    return [mine + x, other + x] + [mine + s for s in steps] + [other + s for s in steps]


def shards(activations, projector, out_grad, first_moment, second_moment):
    n_fsdp = YHI * X
    zh, zl, core, ylo, yhi, x = (
        lax.axis_index(a) for a in ("zh", "zl", "core", "ylo", "yhi", "x")
    )
    tokens, rank = activations.shape[0], projector.shape[1]
    cols = first_moment.shape[1]
    block = CORE * cols
    sources = [(x + X - step) % X for step in (0, 1, 3, 2)]
    place = jnp.stack([ylo, zl, zh, core] + gathered_from(yhi, x) + sources)

    partial_value = jnp.dot(activations, projector, preferred_element_type=wide).astype(narrow)
    partial_value, out_grad = lax.optimization_barrier((partial_value, out_grad))
    share = partial_value.reshape(1, X, tokens // X, rank)
    pieces = lax.all_to_all(
        jnp.broadcast_to(share, (YHI,) + share.shape[1:]).reshape((n_fsdp,) + share.shape[2:]),
        FSDP,
        0,
        0,
    )

    grads = local(
        turn_kernel,
        [((ZH, block, tokens), narrow)] * PARTS,
        1,
        scratch_shapes=[pltpu.VMEM((YLO * ZH * ZL * block, tokens), narrow)],
    )(place, out_grad.reshape(tokens, YLO * ZH * ZL * block))
    moved = exchanged(*grads[1:])
    piece = pieces.astype(wide).sum(0).astype(narrow)
    piece = jnp.stack([piece] + exchanged(piece, piece, piece))
    piece, moved[:2] = lax.optimization_barrier((piece, moved[:2]))
    projected = [piece] + [shift(piece, "x", X, step) for step in (1, 3, 2)]
    grads = [g.reshape(ZH, CORE, cols, tokens) for g in [grads[0]] + moved]
    one = (cols, rank)
    (sent,) = gradient_call(send_kernel, [((ZH,) + one, narrow)], tokens, rank, 0)(
        place, *projected, *grads
    )
    came = swap(sent, "core")
    part = (cols, rank // 2)
    own, up_far, down_far, up, down, up_held, down_held = gradient_call(
        keep_kernel,
        [(one, wide)] + [(part, narrow)] * 4 + [(part, wide)] * 2,
        tokens,
        rank,
        1,
    )(place, *projected, *grads, came)
    up_far, down_far = shift(up_far, "zh", ZH, 1), shift(down_far, "zh", ZH, 3)
    up, down = shift(up, "zh", ZH, 1), shift(down, "zh", ZH, 3)
    up_sum, down_sum = pl.pallas_call(
        relay_kernel,
        out_shape=[jax.ShapeDtypeStruct(part, narrow)] * 2,
        in_specs=[VMEM] * 4,
        out_specs=[VMEM] * 2,
        compiler_params=pltpu.CompilerParams(vmem_limit_bytes=16 * 2**20),
    )(up_held, down_held, up_far, down_far)
    up_sum, down_sum = shift(up_sum, "zh", ZH, 1), shift(down_sum, "zh", ZH, 3)
    moment = jax.ShapeDtypeStruct((1,) + one, wide)
    direction, first_new, second_new = pl.pallas_call(
        adam_kernel,
        out_shape=[jax.ShapeDtypeStruct(one, narrow), moment, moment],
        in_specs=[VMEM] * 7,
        out_specs=[VMEM] * 3,
        compiler_params=pltpu.CompilerParams(vmem_limit_bytes=16 * 2**20),
    )(own, up, down, up_sum, down_sum, first_moment, second_moment)
    directions = gathered(direction)
    weight_update = back(place, projector, directions[:5], 0, None)
    weight_update = back(place, projector, directions[5:], 5, weight_update)
    return (weight_update, first_new, second_new)


def solution(mesh):
    fine = Mesh(
        mesh.devices.reshape(YLO, ZH, ZL, CORE, YHI, X), DP + FSDP
    )
    in_specs = (
        P(DP, FSDP),
        P(FSDP, None),
        P(DP, FSDP, None),
        P(FSDP, DP, None),
        P(FSDP, DP, None),
    )
    out_specs = (P(None, DP, FSDP), P(FSDP, DP, None), P(FSDP, DP, None))
    return jax.shard_map(shards, mesh=fine, in_specs=in_specs, out_specs=out_specs, check_vma=False)
```

time: 98.8 us -> 97.4 us (0.986)
  starting transfers between devices: 52 us -> 42.5 us
  waiting for transfers between devices: 32.4 us -> 39.8 us
    ppermute x16 -> x14, starting transfers between devices: 30.1 us -> 19.1 us  [shift(): lax.ppermute(value, axis, [(i, (i + step) % size) for i in range(size)])]
    ppermute x16 -> x14, waiting for transfers between devices: 13.6 us -> 22.2 us  [shift(): lax.ppermute(value, axis, [(i, (i + step) % size) for i in range(size)])]
    ppermute x7, waiting for transfers between devices: 9.09 us -> 3.29 us  [swap(): return lax.ppermute(value, axis, [(0, 1), (1, 0)])]
    all_to_all x1, waiting for transfers between devices: 3.79 us -> 7.96 us  [shards(): lax.all_to_all(jnp.broadcast_to(share, (YHI,) + share.shape[1:]).reshape(...]
    ppermute x1 -> x2, starting transfers between devices: 0.93 us -> 4.82 us  [exchanged(): lax.ppermute(over_both, ('ylo', 'zl'), [(i, 3 - i) for i in range(4)])]
    ppermute x7, starting transfers between devices: 14 us -> 11.6 us  [swap(): return lax.ppermute(value, axis, [(0, 1), (1, 0)])]
    pallas_call x3 -> x4, Pallas kernels: 2.95 us -> 3.47 us  [the longest x1 1.27 us: shards(): gradient_call(keep_kernel, [(one, wide)] + [(part, narrow)] * 4 + [(part,...]
    ppermute x1 -> x2, waiting for transfers between devices: 5.9 us -> 6.31 us  [exchanged(): lax.ppermute(over_both, ('ylo', 'zl'), [(i, 3 - i) for i in range(4)])]
  transfers between devices with their start and end apart: 25 -> 24, of which waited for: 13 -> 16; matrix products, arithmetic and copies ran while one was open for 0% -> 0% of each run, Pallas kernels for 3% -> 4%
where the time goes in v5:
time: 97.4 us; the launch traced here: 97.2 us
  starting transfers between devices  42.5 us (44%)
  waiting for transfers between devices  39.8 us (41%)
  Pallas kernels  9.9 us (10%)
  matrix products  2.04 us (2%)
  local copies, waits for them, and re-layouts  1.91 us (2%)
    ppermute x14, waiting for transfers between devices, shift(): lax.ppermute(value, axis, [(i, (i + step) % size) for i in range(size)])  22.2 us
    ppermute x14, starting transfers between devices, shift(): lax.ppermute(value, axis, [(i, (i + step) % size) for i in range(size)])  19.1 us
    ppermute x7, starting transfers between devices, swap(): return lax.ppermute(value, axis, [(0, 1), (1, 0)])  11.6 us
    all_to_all x1, waiting for transfers between devices, shards(): lax.all_to_all(jnp.broadcast_to(share, (YHI,) + share.shape[1:]).reshape(...  7.96 us
    all_to_all x1, starting transfers between devices, shards(): lax.all_to_all(jnp.broadcast_to(share, (YHI,) + share.shape[1:]).reshape(...  6.93 us
    ppermute x2, waiting for transfers between devices, exchanged(): lax.ppermute(over_both, ('ylo', 'zl'), [(i, 3 - i) for i in range(4)])  6.31 us
    pallas_call x2, Pallas kernels, back(): pl.pallas_call(functools.partial(back_kernel, count, first), out_shape=ja...  5.28 us
    ppermute x2, starting transfers between devices, exchanged(): lax.ppermute(over_both, ('ylo', 'zl'), [(i, 3 - i) for i in range(4)])  4.82 us
  transfers between devices with their start and end apart: 24, of which 16 were waited for; matrix products, arithmetic and copies ran while one was open for 0% of the time, Pallas kernels for 4%

profile of v5, /device:TPU:64, one launch (start us, length us, event | category | flops | bytes accessed | tf_op | source)
XLA Modules:
  0.0 97.2 jit_solution(12778385860382139679)
XLA Ops:
  0.6 0.0 copy-start
  0.7 0.9 copy-done
  1.6 2.0 %convolution_convert_fusion = bf16[128,1024]{1,0:T(8,128)(2,1)S(1)} fusion(bf16[128,1024]{1,0:T(8,128)(2,1)S(1)} %copy-done, bf16[1024,1024]{1,0:T(8,128)(2,1)} %projector_ref.3), kind=kOutput, calls=%fused_computation | convolution fusion | flops 268566528 | bytes 2621440 | tf_op jit(solution)/shard_map/dot_general | solution.py:183
  3.6 0.9 broadcast_in_dim.8
  4.5 6.9 %all-to-all-start = ((bf16[8,32,1024]{2,1,0:T(8,128)(2,1)}), bf16[8,32,1024]{2,1,0:T(8,128)(2,1)S(1)}, u32[]{:S(2)}, u32[]{:S(2)}) async-start(bf16[8,32,1024]{2,1,0:T(8,128)(2,1)} %bitcast.17), calls=%async_computation | async-start | bytes 1048576 | tf_op jit(solution)/shard_map/all_to_all | solution.py:186
  11.4 0.1 stack.82.place_ref
  11.5 0.9 shard_map.76
  12.4 0.8 collective-permute-start.3
  13.2 1.9 %collective-permute-start.4 = (bf16[4,224,128]{2,1,0:T(8,128)(2,1)S(1)}, bf16[4,224,128]{2,1,0:T(8,128)(2,1)S(1)}, u32[]{:S(2)}, u32[]{:S(2)}) collective-permute-start(bf16[4,224,128]{2,1,0:T(8,128)(2,1)S(1)} %get-tuple-element.27), channel_id=1, source_target_pairs={{0,16},{16,0},{1,17},{17,1},{2,18},{18,2},{3,19},{19,3},{4,20},{20... | collective-permute-start | bytes 688136 | tf_op jit(solution)/shard_map/ppermute | solution.py:25
  15.1 8.0 %all-to-all-done = bf16[8,32,1024]{2,1,0:T(8,128)(2,1)S(1)} async-done(((bf16[8,32,1024]{2,1,0:T(8,128)(2,1)}), bf16[8,32,1024]{2,1,0:T(8,128)(2,1)S(1)}, u32[]{:S(2)}, u32[]{:S(2)}) %all-to-all-start) | async-done | bytes 524320 | tf_op jit(solution)/shard_map/all_to_all | solution.py:186
  23.1 0.1 reduce_sum.12
  23.1 2.1 %collective-permute-start.2 = (bf16[32,1024]{1,0:T(8,128)(2,1)S(1)}, bf16[32,1024]{1,0:T(8,128)(2,1)S(1)}, u32[]{:S(2)}, u32[]{:S(2)}) collective-permute-start(bf16[32,1024]{1,0:T(8,128)(2,1)S(1)} %reduce_sum.12), channel_id=1, source_target_pairs={{0,144},{16,128},{128,16},{144,0},{1,145},{17,129},{129,17},{145,1... | collective-permute-start | bytes 196616 | tf_op jit(solution)/shard_map/ppermute | solution.py:33
  25.3 0.1 collective-permute-start.1
  25.4 1.3 %collective-permute-start = (bf16[32,1024]{1,0:T(8,128)(2,1)S(1)}, bf16[32,1024]{1,0:T(8,128)(2,1)S(1)}, u32[]{:S(2)}, u32[]{:S(2)}) collective-permute-start(bf16[32,1024]{1,0:T(8,128)(2,1)S(1)} %reduce_sum.12), channel_id=1, source_target_pairs={{0,128},{128,0},{1,129},{129,1},{2,130},{130,2},{3,131},{131,3},{4... | collective-permute-start | bytes 196616 | tf_op jit(solution)/shard_map/ppermute | solution.py:25
  26.7 2.1 %collective-permute-done.2 = bf16[32,1024]{1,0:T(8,128)(2,1)S(1)} collective-permute-done((bf16[32,1024]{1,0:T(8,128)(2,1)S(1)}, bf16[32,1024]{1,0:T(8,128)(2,1)S(1)}, u32[]{:S(2)}, u32[]{:S(2)}) %collective-permute-start.2) | collective-permute-done | bytes 65568 | tf_op jit(solution)/shard_map/ppermute | solution.py:33
  28.8 0.7 collective-permute-done.1
  29.5 0.1 collective-permute-done
  29.7 0.0 collective-permute-done.3
  29.7 0.0 collective-permute-done.4
  29.7 1.4 %collective-permute-start.7 = (bf16[4,32,1024]{2,1,0:T(8,128)(2,1)S(1)}, bf16[4,32,1024]{2,1,0:T(8,128)(2,1)S(1)}, u32[]{:S(2)}, u32[]{:S(2)}) collective-permute-start(bf16[4,32,1024]{2,1,0:T(8,128)(2,1)S(1)} %pad_maximum_fusion.refs_0_), channel_id=1, source_target_pairs={{0,2},{1,3},{2,0},{3,1},{4,6},{5,7},{6,4},{7,5},{8,10},{9,11},{10,... | collective-permute-start | bytes 786440 | tf_op jit(solution)/shard_map/ppermute | solution.py:29
  31.1 2.2 %collective-permute-start.6 = (bf16[4,32,1024]{2,1,0:T(8,128)(2,1)S(1)}, bf16[4,32,1024]{2,1,0:T(8,128)(2,1)S(1)}, u32[]{:S(2)}, u32[]{:S(2)}) collective-permute-start(bf16[4,32,1024]{2,1,0:T(8,128)(2,1)S(1)} %pad_maximum_fusion.refs_0_), channel_id=1, source_target_pairs={{0,3},{1,0},{2,1},{3,2},{4,7},{5,4},{6,5},{7,6},{8,11},{9,8},{10,9... | collective-permute-start | bytes 786440 | tf_op jit(solution)/shard_map/ppermute | solution.py:29
  33.4 0.0 collective-permute-start.5
  33.4 2.7 %collective-permute-start.8 = (bf16[4,224,128]{2,1,0:T(8,128)(2,1)S(1)}, bf16[4,224,128]{2,1,0:T(8,128)(2,1)S(1)}, u32[]{:S(2)}, u32[]{:S(2)}) collective-permute-start(bf16[4,224,128]{2,1,0:T(8,128)(2,1)S(1)} %get-tuple-element.32), channel_id=1, source_target_pairs={{0,144},{16,128},{128,16},{144,0},{1,145},{17,129},{129,17},{145,1... | collective-permute-start | bytes 688136 | tf_op jit(solution)/shard_map/ppermute | solution.py:33
  36.1 4.2 %collective-permute-done.8 = bf16[4,224,128]{2,1,0:T(8,128)(2,1)S(1)} collective-permute-done((bf16[4,224,128]{2,1,0:T(8,128)(2,1)S(1)}, bf16[4,224,128]{2,1,0:T(8,128)(2,1)S(1)}, u32[]{:S(2)}, u32[]{:S(2)}) %collective-permute-start.8) | collective-permute-done | bytes 229408 | tf_op jit(solution)/shard_map/ppermute | solution.py:33
  40.3 0.3 collective-permute-done.7.refs_3_
  40.6 0.0 collective-permute-done.6.refs_2_
  40.6 3.4 %collective-permute-done.5.refs_1_ = bf16[4,32,1024]{2,1,0:T(8,128)(2,1)S(1)} collective-permute-done((bf16[4,32,1024]{2,1,0:T(8,128)(2,1)S(1)}, bf16[4,32,1024]{2,1,0:T(8,128)(2,1)S(1)}, u32[]{:S(2)}, u32[]{:S(2)}) %collective-permute-start.5) | collective-permute-done | bytes 262176 | tf_op jit(solution)/shard_map/ppermute | solution.py:29
  43.9 1.3 %shard_map.77 = bf16[4,112,1024]{2,1,0:T(8,128)(2,1)S(1)} custom-call(s32[16]{0:T(128)S(1)} %stack.82.place_ref, bf16[4,32,1024]{2,1,0:T(8,128)(2,1)S(1)} %pad_maximum_fusion.refs_0_, bf16[4,32,1024]{2,1,0:T(8,128)(2,1)S(1)} %collective-permute-done.5.refs_1_, bf16[4,32,1024]{2,1,0:T(8,128)(2,1)S(1)} %collective-permute-done.6.refs_2_, ...), custom_call_target="tpu_custom_call" | custom-call | tf_op jit(solution)/shard_map/pallas_call | solution.py:206
  45.2 0.0 copy-start.3
  45.2 0.0 copy-start.4
  45.2 0.0 copy-start.1
  45.3 0.1 collective-permute-start.9
  45.4 2.5 %collective-permute-done.9.refs_8_ = bf16[4,112,1024]{2,1,0:T(8,128)(2,1)S(1)} collective-permute-done((bf16[4,112,1024]{2,1,0:T(8,128)(2,1)S(1)}, bf16[4,112,1024]{2,1,0:T(8,128)(2,1)S(1)}, u32[]{:S(2)}, u32[]{:S(2)}) %collective-permute-start.9) | collective-permute-done | bytes 917536 | tf_op jit(solution)/shard_map/ppermute | solution.py:25
  47.8 1.3 %shard_map.78 = (f32[112,1024]{1,0:T(8,128)S(1)}, bf16[112,512]{1,0:T(8,128)(2,1)S(1)}, bf16[112,512]{1,0:T(8,128)(2,1)S(1)}, bf16[112,512]{1,0:T(8,128)(2,1)S(1...) custom-call(s32[16]{0:T(128)S(1)} %stack.82.place_ref, ...), custom_call_target="tpu_custom_call" | custom-call | tf_op jit(solution)/shard_map/pallas_call | solution.py:211
  49.1 3.9 %collective-permute-start.12 = (bf16[112,512]{1,0:T(8,128)(2,1)S(1)}, bf16[112,512]{1,0:T(8,128)(2,1)S(1)}, u32[]{:S(2)}, u32[]{:S(2)}) collective-permute-start(bf16[112,512]{1,0:T(8,128)(2,1)S(1)} %get-tuple-element.38), channel_id=1, source_target_pairs={{0,32},{32,64},{64,96},{96,0},{1,33},{33,65},{65,97},{97,1},{2,34}... | collective-permute-start | bytes 344072 | tf_op jit(solution)/shard_map/ppermute | solution.py:29
  53.0 0.0 collective-permute-start.13
  53.0 4.1 %collective-permute-start.10 = (bf16[112,512]{1,0:T(8,128)(2,1)S(1)}, bf16[112,512]{1,0:T(8,128)(2,1)S(1)}, u32[]{:S(2)}, u32[]{:S(2)}) collective-permute-start(bf16[112,512]{1,0:T(8,128)(2,1)S(1)} %get-tuple-element.34), channel_id=1, source_target_pairs={{0,32},{32,64},{64,96},{96,0},{1,33},{33,65},{65,97},{97,1},{2,34}... | collective-permute-start | bytes 344072 | tf_op jit(solution)/shard_map/ppermute | solution.py:29
  57.2 0.0 collective-permute-start.11
  57.2 1.7 %collective-permute-done.12.up_ref = bf16[112,512]{1,0:T(8,128)(2,1)S(1)} collective-permute-done((bf16[112,512]{1,0:T(8,128)(2,1)S(1)}, bf16[112,512]{1,0:T(8,128)(2,1)S(1)}, u32[]{:S(2)}, u32[]{:S(2)}) %collective-permute-start.12) | collective-permute-done | bytes 114720 | tf_op jit(solution)/shard_map/ppermute | solution.py:29
  58.9 4.5 %collective-permute-done.13.down_ref = bf16[112,512]{1,0:T(8,128)(2,1)S(1)} collective-permute-done((bf16[112,512]{1,0:T(8,128)(2,1)S(1)}, bf16[112,512]{1,0:T(8,128)(2,1)S(1)}, u32[]{:S(2)}, u32[]{:S(2)}) %collective-permute-start.13) | collective-permute-done | bytes 114720 | tf_op jit(solution)/shard_map/ppermute | solution.py:29
  63.4 0.8 collective-permute-start.14
  64.2 2.2 %collective-permute-start.15 = (bf16[112,512]{1,0:T(8,128)(2,1)S(1)}, bf16[112,512]{1,0:T(8,128)(2,1)S(1)}, u32[]{:S(2)}, u32[]{:S(2)}) collective-permute-start(bf16[112,512]{1,0:T(8,128)(2,1)S(1)} %get-tuple-element.41), channel_id=1, source_target_pairs={{0,96},{32,0},{64,32},{96,64},{1,97},{33,1},{65,33},{97,65},{2,98}... | collective-permute-start | bytes 344072 | tf_op jit(solution)/shard_map/ppermute | solution.py:29
  66.4 0.0 collective-permute-done.10.up_ref
  66.4 0.9 collective-permute-done.11.down_ref
  67.3 2.5 %collective-permute-done.14.up_sum_ref = bf16[112,512]{1,0:T(8,128)(2,1)S(1)} collective-permute-done((bf16[112,512]{1,0:T(8,128)(2,1)S(1)}, bf16[112,512]{1,0:T(8,128)(2,1)S(1)}, u32[]{:S(2)}, u32[]{:S(2)}) %collective-permute-start.14) | collective-permute-done | bytes 114720 | tf_op jit(solution)/shard_map/ppermute | solution.py:29
  69.8 2.8 %collective-permute-done.15.down_sum_ref = bf16[112,512]{1,0:T(8,128)(2,1)S(1)} collective-permute-done((bf16[112,512]{1,0:T(8,128)(2,1)S(1)}, bf16[112,512]{1,0:T(8,128)(2,1)S(1)}, u32[]{:S(2)}, u32[]{:S(2)}) %collective-permute-start.15) | collective-permute-done | bytes 114720 | tf_op jit(solution)/shard_map/ppermute | solution.py:29
  72.6 0.0 copy-done.4
  72.6 1.1 %shard_map.80 = (bf16[112,1024]{1,0:T(8,128)(2,1)S(1)}, f32[1,112,1024]{2,1,0:T(8,128)}, f32[1,112,1024]{2,1,0:T(8,128)}) custom-call(f32[112,1024]{1,0:T(8,128)S(1)} %get-tuple-element.33.own_ref, bf16[112,512]{1,0:T(8,128)(2,1)S(1)} %collective-permute-done.10.up_ref, bf16[112,512]{1,0:T(8,128)(2,1)S(1)} %collective-permute-done.11.down_ref, ...), custom_call_target="tpu_custom_call" | custom-call | tf_op jit(solution)/shard_map/pallas_call | solution.py:229
  73.8 0.3 collective-permute-start.19
  74.1 4.9 %collective-permute-start.16 = (bf16[112,1024]{1,0:T(8,128)(2,1)S(1)}, bf16[112,1024]{1,0:T(8,128)(2,1)S(1)}, u32[]{:S(2)}, u32[]{:S(2)}) collective-permute-start(bf16[112,1024]{1,0:T(8,128)(2,1)S(1)} %get-tuple-element.42.refs_0_), channel_id=1, source_target_pairs={{0,4},{4,0},{1,5},{5,1},{2,6},{6,2},{3,7},{7,3},{8,12},{12,8},{9,1... | collective-permute-start | bytes 688136 | tf_op jit(solution)/shard_map/ppermute | solution.py:25
  79.0 1.2 %collective-permute-start.22 = (bf16[112,1024]{1,0:T(8,128)(2,1)S(1)}, bf16[112,1024]{1,0:T(8,128)(2,1)S(1)}, u32[]{:S(2)}, u32[]{:S(2)}) collective-permute-start(bf16[112,1024]{1,0:T(8,128)(2,1)S(1)} %get-tuple-element.42.refs_0_), channel_id=1, source_target_pairs={{0,3},{1,0},{2,1},{3,2},{4,7},{5,4},{6,5},{7,6},{8,11},{9,8},{10,9... | collective-permute-start | bytes 688136 | tf_op jit(solution)/shard_map/ppermute | solution.py:29
  80.3 0.8 collective-permute-start.21
  81.1 2.1 %collective-permute-done.19.refs_4_ = bf16[112,1024]{1,0:T(8,128)(2,1)S(1)} collective-permute-done((bf16[112,1024]{1,0:T(8,128)(2,1)S(1)}, bf16[112,1024]{1,0:T(8,128)(2,1)S(1)}, u32[]{:S(2)}, u32[]{:S(2)}) %collective-permute-start.19) | collective-permute-done | bytes 229408 | tf_op jit(solution)/shard_map/ppermute | solution.py:29
  83.2 2.5 %collective-permute-start.20 = (bf16[112,1024]{1,0:T(8,128)(2,1)S(1)}, bf16[112,1024]{1,0:T(8,128)(2,1)S(1)}, u32[]{:S(2)}, u32[]{:S(2)}) collective-permute-start(bf16[112,1024]{1,0:T(8,128)(2,1)S(1)} %collective-permute-done.19.refs_4_), channel_id=1, source_target_pairs={{0,4},{4,0},{1,5},{5,1},{2,6},{6,2},{3,7},{7,3},{8,12},{12,8},{9,1... | collective-permute-start | bytes 688136 | tf_op jit(solution)/shard_map/ppermute | solution.py:25
  85.7 0.0 collective-permute-done.16.refs_1_
  85.7 1.8 %collective-permute-start.18 = (bf16[112,1024]{1,0:T(8,128)(2,1)S(1)}, bf16[112,1024]{1,0:T(8,128)(2,1)S(1)}, u32[]{:S(2)}, u32[]{:S(2)}) collective-permute-start(bf16[112,1024]{1,0:T(8,128)(2,1)S(1)} %collective-permute-done.16.refs_1_), channel_id=1, source_target_pairs={{0,3},{1,0},{2,1},{3,2},{4,7},{5,4},{6,5},{7,6},{8,11},{9,8},{10,9... | collective-permute-start | bytes 688136 | tf_op jit(solution)/shard_map/ppermute | solution.py:29
  87.5 0.2 collective-permute-start.17
  87.7 0.0 collective-permute-done.22.refs_3_
  87.7 1.7 %collective-permute-done.21.refs_2_ = bf16[112,1024]{1,0:T(8,128)(2,1)S(1)} collective-permute-done((bf16[112,1024]{1,0:T(8,128)(2,1)S(1)}, bf16[112,1024]{1,0:T(8,128)(2,1)S(1)}, u32[]{:S(2)}, u32[]{:S(2)}) %collective-permute-start.21) | collective-permute-done | bytes 229408 | tf_op jit(solution)/shard_map/ppermute | solution.py:29
  89.5 3.0 %shard_map.81.refs_3_ = bf16[8,112,1024]{2,1,0:T(8,128)(2,1)} custom-call(s32[16]{0:T(128)S(1)} %stack.82.place_ref, bf16[1024,1024]{1,0:T(8,128)(2,1)S(1)} %copy-done.1, bf16[112,1024]{1,0:T(8,128)(2,1)S(1)} %get-tuple-element.42.refs_0_, bf16[112,1024]{1,0:T(8,128)(2,1)S(1)} %collective-permute-done.16.refs_1_, ...), custom_call_target="tpu_custom_call" | custom-call | tf_op jit(solution)/shard_map/pallas_call | solution.py:145
  92.4 0.0 collective-permute-done.20.refs_2_
  92.4 0.0 collective-permute-done.18.refs_1_
  92.5 2.3 %collective-permute-done.17.refs_0_ = bf16[112,1024]{1,0:T(8,128)(2,1)S(1)} collective-permute-done((bf16[112,1024]{1,0:T(8,128)(2,1)S(1)}, bf16[112,1024]{1,0:T(8,128)(2,1)S(1)}, u32[]{:S(2)}, u32[]{:S(2)}) %collective-permute-start.17) | collective-permute-done | bytes 229408 | tf_op jit(solution)/shard_map/ppermute | solution.py:29
  94.7 2.3 %shard_map.82 = bf16[8,112,1024]{2,1,0:T(8,128)(2,1)} custom-call(s32[16]{0:T(128)S(1)} %stack.82.place_ref, bf16[1024,1024]{1,0:T(8,128)(2,1)S(1)} %copy-done.1, bf16[112,1024]{1,0:T(8,128)(2,1)S(1)} %collective-permute-done.17.refs_0_, bf16[112,1024]{1,0:T(8,128)(2,1)S(1)} %collective-permute-done.18.refs_1_, ...), custom_call_target="tpu_custom_call", output_to_operand_aliasing={{}: (5, {})} | custom-call | tf_op jit(solution)/shard_map/pallas_call | solution.py:145
  (6 shorter events, 0.1 us)
Async XLA Ops:
  0.6 1.0 copy-start
  0.6 10.9 %copy-start.2 = (bf16[128,1,3584]{2,0,1:T(8,128)(2,1)S(1)}, bf16[128,1,3584]{2,0,1:T(8,128)(2,1)}, u32[]{:S(2)}) copy-start(bf16[128,1,3584]{2,0,1:T(8,128)(2,1)} %param.7) | copy-start | bytes 2752516
  4.5 18.6 %all-to-all-start = ((bf16[8,32,1024]{2,1,0:T(8,128)(2,1)}), bf16[8,32,1024]{2,1,0:T(8,128)(2,1)S(1)}, u32[]{:S(2)}, u32[]{:S(2)}) async-start(bf16[8,32,1024]{2,1,0:T(8,128)(2,1)} %bitcast.17), calls=%async_computation | async-start | bytes 1048576 | tf_op jit(solution)/shard_map/all_to_all | solution.py:186
  12.4 17.3 %collective-permute-start.3 = (bf16[4,224,128]{2,1,0:T(8,128)(2,1)S(1)}, bf16[4,224,128]{2,1,0:T(8,128)(2,1)S(1)}, u32[]{:S(2)}, u32[]{:S(2)}) collective-permute-start(bf16[4,224,128]{2,1,0:T(8,128)(2,1)S(1)} %get-tuple-element.26), channel_id=1, source_target_pairs={{0,128},{128,0},{1,129},{129,1},{2,130},{130,2},{3,131},{131,3},{4... | collective-permute-start | bytes 688136 | tf_op jit(solution)/shard_map/ppermute | solution.py:25
  13.2 16.5 %collective-permute-start.4 = (bf16[4,224,128]{2,1,0:T(8,128)(2,1)S(1)}, bf16[4,224,128]{2,1,0:T(8,128)(2,1)S(1)}, u32[]{:S(2)}, u32[]{:S(2)}) collective-permute-start(bf16[4,224,128]{2,1,0:T(8,128)(2,1)S(1)} %get-tuple-element.27), channel_id=1, source_target_pairs={{0,16},{16,0},{1,17},{17,1},{2,18},{18,2},{3,19},{19,3},{4,20},{20... | collective-permute-start | bytes 688136 | tf_op jit(solution)/shard_map/ppermute | solution.py:25
  23.1 5.7 %collective-permute-start.2 = (bf16[32,1024]{1,0:T(8,128)(2,1)S(1)}, bf16[32,1024]{1,0:T(8,128)(2,1)S(1)}, u32[]{:S(2)}, u32[]{:S(2)}) collective-permute-start(bf16[32,1024]{1,0:T(8,128)(2,1)S(1)} %reduce_sum.12), channel_id=1, source_target_pairs={{0,144},{16,128},{128,16},{144,0},{1,145},{17,129},{129,17},{145,1... | collective-permute-start | bytes 196616 | tf_op jit(solution)/shard_map/ppermute | solution.py:33
  25.3 4.3 %collective-permute-start.1 = (bf16[32,1024]{1,0:T(8,128)(2,1)S(1)}, bf16[32,1024]{1,0:T(8,128)(2,1)S(1)}, u32[]{:S(2)}, u32[]{:S(2)}) collective-permute-start(bf16[32,1024]{1,0:T(8,128)(2,1)S(1)} %reduce_sum.12), channel_id=1, source_target_pairs={{0,16},{16,0},{1,17},{17,1},{2,18},{18,2},{3,19},{19,3},{4,20},{20... | collective-permute-start | bytes 196616 | tf_op jit(solution)/shard_map/ppermute | solution.py:25
  25.4 4.3 %collective-permute-start = (bf16[32,1024]{1,0:T(8,128)(2,1)S(1)}, bf16[32,1024]{1,0:T(8,128)(2,1)S(1)}, u32[]{:S(2)}, u32[]{:S(2)}) collective-permute-start(bf16[32,1024]{1,0:T(8,128)(2,1)S(1)} %reduce_sum.12), channel_id=1, source_target_pairs={{0,128},{128,0},{1,129},{129,1},{2,130},{130,2},{3,131},{131,3},{4... | collective-permute-start | bytes 196616 | tf_op jit(solution)/shard_map/ppermute | solution.py:25
  29.7 10.9 %collective-permute-start.7 = (bf16[4,32,1024]{2,1,0:T(8,128)(2,1)S(1)}, bf16[4,32,1024]{2,1,0:T(8,128)(2,1)S(1)}, u32[]{:S(2)}, u32[]{:S(2)}) collective-permute-start(bf16[4,32,1024]{2,1,0:T(8,128)(2,1)S(1)} %pad_maximum_fusion.refs_0_), channel_id=1, source_target_pairs={{0,2},{1,3},{2,0},{3,1},{4,6},{5,7},{6,4},{7,5},{8,10},{9,11},{10,... | collective-permute-start | bytes 786440 | tf_op jit(solution)/shard_map/ppermute | solution.py:29
  31.1 9.4 %collective-permute-start.6 = (bf16[4,32,1024]{2,1,0:T(8,128)(2,1)S(1)}, bf16[4,32,1024]{2,1,0:T(8,128)(2,1)S(1)}, u32[]{:S(2)}, u32[]{:S(2)}) collective-permute-start(bf16[4,32,1024]{2,1,0:T(8,128)(2,1)S(1)} %pad_maximum_fusion.refs_0_), channel_id=1, source_target_pairs={{0,3},{1,0},{2,1},{3,2},{4,7},{5,4},{6,5},{7,6},{8,11},{9,8},{10,9... | collective-permute-start | bytes 786440 | tf_op jit(solution)/shard_map/ppermute | solution.py:29
  33.4 10.6 %collective-permute-start.5 = (bf16[4,32,1024]{2,1,0:T(8,128)(2,1)S(1)}, bf16[4,32,1024]{2,1,0:T(8,128)(2,1)S(1)}, u32[]{:S(2)}, u32[]{:S(2)}) collective-permute-start(bf16[4,32,1024]{2,1,0:T(8,128)(2,1)S(1)} %pad_maximum_fusion.refs_0_), channel_id=1, source_target_pairs={{0,1},{1,2},{2,3},{3,0},{4,5},{5,6},{6,7},{7,4},{8,9},{9,10},{10,1... | collective-permute-start | bytes 786440 | tf_op jit(solution)/shard_map/ppermute | solution.py:29
  33.4 6.9 %collective-permute-start.8 = (bf16[4,224,128]{2,1,0:T(8,128)(2,1)S(1)}, bf16[4,224,128]{2,1,0:T(8,128)(2,1)S(1)}, u32[]{:S(2)}, u32[]{:S(2)}) collective-permute-start(bf16[4,224,128]{2,1,0:T(8,128)(2,1)S(1)} %get-tuple-element.32), channel_id=1, source_target_pairs={{0,144},{16,128},{128,16},{144,0},{1,145},{17,129},{129,17},{145,1... | collective-permute-start | bytes 688136 | tf_op jit(solution)/shard_map/ppermute | solution.py:33
  45.2 27.4 %copy-start.3 = (f32[1,112,1024]{2,1,0:T(8,128)S(1)}, f32[1,112,1024]{2,1,0:T(8,128)}, u32[]{:S(2)}) copy-start(f32[1,112,1024]{2,1,0:T(8,128)} %first_ref.1) | copy-start | bytes 1376260
  45.2 27.4 %copy-start.4 = (f32[1,112,1024]{2,1,0:T(8,128)S(1)}, f32[1,112,1024]{2,1,0:T(8,128)}, u32[]{:S(2)}) copy-start(f32[1,112,1024]{2,1,0:T(8,128)} %second_ref.1) | copy-start | bytes 1376260
  45.2 44.2 %copy-start.1 = (bf16[1024,1024]{1,0:T(8,128)(2,1)S(1)}, bf16[1024,1024]{1,0:T(8,128)(2,1)}, u32[]{:S(2)}) copy-start(bf16[1024,1024]{1,0:T(8,128)(2,1)} %projector_ref.3) | copy-start | bytes 6291460
  45.3 2.6 %collective-permute-start.9 = (bf16[4,112,1024]{2,1,0:T(8,128)(2,1)S(1)}, bf16[4,112,1024]{2,1,0:T(8,128)(2,1)S(1)}, u32[]{:S(2)}, u32[]{:S(2)}) collective-permute-start(bf16[4,112,1024]{2,1,0:T(8,128)(2,1)S(1)} %shard_map.77), channel_id=1, source_target_pairs={{0,8},{8,0},{1,9},{9,1},{2,10},{10,2},{3,11},{11,3},{4,12},{12,4},... | collective-permute-start | bytes 2752520 | tf_op jit(solution)/shard_map/ppermute | solution.py:25
  49.1 9.8 %collective-permute-start.12 = (bf16[112,512]{1,0:T(8,128)(2,1)S(1)}, bf16[112,512]{1,0:T(8,128)(2,1)S(1)}, u32[]{:S(2)}, u32[]{:S(2)}) collective-permute-start(bf16[112,512]{1,0:T(8,128)(2,1)S(1)} %get-tuple-element.38), channel_id=1, source_target_pairs={{0,32},{32,64},{64,96},{96,0},{1,33},{33,65},{65,97},{97,1},{2,34}... | collective-permute-start | bytes 344072 | tf_op jit(solution)/shard_map/ppermute | solution.py:29
  53.0 10.3 %collective-permute-start.13 = (bf16[112,512]{1,0:T(8,128)(2,1)S(1)}, bf16[112,512]{1,0:T(8,128)(2,1)S(1)}, u32[]{:S(2)}, u32[]{:S(2)}) collective-permute-start(bf16[112,512]{1,0:T(8,128)(2,1)S(1)} %get-tuple-element.39), channel_id=1, source_target_pairs={{0,96},{32,0},{64,32},{96,64},{1,97},{33,1},{65,33},{97,65},{2,98}... | collective-permute-start | bytes 344072 | tf_op jit(solution)/shard_map/ppermute | solution.py:29
  53.0 13.3 %collective-permute-start.10 = (bf16[112,512]{1,0:T(8,128)(2,1)S(1)}, bf16[112,512]{1,0:T(8,128)(2,1)S(1)}, u32[]{:S(2)}, u32[]{:S(2)}) collective-permute-start(bf16[112,512]{1,0:T(8,128)(2,1)S(1)} %get-tuple-element.34), channel_id=1, source_target_pairs={{0,32},{32,64},{64,96},{96,0},{1,33},{33,65},{65,97},{97,1},{2,34}... | collective-permute-start | bytes 344072 | tf_op jit(solution)/shard_map/ppermute | solution.py:29
  57.2 10.1 %collective-permute-start.11 = (bf16[112,512]{1,0:T(8,128)(2,1)S(1)}, bf16[112,512]{1,0:T(8,128)(2,1)S(1)}, u32[]{:S(2)}, u32[]{:S(2)}) collective-permute-start(bf16[112,512]{1,0:T(8,128)(2,1)S(1)} %get-tuple-element.35), channel_id=1, source_target_pairs={{0,96},{32,0},{64,32},{96,64},{1,97},{33,1},{65,33},{97,65},{2,98}... | collective-permute-start | bytes 344072 | tf_op jit(solution)/shard_map/ppermute | solution.py:29
  63.4 6.4 %collective-permute-start.14 = (bf16[112,512]{1,0:T(8,128)(2,1)S(1)}, bf16[112,512]{1,0:T(8,128)(2,1)S(1)}, u32[]{:S(2)}, u32[]{:S(2)}) collective-permute-start(bf16[112,512]{1,0:T(8,128)(2,1)S(1)} %get-tuple-element.40), channel_id=1, source_target_pairs={{0,32},{32,64},{64,96},{96,0},{1,33},{33,65},{65,97},{97,1},{2,34}... | collective-permute-start | bytes 344072 | tf_op jit(solution)/shard_map/ppermute | solution.py:29
  64.2 8.5 %collective-permute-start.15 = (bf16[112,512]{1,0:T(8,128)(2,1)S(1)}, bf16[112,512]{1,0:T(8,128)(2,1)S(1)}, u32[]{:S(2)}, u32[]{:S(2)}) collective-permute-start(bf16[112,512]{1,0:T(8,128)(2,1)S(1)} %get-tuple-element.41), channel_id=1, source_target_pairs={{0,96},{32,0},{64,32},{96,64},{1,97},{33,1},{65,33},{97,65},{2,98}... | collective-permute-start | bytes 344072 | tf_op jit(solution)/shard_map/ppermute | solution.py:29
  73.8 9.4 %collective-permute-start.19 = (bf16[112,1024]{1,0:T(8,128)(2,1)S(1)}, bf16[112,1024]{1,0:T(8,128)(2,1)S(1)}, u32[]{:S(2)}, u32[]{:S(2)}) collective-permute-start(bf16[112,1024]{1,0:T(8,128)(2,1)S(1)} %get-tuple-element.42.refs_0_), channel_id=1, source_target_pairs={{0,2},{1,3},{2,0},{3,1},{4,6},{5,7},{6,4},{7,5},{8,10},{9,11},{10,... | collective-permute-start | bytes 688136 | tf_op jit(solution)/shard_map/ppermute | solution.py:29
  74.1 11.6 %collective-permute-start.16 = (bf16[112,1024]{1,0:T(8,128)(2,1)S(1)}, bf16[112,1024]{1,0:T(8,128)(2,1)S(1)}, u32[]{:S(2)}, u32[]{:S(2)}) collective-permute-start(bf16[112,1024]{1,0:T(8,128)(2,1)S(1)} %get-tuple-element.42.refs_0_), channel_id=1, source_target_pairs={{0,4},{4,0},{1,5},{5,1},{2,6},{6,2},{3,7},{7,3},{8,12},{12,8},{9,1... | collective-permute-start | bytes 688136 | tf_op jit(solution)/shard_map/ppermute | solution.py:25
  79.0 8.7 %collective-permute-start.22 = (bf16[112,1024]{1,0:T(8,128)(2,1)S(1)}, bf16[112,1024]{1,0:T(8,128)(2,1)S(1)}, u32[]{:S(2)}, u32[]{:S(2)}) collective-permute-start(bf16[112,1024]{1,0:T(8,128)(2,1)S(1)} %get-tuple-element.42.refs_0_), channel_id=1, source_target_pairs={{0,3},{1,0},{2,1},{3,2},{4,7},{5,4},{6,5},{7,6},{8,11},{9,8},{10,9... | collective-permute-start | bytes 688136 | tf_op jit(solution)/shard_map/ppermute | solution.py:29
  80.3 9.2 %collective-permute-start.21 = (bf16[112,1024]{1,0:T(8,128)(2,1)S(1)}, bf16[112,1024]{1,0:T(8,128)(2,1)S(1)}, u32[]{:S(2)}, u32[]{:S(2)}) collective-permute-start(bf16[112,1024]{1,0:T(8,128)(2,1)S(1)} %get-tuple-element.42.refs_0_), channel_id=1, source_target_pairs={{0,1},{1,2},{2,3},{3,0},{4,5},{5,6},{6,7},{7,4},{8,9},{9,10},{10,1... | collective-permute-start | bytes 688136 | tf_op jit(solution)/shard_map/ppermute | solution.py:29
  83.2 9.2 %collective-permute-start.20 = (bf16[112,1024]{1,0:T(8,128)(2,1)S(1)}, bf16[112,1024]{1,0:T(8,128)(2,1)S(1)}, u32[]{:S(2)}, u32[]{:S(2)}) collective-permute-start(bf16[112,1024]{1,0:T(8,128)(2,1)S(1)} %collective-permute-done.19.refs_4_), channel_id=1, source_target_pairs={{0,4},{4,0},{1,5},{5,1},{2,6},{6,2},{3,7},{7,3},{8,12},{12,8},{9,1... | collective-permute-start | bytes 688136 | tf_op jit(solution)/shard_map/ppermute | solution.py:25
  85.7 6.8 %collective-permute-start.18 = (bf16[112,1024]{1,0:T(8,128)(2,1)S(1)}, bf16[112,1024]{1,0:T(8,128)(2,1)S(1)}, u32[]{:S(2)}, u32[]{:S(2)}) collective-permute-start(bf16[112,1024]{1,0:T(8,128)(2,1)S(1)} %collective-permute-done.16.refs_1_), channel_id=1, source_target_pairs={{0,3},{1,0},{2,1},{3,2},{4,7},{5,4},{6,5},{7,6},{8,11},{9,8},{10,9... | collective-permute-start | bytes 688136 | tf_op jit(solution)/shard_map/ppermute | solution.py:29
  87.5 7.2 %collective-permute-start.17 = (bf16[112,1024]{1,0:T(8,128)(2,1)S(1)}, bf16[112,1024]{1,0:T(8,128)(2,1)S(1)}, u32[]{:S(2)}, u32[]{:S(2)}) collective-permute-start(bf16[112,1024]{1,0:T(8,128)(2,1)S(1)} %collective-permute-done.16.refs_1_), channel_id=1, source_target_pairs={{0,1},{1,2},{2,3},{3,0},{4,5},{5,6},{6,7},{7,4},{8,9},{9,10},{10,1... | collective-permute-start | bytes 688136 | tf_op jit(solution)/shard_map/ppermute | solution.py:29

commit v6 on v5

--- a/solution.py
+++ b/solution.py
@@ -57,10 +57,8 @@
             outs[part][h] = turned[pl.ds(start, block), :]
 
 
-def product(place_ref, core, pieces, grads, whole):
+def product(place_ref, core, grads, whole):
     cols, tokens = grads[0].shape[2:]
-    for j, piece in enumerate(pieces):
-        whole[:, pl.ds(place_ref[4 + YHI * X + j], 1)] = piece[...][:, None]
     rows = []
     for step in range(ZH):
         h = lax.rem(place_ref[2] + step, ZH)
@@ -75,37 +73,37 @@
 
 def send_kernel(place_ref, *refs):
     pieces, grads, (out_ref, whole) = refs[:X], refs[X : X + PARTS], refs[X + PARTS :]
-    out_ref[...] = product(place_ref, 1 - place_ref[3], pieces, grads, whole).astype(narrow)
-
-
-def keep_kernel(place_ref, *refs):
-    pieces, grads, rest = refs[:X], refs[X : X + PARTS], refs[X + PARTS :]
-    came_ref, own_ref, up_far_ref, down_far_ref, up_ref, down_ref, up_held_ref, down_held_ref, whole = rest
-    total = product(place_ref, place_ref[3], pieces, grads, whole) + came_ref[...].astype(wide)
-    lanes = total.shape[-1] // 2
-    own_ref[...] = total[0]
-    up_far_ref[...] = total[2, :, :lanes].astype(narrow)
-    down_far_ref[...] = total[2, :, lanes:].astype(narrow)
-    up_ref[...] = total[1, :, lanes:].astype(narrow)
-    down_ref[...] = total[3, :, :lanes].astype(narrow)
-    up_held_ref[...] = total[1, :, :lanes]
-    down_held_ref[...] = total[3, :, lanes:]
+    for j, piece in enumerate(pieces):
+        whole[:, pl.ds(place_ref[4 + YHI * X + j], 1)] = piece[...][:, None]
+    out_ref[...] = product(place_ref, 1 - place_ref[3], grads, whole).astype(narrow)
+
+
+def keep_kernel(place_ref, whole, *refs):
+    grads, out_ref = refs[:PARTS], refs[PARTS]
+    out_ref[...] = product(place_ref, place_ref[3], grads, whole)
+
+
+def split_kernel(_, mine_ref, came_ref, *outs):
+    own_ref, up_far_ref, down_far_ref, up_ref, down_ref, up_held_ref, down_held_ref = outs
+    lanes = own_ref.shape[-1] // 2
+    left, right = slice(0, lanes), slice(lanes, 2 * lanes)
+
+    def total(step, half):
+        return mine_ref[step, :, half] + came_ref[step, :, half].astype(wide)
+
+    own_ref[:, left] = total(0, left)
+    own_ref[:, right] = total(0, right)
+    up_far_ref[...] = total(2, left).astype(narrow)
+    down_far_ref[...] = total(2, right).astype(narrow)
+    up_ref[...] = total(1, right).astype(narrow)
+    down_ref[...] = total(3, left).astype(narrow)
+    up_held_ref[...] = total(1, left)
+    down_held_ref[...] = total(3, right)
 
 
 def relay_kernel(up_held_ref, down_held_ref, up_ref, down_ref, up_out_ref, down_out_ref):
     up_out_ref[...] = (up_held_ref[...] + up_ref[...].astype(wide)).astype(narrow)
     down_out_ref[...] = (down_held_ref[...] + down_ref[...].astype(wide)).astype(narrow)
-
-
-def gradient_call(body, outs, tokens, rank, extra):
-    return pl.pallas_call(
-        body,
-        out_shape=[jax.ShapeDtypeStruct(shape, dtype) for shape, dtype in outs],
-        in_specs=[SMEM] + [VMEM] * (X + PARTS + extra),
-        out_specs=[VMEM] * len(outs),
-        scratch_shapes=[pltpu.VMEM((PARTS, X, tokens // X, rank), narrow)],
-        compiler_params=pltpu.CompilerParams(vmem_limit_bytes=16 * 2**20),
-    )
 
 
 def adam_kernel(own_ref, up_ref, down_ref, up_sum_ref, down_sum_ref, first_ref, second_ref, *outs):
@@ -203,18 +201,17 @@
     projected = [piece] + [shift(piece, "x", X, step) for step in (1, 3, 2)]
     grads = [g.reshape(ZH, CORE, cols, tokens) for g in [grads[0]] + moved]
     one = (cols, rank)
-    (sent,) = gradient_call(send_kernel, [((ZH,) + one, narrow)], tokens, rank, 0)(
-        place, *projected, *grads
-    )
+    part = (cols, rank // 2)
+    sent, whole = local(
+        send_kernel,
+        [((ZH,) + one, narrow), ((PARTS, X, tokens // X, rank), narrow)],
+        X + PARTS,
+    )(place, *projected, *grads)
     came = swap(sent, "core")
-    part = (cols, rank // 2)
-    own, up_far, down_far, up, down, up_held, down_held = gradient_call(
-        keep_kernel,
-        [(one, wide)] + [(part, narrow)] * 4 + [(part, wide)] * 2,
-        tokens,
-        rank,
-        1,
-    )(place, *projected, *grads, came)
+    (mine,) = local(keep_kernel, [((ZH,) + one, wide)], 1 + PARTS)(place, whole, *grads)
+    own, up_far, down_far, up, down, up_held, down_held = local(
+        split_kernel, [(one, wide)] + [(part, narrow)] * 4 + [(part, wide)] * 2, 2
+    )(place, mine, came)
     up_far, down_far = shift(up_far, "zh", ZH, 1), shift(down_far, "zh", ZH, 3)
     up, down = shift(up, "zh", ZH, 1), shift(down, "zh", ZH, 3)
     up_sum, down_sum = pl.pallas_call(

time: 97.4 us -> 96.8 us (level)
  waiting for transfers between devices: 39.8 us -> 38.2 us
    ppermute x7, waiting for transfers between devices: 3.29 us -> 2.06 us  [swap(): return lax.ppermute(value, axis, [(0, 1), (1, 0)])]
    pallas_call x2 -> x3, Pallas kernels: 2.53 us -> 3.13 us  [the longest x1 1.26 us: shards(): local(send_kernel, [((ZH,) + one, narrow), ((PARTS, X, tokens // X, rank)...]
  transfers between devices with their start and end apart: 24 -> 24, of which waited for: 16 -> 16; matrix products, arithmetic and copies ran while one was open for 0% -> 0% of each run, Pallas kernels for 4% -> 5%
where the time goes in v6:
time: 96.8 us; the launch traced here: 96.6 us
  starting transfers between devices  42.9 us (44%)
  waiting for transfers between devices  38.2 us (39%)
  Pallas kernels  10.5 us (11%)
  matrix products  2.04 us (2%)
  local copies, waits for them, and re-layouts  1.91 us (2%)
    ppermute x14, waiting for transfers between devices, shift(): lax.ppermute(value, axis, [(i, (i + step) % size) for i in range(size)])  21.9 us
    ppermute x14, starting transfers between devices, shift(): lax.ppermute(value, axis, [(i, (i + step) % size) for i in range(size)])  19.1 us
    ppermute x7, starting transfers between devices, swap(): return lax.ppermute(value, axis, [(0, 1), (1, 0)])  12 us
    all_to_all x1, waiting for transfers between devices, shards(): lax.all_to_all(jnp.broadcast_to(share, (YHI,) + share.shape[1:]).reshape(...  7.96 us
    all_to_all x1, starting transfers between devices, shards(): lax.all_to_all(jnp.broadcast_to(share, (YHI,) + share.shape[1:]).reshape(...  6.93 us
    ppermute x2, waiting for transfers between devices, exchanged(): lax.ppermute(over_both, ('ylo', 'zl'), [(i, 3 - i) for i in range(4)])  6.31 us
    pallas_call x2, Pallas kernels, back(): pl.pallas_call(functools.partial(back_kernel, count, first), out_shape=ja...  5.28 us
    ppermute x2, starting transfers between devices, exchanged(): lax.ppermute(over_both, ('ylo', 'zl'), [(i, 3 - i) for i in range(4)])  4.82 us
  transfers between devices with their start and end apart: 24, of which 16 were waited for; matrix products, arithmetic and copies ran while one was open for 0% of the time, Pallas kernels for 5%

profile of v6, /device:TPU:64, one launch (start us, length us, event | category | flops | bytes accessed | tf_op | source)
XLA Modules:
  0.0 96.6 jit_solution(1146544819969818318)
XLA Ops:
  0.6 0.0 copy-start
  0.7 0.9 copy-done
  1.6 2.0 %convolution_convert_fusion = bf16[128,1024]{1,0:T(8,128)(2,1)S(1)} fusion(bf16[128,1024]{1,0:T(8,128)(2,1)S(1)} %copy-done, bf16[1024,1024]{1,0:T(8,128)(2,1)} %projector_ref.3), kind=kOutput, calls=%fused_computation | convolution fusion | flops 268566528 | bytes 2621440 | tf_op jit(solution)/shard_map/dot_general | solution.py:181
  3.6 0.9 broadcast_in_dim.8
  4.5 6.9 %all-to-all-start = ((bf16[8,32,1024]{2,1,0:T(8,128)(2,1)}), bf16[8,32,1024]{2,1,0:T(8,128)(2,1)S(1)}, u32[]{:S(2)}, u32[]{:S(2)}) async-start(bf16[8,32,1024]{2,1,0:T(8,128)(2,1)} %bitcast.17), calls=%async_computation | async-start | bytes 1048576 | tf_op jit(solution)/shard_map/all_to_all | solution.py:184
  11.4 0.1 stack.82.place_ref._
  11.5 0.9 shard_map.76
  12.4 0.8 collective-permute-start.3
  13.2 1.9 %collective-permute-start.4 = (bf16[4,224,128]{2,1,0:T(8,128)(2,1)S(1)}, bf16[4,224,128]{2,1,0:T(8,128)(2,1)S(1)}, u32[]{:S(2)}, u32[]{:S(2)}) collective-permute-start(bf16[4,224,128]{2,1,0:T(8,128)(2,1)S(1)} %get-tuple-element.29), channel_id=1, source_target_pairs={{0,16},{16,0},{1,17},{17,1},{2,18},{18,2},{3,19},{19,3},{4,20},{20... | collective-permute-start | bytes 688136 | tf_op jit(solution)/shard_map/ppermute | solution.py:25
  15.1 8.0 %all-to-all-done = bf16[8,32,1024]{2,1,0:T(8,128)(2,1)S(1)} async-done(((bf16[8,32,1024]{2,1,0:T(8,128)(2,1)}), bf16[8,32,1024]{2,1,0:T(8,128)(2,1)S(1)}, u32[]{:S(2)}, u32[]{:S(2)}) %all-to-all-start) | async-done | bytes 524320 | tf_op jit(solution)/shard_map/all_to_all | solution.py:184
  23.1 0.1 reduce_sum.12
  23.1 2.1 %collective-permute-start.2 = (bf16[32,1024]{1,0:T(8,128)(2,1)S(1)}, bf16[32,1024]{1,0:T(8,128)(2,1)S(1)}, u32[]{:S(2)}, u32[]{:S(2)}) collective-permute-start(bf16[32,1024]{1,0:T(8,128)(2,1)S(1)} %reduce_sum.12), channel_id=1, source_target_pairs={{0,144},{16,128},{128,16},{144,0},{1,145},{17,129},{129,17},{145,1... | collective-permute-start | bytes 196616 | tf_op jit(solution)/shard_map/ppermute | solution.py:33
  25.3 0.1 collective-permute-start.1
  25.4 1.3 %collective-permute-start = (bf16[32,1024]{1,0:T(8,128)(2,1)S(1)}, bf16[32,1024]{1,0:T(8,128)(2,1)S(1)}, u32[]{:S(2)}, u32[]{:S(2)}) collective-permute-start(bf16[32,1024]{1,0:T(8,128)(2,1)S(1)} %reduce_sum.12), channel_id=1, source_target_pairs={{0,128},{128,0},{1,129},{129,1},{2,130},{130,2},{3,131},{131,3},{4... | collective-permute-start | bytes 196616 | tf_op jit(solution)/shard_map/ppermute | solution.py:25
  26.7 2.1 %collective-permute-done.2 = bf16[32,1024]{1,0:T(8,128)(2,1)S(1)} collective-permute-done((bf16[32,1024]{1,0:T(8,128)(2,1)S(1)}, bf16[32,1024]{1,0:T(8,128)(2,1)S(1)}, u32[]{:S(2)}, u32[]{:S(2)}) %collective-permute-start.2) | collective-permute-done | bytes 65568 | tf_op jit(solution)/shard_map/ppermute | solution.py:33
  28.8 0.7 collective-permute-done.1
  29.5 0.1 collective-permute-done
  29.7 0.0 collective-permute-done.3
  29.7 0.0 collective-permute-done.4
  29.7 1.4 %collective-permute-start.7 = (bf16[4,32,1024]{2,1,0:T(8,128)(2,1)S(1)}, bf16[4,32,1024]{2,1,0:T(8,128)(2,1)S(1)}, u32[]{:S(2)}, u32[]{:S(2)}) collective-permute-start(bf16[4,32,1024]{2,1,0:T(8,128)(2,1)S(1)} %pad_maximum_fusion.refs_0_), channel_id=1, source_target_pairs={{0,2},{1,3},{2,0},{3,1},{4,6},{5,7},{6,4},{7,5},{8,10},{9,11},{10,... | collective-permute-start | bytes 786440 | tf_op jit(solution)/shard_map/ppermute | solution.py:29
  31.1 2.2 %collective-permute-start.6 = (bf16[4,32,1024]{2,1,0:T(8,128)(2,1)S(1)}, bf16[4,32,1024]{2,1,0:T(8,128)(2,1)S(1)}, u32[]{:S(2)}, u32[]{:S(2)}) collective-permute-start(bf16[4,32,1024]{2,1,0:T(8,128)(2,1)S(1)} %pad_maximum_fusion.refs_0_), channel_id=1, source_target_pairs={{0,3},{1,0},{2,1},{3,2},{4,7},{5,4},{6,5},{7,6},{8,11},{9,8},{10,9... | collective-permute-start | bytes 786440 | tf_op jit(solution)/shard_map/ppermute | solution.py:29
  33.4 0.0 collective-permute-start.5
  33.4 2.7 %collective-permute-start.8 = (bf16[4,224,128]{2,1,0:T(8,128)(2,1)S(1)}, bf16[4,224,128]{2,1,0:T(8,128)(2,1)S(1)}, u32[]{:S(2)}, u32[]{:S(2)}) collective-permute-start(bf16[4,224,128]{2,1,0:T(8,128)(2,1)S(1)} %get-tuple-element.34), channel_id=1, source_target_pairs={{0,144},{16,128},{128,16},{144,0},{1,145},{17,129},{129,17},{145,1... | collective-permute-start | bytes 688136 | tf_op jit(solution)/shard_map/ppermute | solution.py:33
  36.1 4.2 %collective-permute-done.8 = bf16[4,224,128]{2,1,0:T(8,128)(2,1)S(1)} collective-permute-done((bf16[4,224,128]{2,1,0:T(8,128)(2,1)S(1)}, bf16[4,224,128]{2,1,0:T(8,128)(2,1)S(1)}, u32[]{:S(2)}, u32[]{:S(2)}) %collective-permute-start.8) | collective-permute-done | bytes 229408 | tf_op jit(solution)/shard_map/ppermute | solution.py:33
  40.3 0.3 collective-permute-done.7.refs_3_
  40.6 0.0 collective-permute-done.6.refs_2_
  40.6 3.4 %collective-permute-done.5.refs_1_ = bf16[4,32,1024]{2,1,0:T(8,128)(2,1)S(1)} collective-permute-done((bf16[4,32,1024]{2,1,0:T(8,128)(2,1)S(1)}, bf16[4,32,1024]{2,1,0:T(8,128)(2,1)S(1)}, u32[]{:S(2)}, u32[]{:S(2)}) %collective-permute-start.5) | collective-permute-done | bytes 262176 | tf_op jit(solution)/shard_map/ppermute | solution.py:29
  43.9 1.3 %shard_map.77 = (bf16[4,112,1024]{2,1,0:T(8,128)(2,1)S(1)}, bf16[4,4,32,1024]{3,2,1,0:T(8,128)(2,1)S(1)}) custom-call(s32[16]{0:T(128)S(1)} %stack.82.place_ref._, bf16[4,32,1024]{2,1,0:T(8,128)(2,1)S(1)} %pad_maximum_fusion.refs_0_, bf16[4,32,1024]{2,1,0:T(8,128)(2,1)S(1)} %collective-permute-done.5.refs_1_, ...), custom_call_target="tpu_custom_call" | custom-call | tf_op jit(solution)/shard_map/pallas_call | solution.py:205
  45.2 0.1 collective-permute-start.9
  45.3 1.2 %shard_map.78.mine_ref = f32[4,112,1024]{2,1,0:T(8,128)S(1)} custom-call(s32[16]{0:T(128)S(1)} %stack.82.place_ref._, bf16[4,4,32,1024]{3,2,1,0:T(8,128)(2,1)S(1)} %get-tuple-element.35.whole, bf16[4,2,112,128]{3,2,1,0:T(8,128)(2,1)S(1)} %bitcast.31, bf16[4,2,112,128]{3,2,1,0:T(8,128)(2,1)S(1)} %bitcast.33, bf16[4,2,112,128]{3,2,1,0:T(8,128)(2,1)S(1)} %bitcast.35, ...), custom_call_target="tpu_custom_call" | custom-call | tf_op jit(solution)/shard_map/pallas_call | solution.py:211
  46.5 0.0 copy-start.3
  46.5 0.0 copy-start.4
  46.5 0.0 copy-start.1
  46.5 1.2 %collective-permute-done.9.came_ref = bf16[4,112,1024]{2,1,0:T(8,128)(2,1)S(1)} collective-permute-done((bf16[4,112,1024]{2,1,0:T(8,128)(2,1)S(1)}, bf16[4,112,1024]{2,1,0:T(8,128)(2,1)S(1)}, u32[]{:S(2)}, u32[]{:S(2)}) %collective-permute-start.9) | collective-permute-done | bytes 917536 | tf_op jit(solution)/shard_map/ppermute | solution.py:25
  47.8 0.7 shard_map.79
  48.5 4.0 %collective-permute-start.12 = (bf16[112,512]{1,0:T(8,128)(2,1)S(1)}, bf16[112,512]{1,0:T(8,128)(2,1)S(1)}, u32[]{:S(2)}, u32[]{:S(2)}) collective-permute-start(bf16[112,512]{1,0:T(8,128)(2,1)S(1)} %get-tuple-element.42), channel_id=1, source_target_pairs={{0,32},{32,64},{64,96},{96,0},{1,33},{33,65},{65,97},{97,1},{2,34}... | collective-permute-start | bytes 344072 | tf_op jit(solution)/shard_map/ppermute | solution.py:29
  52.4 0.0 collective-permute-start.13
  52.4 4.1 %collective-permute-start.10 = (bf16[112,512]{1,0:T(8,128)(2,1)S(1)}, bf16[112,512]{1,0:T(8,128)(2,1)S(1)}, u32[]{:S(2)}, u32[]{:S(2)}) collective-permute-start(bf16[112,512]{1,0:T(8,128)(2,1)S(1)} %get-tuple-element.38), channel_id=1, source_target_pairs={{0,32},{32,64},{64,96},{96,0},{1,33},{33,65},{65,97},{97,1},{2,34}... | collective-permute-start | bytes 344072 | tf_op jit(solution)/shard_map/ppermute | solution.py:29
  56.6 0.0 collective-permute-start.11
  56.6 1.7 %collective-permute-done.12.up_ref = bf16[112,512]{1,0:T(8,128)(2,1)S(1)} collective-permute-done((bf16[112,512]{1,0:T(8,128)(2,1)S(1)}, bf16[112,512]{1,0:T(8,128)(2,1)S(1)}, u32[]{:S(2)}, u32[]{:S(2)}) %collective-permute-start.12) | collective-permute-done | bytes 114720 | tf_op jit(solution)/shard_map/ppermute | solution.py:29
  58.2 4.5 %collective-permute-done.13.down_ref = bf16[112,512]{1,0:T(8,128)(2,1)S(1)} collective-permute-done((bf16[112,512]{1,0:T(8,128)(2,1)S(1)}, bf16[112,512]{1,0:T(8,128)(2,1)S(1)}, u32[]{:S(2)}, u32[]{:S(2)}) %collective-permute-start.13) | collective-permute-done | bytes 114720 | tf_op jit(solution)/shard_map/ppermute | solution.py:29
  62.7 0.1 shard_map.80
  62.8 0.8 collective-permute-start.14
  63.5 2.2 %collective-permute-start.15 = (bf16[112,512]{1,0:T(8,128)(2,1)S(1)}, bf16[112,512]{1,0:T(8,128)(2,1)S(1)}, u32[]{:S(2)}, u32[]{:S(2)}) collective-permute-start(bf16[112,512]{1,0:T(8,128)(2,1)S(1)} %get-tuple-element.45), channel_id=1, source_target_pairs={{0,96},{32,0},{64,32},{96,64},{1,97},{33,1},{65,33},{97,65},{2,98}... | collective-permute-start | bytes 344072 | tf_op jit(solution)/shard_map/ppermute | solution.py:29
  65.8 0.0 collective-permute-done.10.up_ref
  65.8 0.9 collective-permute-done.11.down_ref
  66.6 2.5 %collective-permute-done.14.up_sum_ref = bf16[112,512]{1,0:T(8,128)(2,1)S(1)} collective-permute-done((bf16[112,512]{1,0:T(8,128)(2,1)S(1)}, bf16[112,512]{1,0:T(8,128)(2,1)S(1)}, u32[]{:S(2)}, u32[]{:S(2)}) %collective-permute-start.14) | collective-permute-done | bytes 114720 | tf_op jit(solution)/shard_map/ppermute | solution.py:29
  69.2 2.8 %collective-permute-done.15.down_sum_ref = bf16[112,512]{1,0:T(8,128)(2,1)S(1)} collective-permute-done((bf16[112,512]{1,0:T(8,128)(2,1)S(1)}, bf16[112,512]{1,0:T(8,128)(2,1)S(1)}, u32[]{:S(2)}, u32[]{:S(2)}) %collective-permute-start.15) | collective-permute-done | bytes 114720 | tf_op jit(solution)/shard_map/ppermute | solution.py:29
  72.0 1.1 %shard_map.81 = (bf16[112,1024]{1,0:T(8,128)(2,1)S(1)}, f32[1,112,1024]{2,1,0:T(8,128)}, f32[1,112,1024]{2,1,0:T(8,128)}) custom-call(f32[112,1024]{1,0:T(8,128)S(1)} %get-tuple-element.37.own_ref, bf16[112,512]{1,0:T(8,128)(2,1)S(1)} %collective-permute-done.10.up_ref, bf16[112,512]{1,0:T(8,128)(2,1)S(1)} %collective-permute-done.11.down_ref, ...), custom_call_target="tpu_custom_call" | custom-call | tf_op jit(solution)/shard_map/pallas_call | solution.py:226
  73.2 0.3 collective-permute-start.19
  73.5 4.9 %collective-permute-start.16 = (bf16[112,1024]{1,0:T(8,128)(2,1)S(1)}, bf16[112,1024]{1,0:T(8,128)(2,1)S(1)}, u32[]{:S(2)}, u32[]{:S(2)}) collective-permute-start(bf16[112,1024]{1,0:T(8,128)(2,1)S(1)} %get-tuple-element.46.refs_0_), channel_id=1, source_target_pairs={{0,4},{4,0},{1,5},{5,1},{2,6},{6,2},{3,7},{7,3},{8,12},{12,8},{9,1... | collective-permute-start | bytes 688136 | tf_op jit(solution)/shard_map/ppermute | solution.py:25
  78.4 1.2 %collective-permute-start.22 = (bf16[112,1024]{1,0:T(8,128)(2,1)S(1)}, bf16[112,1024]{1,0:T(8,128)(2,1)S(1)}, u32[]{:S(2)}, u32[]{:S(2)}) collective-permute-start(bf16[112,1024]{1,0:T(8,128)(2,1)S(1)} %get-tuple-element.46.refs_0_), channel_id=1, source_target_pairs={{0,3},{1,0},{2,1},{3,2},{4,7},{5,4},{6,5},{7,6},{8,11},{9,8},{10,9... | collective-permute-start | bytes 688136 | tf_op jit(solution)/shard_map/ppermute | solution.py:29
  79.6 0.8 collective-permute-start.21
  80.4 2.0 %collective-permute-done.19.refs_4_ = bf16[112,1024]{1,0:T(8,128)(2,1)S(1)} collective-permute-done((bf16[112,1024]{1,0:T(8,128)(2,1)S(1)}, bf16[112,1024]{1,0:T(8,128)(2,1)S(1)}, u32[]{:S(2)}, u32[]{:S(2)}) %collective-permute-start.19) | collective-permute-done | bytes 229408 | tf_op jit(solution)/shard_map/ppermute | solution.py:29
  82.4 2.8 %collective-permute-start.20 = (bf16[112,1024]{1,0:T(8,128)(2,1)S(1)}, bf16[112,1024]{1,0:T(8,128)(2,1)S(1)}, u32[]{:S(2)}, u32[]{:S(2)}) collective-permute-start(bf16[112,1024]{1,0:T(8,128)(2,1)S(1)} %collective-permute-done.19.refs_4_), channel_id=1, source_target_pairs={{0,4},{4,0},{1,5},{5,1},{2,6},{6,2},{3,7},{7,3},{8,12},{12,8},{9,1... | collective-permute-start | bytes 688136 | tf_op jit(solution)/shard_map/ppermute | solution.py:25
  85.2 0.0 collective-permute-done.16.refs_1_
  85.2 1.7 %collective-permute-start.18 = (bf16[112,1024]{1,0:T(8,128)(2,1)S(1)}, bf16[112,1024]{1,0:T(8,128)(2,1)S(1)}, u32[]{:S(2)}, u32[]{:S(2)}) collective-permute-start(bf16[112,1024]{1,0:T(8,128)(2,1)S(1)} %collective-permute-done.16.refs_1_), channel_id=1, source_target_pairs={{0,3},{1,0},{2,1},{3,2},{4,7},{5,4},{6,5},{7,6},{8,11},{9,8},{10,9... | collective-permute-start | bytes 688136 | tf_op jit(solution)/shard_map/ppermute | solution.py:29
  86.9 0.3 collective-permute-start.17
  87.2 1.6 %collective-permute-done.21.refs_2_ = bf16[112,1024]{1,0:T(8,128)(2,1)S(1)} collective-permute-done((bf16[112,1024]{1,0:T(8,128)(2,1)S(1)}, bf16[112,1024]{1,0:T(8,128)(2,1)S(1)}, u32[]{:S(2)}, u32[]{:S(2)}) %collective-permute-start.21) | collective-permute-done | bytes 229408 | tf_op jit(solution)/shard_map/ppermute | solution.py:29
  88.8 3.0 %shard_map.82.refs_3_ = bf16[8,112,1024]{2,1,0:T(8,128)(2,1)} custom-call(s32[16]{0:T(128)S(1)} %stack.82.place_ref._, bf16[1024,1024]{1,0:T(8,128)(2,1)S(1)} %copy-done.1, bf16[112,1024]{1,0:T(8,128)(2,1)S(1)} %get-tuple-element.46.refs_0_, bf16[112,1024]{1,0:T(8,128)(2,1)S(1)} %collective-permute-done.16.refs_1_, ...), custom_call_target="tpu_custom_call" | custom-call | tf_op jit(solution)/shard_map/pallas_call | solution.py:143
  91.8 0.0 collective-permute-done.20.refs_2_
  91.8 0.0 collective-permute-done.18.refs_1_
  91.8 2.3 %collective-permute-done.17.refs_0_ = bf16[112,1024]{1,0:T(8,128)(2,1)S(1)} collective-permute-done((bf16[112,1024]{1,0:T(8,128)(2,1)S(1)}, bf16[112,1024]{1,0:T(8,128)(2,1)S(1)}, u32[]{:S(2)}, u32[]{:S(2)}) %collective-permute-start.17) | collective-permute-done | bytes 229408 | tf_op jit(solution)/shard_map/ppermute | solution.py:29
  94.1 2.3 %shard_map.83 = bf16[8,112,1024]{2,1,0:T(8,128)(2,1)} custom-call(s32[16]{0:T(128)S(1)} %stack.82.place_ref._, bf16[1024,1024]{1,0:T(8,128)(2,1)S(1)} %copy-done.1, bf16[112,1024]{1,0:T(8,128)(2,1)S(1)} %collective-permute-done.17.refs_0_, bf16[112,1024]{1,0:T(8,128)(2,1)S(1)} %collective-permute-done.18.refs_1_, ...), custom_call_target="tpu_custom_call", output_to_operand_aliasing={{}: (5, {})} | custom-call | tf_op jit(solution)/shard_map/pallas_call | solution.py:143
  (7 shorter events, 0.0 us)
Async XLA Ops:
  0.6 1.0 copy-start
  0.6 10.9 %copy-start.2 = (bf16[128,1,3584]{2,0,1:T(8,128)(2,1)S(1)}, bf16[128,1,3584]{2,0,1:T(8,128)(2,1)}, u32[]{:S(2)}) copy-start(bf16[128,1,3584]{2,0,1:T(8,128)(2,1)} %param.7) | copy-start | bytes 2752516
  4.5 18.6 %all-to-all-start = ((bf16[8,32,1024]{2,1,0:T(8,128)(2,1)}), bf16[8,32,1024]{2,1,0:T(8,128)(2,1)S(1)}, u32[]{:S(2)}, u32[]{:S(2)}) async-start(bf16[8,32,1024]{2,1,0:T(8,128)(2,1)} %bitcast.17), calls=%async_computation | async-start | bytes 1048576 | tf_op jit(solution)/shard_map/all_to_all | solution.py:184
  12.4 17.3 %collective-permute-start.3 = (bf16[4,224,128]{2,1,0:T(8,128)(2,1)S(1)}, bf16[4,224,128]{2,1,0:T(8,128)(2,1)S(1)}, u32[]{:S(2)}, u32[]{:S(2)}) collective-permute-start(bf16[4,224,128]{2,1,0:T(8,128)(2,1)S(1)} %get-tuple-element.28), channel_id=1, source_target_pairs={{0,128},{128,0},{1,129},{129,1},{2,130},{130,2},{3,131},{131,3},{4... | collective-permute-start | bytes 688136 | tf_op jit(solution)/shard_map/ppermute | solution.py:25
  13.2 16.5 %collective-permute-start.4 = (bf16[4,224,128]{2,1,0:T(8,128)(2,1)S(1)}, bf16[4,224,128]{2,1,0:T(8,128)(2,1)S(1)}, u32[]{:S(2)}, u32[]{:S(2)}) collective-permute-start(bf16[4,224,128]{2,1,0:T(8,128)(2,1)S(1)} %get-tuple-element.29), channel_id=1, source_target_pairs={{0,16},{16,0},{1,17},{17,1},{2,18},{18,2},{3,19},{19,3},{4,20},{20... | collective-permute-start | bytes 688136 | tf_op jit(solution)/shard_map/ppermute | solution.py:25
  23.1 5.7 %collective-permute-start.2 = (bf16[32,1024]{1,0:T(8,128)(2,1)S(1)}, bf16[32,1024]{1,0:T(8,128)(2,1)S(1)}, u32[]{:S(2)}, u32[]{:S(2)}) collective-permute-start(bf16[32,1024]{1,0:T(8,128)(2,1)S(1)} %reduce_sum.12), channel_id=1, source_target_pairs={{0,144},{16,128},{128,16},{144,0},{1,145},{17,129},{129,17},{145,1... | collective-permute-start | bytes 196616 | tf_op jit(solution)/shard_map/ppermute | solution.py:33
  25.3 4.3 %collective-permute-start.1 = (bf16[32,1024]{1,0:T(8,128)(2,1)S(1)}, bf16[32,1024]{1,0:T(8,128)(2,1)S(1)}, u32[]{:S(2)}, u32[]{:S(2)}) collective-permute-start(bf16[32,1024]{1,0:T(8,128)(2,1)S(1)} %reduce_sum.12), channel_id=1, source_target_pairs={{0,16},{16,0},{1,17},{17,1},{2,18},{18,2},{3,19},{19,3},{4,20},{20... | collective-permute-start | bytes 196616 | tf_op jit(solution)/shard_map/ppermute | solution.py:25
  25.4 4.3 %collective-permute-start = (bf16[32,1024]{1,0:T(8,128)(2,1)S(1)}, bf16[32,1024]{1,0:T(8,128)(2,1)S(1)}, u32[]{:S(2)}, u32[]{:S(2)}) collective-permute-start(bf16[32,1024]{1,0:T(8,128)(2,1)S(1)} %reduce_sum.12), channel_id=1, source_target_pairs={{0,128},{128,0},{1,129},{129,1},{2,130},{130,2},{3,131},{131,3},{4... | collective-permute-start | bytes 196616 | tf_op jit(solution)/shard_map/ppermute | solution.py:25
  29.7 10.9 %collective-permute-start.7 = (bf16[4,32,1024]{2,1,0:T(8,128)(2,1)S(1)}, bf16[4,32,1024]{2,1,0:T(8,128)(2,1)S(1)}, u32[]{:S(2)}, u32[]{:S(2)}) collective-permute-start(bf16[4,32,1024]{2,1,0:T(8,128)(2,1)S(1)} %pad_maximum_fusion.refs_0_), channel_id=1, source_target_pairs={{0,2},{1,3},{2,0},{3,1},{4,6},{5,7},{6,4},{7,5},{8,10},{9,11},{10,... | collective-permute-start | bytes 786440 | tf_op jit(solution)/shard_map/ppermute | solution.py:29
  31.1 9.4 %collective-permute-start.6 = (bf16[4,32,1024]{2,1,0:T(8,128)(2,1)S(1)}, bf16[4,32,1024]{2,1,0:T(8,128)(2,1)S(1)}, u32[]{:S(2)}, u32[]{:S(2)}) collective-permute-start(bf16[4,32,1024]{2,1,0:T(8,128)(2,1)S(1)} %pad_maximum_fusion.refs_0_), channel_id=1, source_target_pairs={{0,3},{1,0},{2,1},{3,2},{4,7},{5,4},{6,5},{7,6},{8,11},{9,8},{10,9... | collective-permute-start | bytes 786440 | tf_op jit(solution)/shard_map/ppermute | solution.py:29
  33.4 10.6 %collective-permute-start.5 = (bf16[4,32,1024]{2,1,0:T(8,128)(2,1)S(1)}, bf16[4,32,1024]{2,1,0:T(8,128)(2,1)S(1)}, u32[]{:S(2)}, u32[]{:S(2)}) collective-permute-start(bf16[4,32,1024]{2,1,0:T(8,128)(2,1)S(1)} %pad_maximum_fusion.refs_0_), channel_id=1, source_target_pairs={{0,1},{1,2},{2,3},{3,0},{4,5},{5,6},{6,7},{7,4},{8,9},{9,10},{10,1... | collective-permute-start | bytes 786440 | tf_op jit(solution)/shard_map/ppermute | solution.py:29
  33.4 6.9 %collective-permute-start.8 = (bf16[4,224,128]{2,1,0:T(8,128)(2,1)S(1)}, bf16[4,224,128]{2,1,0:T(8,128)(2,1)S(1)}, u32[]{:S(2)}, u32[]{:S(2)}) collective-permute-start(bf16[4,224,128]{2,1,0:T(8,128)(2,1)S(1)} %get-tuple-element.34), channel_id=1, source_target_pairs={{0,144},{16,128},{128,16},{144,0},{1,145},{17,129},{129,17},{145,1... | collective-permute-start | bytes 688136 | tf_op jit(solution)/shard_map/ppermute | solution.py:33
  45.2 2.6 %collective-permute-start.9 = (bf16[4,112,1024]{2,1,0:T(8,128)(2,1)S(1)}, bf16[4,112,1024]{2,1,0:T(8,128)(2,1)S(1)}, u32[]{:S(2)}, u32[]{:S(2)}) collective-permute-start(bf16[4,112,1024]{2,1,0:T(8,128)(2,1)S(1)} %get-tuple-element.36), channel_id=1, source_target_pairs={{0,8},{8,0},{1,9},{9,1},{2,10},{10,2},{3,11},{11,3},{4,12},{12,4},... | collective-permute-start | bytes 2752520 | tf_op jit(solution)/shard_map/ppermute | solution.py:25
  46.5 25.5 %copy-start.3 = (f32[1,112,1024]{2,1,0:T(8,128)S(1)}, f32[1,112,1024]{2,1,0:T(8,128)}, u32[]{:S(2)}) copy-start(f32[1,112,1024]{2,1,0:T(8,128)} %first_ref.1) | copy-start | bytes 1376260
  46.5 25.5 %copy-start.4 = (f32[1,112,1024]{2,1,0:T(8,128)S(1)}, f32[1,112,1024]{2,1,0:T(8,128)}, u32[]{:S(2)}) copy-start(f32[1,112,1024]{2,1,0:T(8,128)} %second_ref.1) | copy-start | bytes 1376260
  46.5 42.3 %copy-start.1 = (bf16[1024,1024]{1,0:T(8,128)(2,1)S(1)}, bf16[1024,1024]{1,0:T(8,128)(2,1)}, u32[]{:S(2)}) copy-start(bf16[1024,1024]{1,0:T(8,128)(2,1)} %projector_ref.3) | copy-start | bytes 6291460
  48.5 9.8 %collective-permute-start.12 = (bf16[112,512]{1,0:T(8,128)(2,1)S(1)}, bf16[112,512]{1,0:T(8,128)(2,1)S(1)}, u32[]{:S(2)}, u32[]{:S(2)}) collective-permute-start(bf16[112,512]{1,0:T(8,128)(2,1)S(1)} %get-tuple-element.42), channel_id=1, source_target_pairs={{0,32},{32,64},{64,96},{96,0},{1,33},{33,65},{65,97},{97,1},{2,34}... | collective-permute-start | bytes 344072 | tf_op jit(solution)/shard_map/ppermute | solution.py:29
  52.4 10.3 %collective-permute-start.13 = (bf16[112,512]{1,0:T(8,128)(2,1)S(1)}, bf16[112,512]{1,0:T(8,128)(2,1)S(1)}, u32[]{:S(2)}, u32[]{:S(2)}) collective-permute-start(bf16[112,512]{1,0:T(8,128)(2,1)S(1)} %get-tuple-element.43), channel_id=1, source_target_pairs={{0,96},{32,0},{64,32},{96,64},{1,97},{33,1},{65,33},{97,65},{2,98}... | collective-permute-start | bytes 344072 | tf_op jit(solution)/shard_map/ppermute | solution.py:29
  52.4 13.3 %collective-permute-start.10 = (bf16[112,512]{1,0:T(8,128)(2,1)S(1)}, bf16[112,512]{1,0:T(8,128)(2,1)S(1)}, u32[]{:S(2)}, u32[]{:S(2)}) collective-permute-start(bf16[112,512]{1,0:T(8,128)(2,1)S(1)} %get-tuple-element.38), channel_id=1, source_target_pairs={{0,32},{32,64},{64,96},{96,0},{1,33},{33,65},{65,97},{97,1},{2,34}... | collective-permute-start | bytes 344072 | tf_op jit(solution)/shard_map/ppermute | solution.py:29
  56.6 10.1 %collective-permute-start.11 = (bf16[112,512]{1,0:T(8,128)(2,1)S(1)}, bf16[112,512]{1,0:T(8,128)(2,1)S(1)}, u32[]{:S(2)}, u32[]{:S(2)}) collective-permute-start(bf16[112,512]{1,0:T(8,128)(2,1)S(1)} %get-tuple-element.39), channel_id=1, source_target_pairs={{0,96},{32,0},{64,32},{96,64},{1,97},{33,1},{65,33},{97,65},{2,98}... | collective-permute-start | bytes 344072 | tf_op jit(solution)/shard_map/ppermute | solution.py:29
  62.8 6.4 %collective-permute-start.14 = (bf16[112,512]{1,0:T(8,128)(2,1)S(1)}, bf16[112,512]{1,0:T(8,128)(2,1)S(1)}, u32[]{:S(2)}, u32[]{:S(2)}) collective-permute-start(bf16[112,512]{1,0:T(8,128)(2,1)S(1)} %get-tuple-element.44), channel_id=1, source_target_pairs={{0,32},{32,64},{64,96},{96,0},{1,33},{33,65},{65,97},{97,1},{2,34}... | collective-permute-start | bytes 344072 | tf_op jit(solution)/shard_map/ppermute | solution.py:29
  63.5 8.5 %collective-permute-start.15 = (bf16[112,512]{1,0:T(8,128)(2,1)S(1)}, bf16[112,512]{1,0:T(8,128)(2,1)S(1)}, u32[]{:S(2)}, u32[]{:S(2)}) collective-permute-start(bf16[112,512]{1,0:T(8,128)(2,1)S(1)} %get-tuple-element.45), channel_id=1, source_target_pairs={{0,96},{32,0},{64,32},{96,64},{1,97},{33,1},{65,33},{97,65},{2,98}... | collective-permute-start | bytes 344072 | tf_op jit(solution)/shard_map/ppermute | solution.py:29
  73.2 9.2 %collective-permute-start.19 = (bf16[112,1024]{1,0:T(8,128)(2,1)S(1)}, bf16[112,1024]{1,0:T(8,128)(2,1)S(1)}, u32[]{:S(2)}, u32[]{:S(2)}) collective-permute-start(bf16[112,1024]{1,0:T(8,128)(2,1)S(1)} %get-tuple-element.46.refs_0_), channel_id=1, source_target_pairs={{0,2},{1,3},{2,0},{3,1},{4,6},{5,7},{6,4},{7,5},{8,10},{9,11},{10,... | collective-permute-start | bytes 688136 | tf_op jit(solution)/shard_map/ppermute | solution.py:29
  73.5 11.7 %collective-permute-start.16 = (bf16[112,1024]{1,0:T(8,128)(2,1)S(1)}, bf16[112,1024]{1,0:T(8,128)(2,1)S(1)}, u32[]{:S(2)}, u32[]{:S(2)}) collective-permute-start(bf16[112,1024]{1,0:T(8,128)(2,1)S(1)} %get-tuple-element.46.refs_0_), channel_id=1, source_target_pairs={{0,4},{4,0},{1,5},{5,1},{2,6},{6,2},{3,7},{7,3},{8,12},{12,8},{9,1... | collective-permute-start | bytes 688136 | tf_op jit(solution)/shard_map/ppermute | solution.py:25
  78.4 8.8 %collective-permute-start.22 = (bf16[112,1024]{1,0:T(8,128)(2,1)S(1)}, bf16[112,1024]{1,0:T(8,128)(2,1)S(1)}, u32[]{:S(2)}, u32[]{:S(2)}) collective-permute-start(bf16[112,1024]{1,0:T(8,128)(2,1)S(1)} %get-tuple-element.46.refs_0_), channel_id=1, source_target_pairs={{0,3},{1,0},{2,1},{3,2},{4,7},{5,4},{6,5},{7,6},{8,11},{9,8},{10,9... | collective-permute-start | bytes 688136 | tf_op jit(solution)/shard_map/ppermute | solution.py:29
  79.6 9.1 %collective-permute-start.21 = (bf16[112,1024]{1,0:T(8,128)(2,1)S(1)}, bf16[112,1024]{1,0:T(8,128)(2,1)S(1)}, u32[]{:S(2)}, u32[]{:S(2)}) collective-permute-start(bf16[112,1024]{1,0:T(8,128)(2,1)S(1)} %get-tuple-element.46.refs_0_), channel_id=1, source_target_pairs={{0,1},{1,2},{2,3},{3,0},{4,5},{5,6},{6,7},{7,4},{8,9},{9,10},{10,1... | collective-permute-start | bytes 688136 | tf_op jit(solution)/shard_map/ppermute | solution.py:29
  82.4 9.4 %collective-permute-start.20 = (bf16[112,1024]{1,0:T(8,128)(2,1)S(1)}, bf16[112,1024]{1,0:T(8,128)(2,1)S(1)}, u32[]{:S(2)}, u32[]{:S(2)}) collective-permute-start(bf16[112,1024]{1,0:T(8,128)(2,1)S(1)} %collective-permute-done.19.refs_4_), channel_id=1, source_target_pairs={{0,4},{4,0},{1,5},{5,1},{2,6},{6,2},{3,7},{7,3},{8,12},{12,8},{9,1... | collective-permute-start | bytes 688136 | tf_op jit(solution)/shard_map/ppermute | solution.py:25
  85.2 6.6 %collective-permute-start.18 = (bf16[112,1024]{1,0:T(8,128)(2,1)S(1)}, bf16[112,1024]{1,0:T(8,128)(2,1)S(1)}, u32[]{:S(2)}, u32[]{:S(2)}) collective-permute-start(bf16[112,1024]{1,0:T(8,128)(2,1)S(1)} %collective-permute-done.16.refs_1_), channel_id=1, source_target_pairs={{0,3},{1,0},{2,1},{3,2},{4,7},{5,4},{6,5},{7,6},{8,11},{9,8},{10,9... | collective-permute-start | bytes 688136 | tf_op jit(solution)/shard_map/ppermute | solution.py:29
  86.9 7.2 %collective-permute-start.17 = (bf16[112,1024]{1,0:T(8,128)(2,1)S(1)}, bf16[112,1024]{1,0:T(8,128)(2,1)S(1)}, u32[]{:S(2)}, u32[]{:S(2)}) collective-permute-start(bf16[112,1024]{1,0:T(8,128)(2,1)S(1)} %collective-permute-done.16.refs_1_), channel_id=1, source_target_pairs={{0,1},{1,2},{2,3},{3,0},{4,5},{5,6},{6,7},{7,4},{8,9},{9,10},{10,1... | collective-permute-start | bytes 688136 | tf_op jit(solution)/shard_map/ppermute | solution.py:29

commit v7 on v6

--- a/solution.py
+++ b/solution.py
@@ -15,6 +15,7 @@
 PARTS = YLO * ZL
 DP = ("ylo", "zh", "zl", "core")
 YHI, X = 2, 4
+CHUNKS = 2
 FSDP = ("yhi", "x")
 wide, narrow = jnp.float32, jnp.bfloat16
 VMEM = pl.BlockSpec(memory_space=pltpu.VMEM)
@@ -106,31 +107,46 @@
     down_out_ref[...] = (down_held_ref[...] + down_ref[...].astype(wide)).astype(narrow)
 
 
-def adam_kernel(own_ref, up_ref, down_ref, up_sum_ref, down_sum_ref, first_ref, second_ref, *outs):
+def moments(own_ref, up_ref, down_ref, up_sum_ref, down_sum_ref, first_ref, second_ref):
     left = down_ref[...].astype(wide) + up_sum_ref[...].astype(wide)
     right = up_ref[...].astype(wide) + down_sum_ref[...].astype(wide)
     gradient = own_ref[...] + jnp.concatenate([left, right], axis=1)
     first_new = 0.9 * first_ref[0] + 0.1 * gradient
     second_new = 0.999 * second_ref[0] + 0.001 * gradient * gradient
+    return first_new, second_new
+
+
+def direction_kernel(*refs):
+    first_new, second_new = moments(*refs[:7])
     root = jnp.sqrt(second_new / bias_second) + epsilon
-    outs[0][...] = (first_new / bias_first / root).astype(narrow)
-    outs[1][0] = first_new
-    outs[2][0] = second_new
+    refs[7][...] = (first_new / bias_first / root).astype(narrow)
+
+
+def moments_kernel(*refs):
+    refs[7][0], refs[8][0] = moments(*refs[:7])
 
 
 def back_kernel(count, first, place_ref, projector_ref, *refs):
     blocks = refs[:count]
     out_ref, held, sems = refs[-3:]
     stacked = jnp.concatenate([block[...] for block in blocks], axis=0)
-    held[...] = lax.dot_general(
-        stacked, projector_ref[...], (((1,), (1,)), ((), ())), preferred_element_type=wide
-    ).astype(narrow).reshape(held.shape)
-    copies = [
-        pltpu.make_async_copy(held.at[j], out_ref.at[place_ref[4 + first + j]], sems.at[j])
-        for j in range(count)
-    ]
-    for copy in copies:
-        copy.start()
+    chunk = projector_ref.shape[0] // CHUNKS
+    copies = []
+    for c in range(CHUNKS):
+        lanes = pl.ds(c * chunk, chunk)
+        value = lax.dot_general(
+            stacked, projector_ref[lanes, :], (((1,), (1,)), ((), ())), preferred_element_type=wide
+        )
+        held[:, :, lanes] = value.astype(narrow).reshape(held.shape[:2] + (chunk,))
+        for j in range(count):
+            copies.append(
+                pltpu.make_async_copy(
+                    held.at[j, :, lanes],
+                    out_ref.at[place_ref[4 + first + j], :, lanes],
+                    sems.at[j, c],
+                )
+            )
+            copies[-1].start()
     for copy in copies:
         copy.wait()
 
@@ -148,7 +164,7 @@
         input_output_aliases={} if out is None else {2 + count: 0},
         scratch_shapes=[
             pltpu.VMEM((count, cols, width), narrow),
-            pltpu.SemaphoreType.DMA((count,)),
+            pltpu.SemaphoreType.DMA((count, CHUNKS)),
         ],
         compiler_params=pltpu.CompilerParams(vmem_limit_bytes=16 * 2**20),
     )(place, projector, *blocks, *before)
@@ -223,14 +239,25 @@
     )(up_held, down_held, up_far, down_far)
     up_sum, down_sum = shift(up_sum, "zh", ZH, 1), shift(down_sum, "zh", ZH, 3)
     moment = jax.ShapeDtypeStruct((1,) + one, wide)
-    direction, first_new, second_new = pl.pallas_call(
-        adam_kernel,
-        out_shape=[jax.ShapeDtypeStruct(one, narrow), moment, moment],
+    sums = (own, up, down, up_sum, down_sum, first_moment, second_moment)
+    direction = pl.pallas_call(
+        direction_kernel,
+        out_shape=jax.ShapeDtypeStruct(one, narrow),
         in_specs=[VMEM] * 7,
-        out_specs=[VMEM] * 3,
-        compiler_params=pltpu.CompilerParams(vmem_limit_bytes=16 * 2**20),
-    )(own, up, down, up_sum, down_sum, first_moment, second_moment)
+        out_specs=VMEM,
+        compiler_params=pltpu.CompilerParams(vmem_limit_bytes=16 * 2**20),
+    )(*sums)
     directions = gathered(direction)
+    first_new, second_new = pl.pallas_call(
+        moments_kernel,
+        out_shape=[moment, moment],
+        in_specs=[VMEM] * 7,
+        out_specs=[VMEM] * 2,
+        compiler_params=pltpu.CompilerParams(vmem_limit_bytes=16 * 2**20),
+    )(*sums)
+    directions[0], first_new, second_new = lax.optimization_barrier(
+        (directions[0], first_new, second_new)
+    )
     weight_update = back(place, projector, directions[:5], 0, None)
     weight_update = back(place, projector, directions[5:], 5, weight_update)
     return (weight_update, first_new, second_new)

time: 96.8 us -> 96 us (level)
  transfers between devices with their start and end apart: 24 -> 24, of which waited for: 16 -> 16; matrix products, arithmetic and copies ran while one was open for 0% -> 0% of each run, Pallas kernels for 5% -> 6%
where the time goes in v7:
time: 96 us; the launch traced here: 95.8 us
  starting transfers between devices  42.5 us (44%)
  waiting for transfers between devices  37.8 us (39%)
  Pallas kernels  10.5 us (11%)
  matrix products  2.04 us (2%)
  local copies, waits for them, and re-layouts  1.91 us (2%)
  between operations  0.96 us (1%)
    ppermute x14, waiting for transfers between devices, shift(): lax.ppermute(value, axis, [(i, (i + step) % size) for i in range(size)])  21.4 us
    ppermute x14, starting transfers between devices, shift(): lax.ppermute(value, axis, [(i, (i + step) % size) for i in range(size)])  19.2 us
    ppermute x7, starting transfers between devices, swap(): return lax.ppermute(value, axis, [(0, 1), (1, 0)])  11.5 us
    all_to_all x1, waiting for transfers between devices, shards(): lax.all_to_all(jnp.broadcast_to(share, (YHI,) + share.shape[1:]).reshape(...  7.96 us
    all_to_all x1, starting transfers between devices, shards(): lax.all_to_all(jnp.broadcast_to(share, (YHI,) + share.shape[1:]).reshape(...  6.93 us
    ppermute x2, waiting for transfers between devices, exchanged(): lax.ppermute(over_both, ('ylo', 'zl'), [(i, 3 - i) for i in range(4)])  6.31 us
    pallas_call x2, Pallas kernels, back(): pl.pallas_call(functools.partial(back_kernel, count, first), out_shape=ja...  5.04 us
    ppermute x2, starting transfers between devices, exchanged(): lax.ppermute(over_both, ('ylo', 'zl'), [(i, 3 - i) for i in range(4)])  4.82 us
  transfers between devices with their start and end apart: 24, of which 16 were waited for; matrix products, arithmetic and copies ran while one was open for 0% of the time, Pallas kernels for 6%

profile of v7, /device:TPU:64, one launch (start us, length us, event | category | flops | bytes accessed | tf_op | source)
XLA Modules:
  0.0 95.8 jit_solution(6834100890418918523)
XLA Ops:
  0.6 0.0 copy-start
  0.7 0.9 copy-done
  1.6 2.0 %convolution_convert_fusion = bf16[128,1024]{1,0:T(8,128)(2,1)S(1)} fusion(bf16[128,1024]{1,0:T(8,128)(2,1)S(1)} %copy-done, bf16[1024,1024]{1,0:T(8,128)(2,1)} %projector_ref.3), kind=kOutput, calls=%fused_computation | convolution fusion | flops 268566528 | bytes 2621440 | tf_op jit(solution)/shard_map/dot_general | solution.py:197
  3.6 0.9 broadcast_in_dim.8
  4.5 6.9 %all-to-all-start = ((bf16[8,32,1024]{2,1,0:T(8,128)(2,1)}), bf16[8,32,1024]{2,1,0:T(8,128)(2,1)S(1)}, u32[]{:S(2)}, u32[]{:S(2)}) async-start(bf16[8,32,1024]{2,1,0:T(8,128)(2,1)} %bitcast.17), calls=%async_computation | async-start | bytes 1048576 | tf_op jit(solution)/shard_map/all_to_all | solution.py:200
  11.4 0.1 stack.82.place_ref._
  11.5 0.9 shard_map.76
  12.4 0.8 collective-permute-start.3
  13.2 1.9 %collective-permute-start.4 = (bf16[4,224,128]{2,1,0:T(8,128)(2,1)S(1)}, bf16[4,224,128]{2,1,0:T(8,128)(2,1)S(1)}, u32[]{:S(2)}, u32[]{:S(2)}) collective-permute-start(bf16[4,224,128]{2,1,0:T(8,128)(2,1)S(1)} %get-tuple-element.31), channel_id=1, source_target_pairs={{0,16},{16,0},{1,17},{17,1},{2,18},{18,2},{3,19},{19,3},{4,20},{20... | collective-permute-start | bytes 688136 | tf_op jit(solution)/shard_map/ppermute | solution.py:26
  15.1 8.0 %all-to-all-done = bf16[8,32,1024]{2,1,0:T(8,128)(2,1)S(1)} async-done(((bf16[8,32,1024]{2,1,0:T(8,128)(2,1)}), bf16[8,32,1024]{2,1,0:T(8,128)(2,1)S(1)}, u32[]{:S(2)}, u32[]{:S(2)}) %all-to-all-start) | async-done | bytes 524320 | tf_op jit(solution)/shard_map/all_to_all | solution.py:200
  23.1 0.1 reduce_sum.12
  23.1 2.1 %collective-permute-start.2 = (bf16[32,1024]{1,0:T(8,128)(2,1)S(1)}, bf16[32,1024]{1,0:T(8,128)(2,1)S(1)}, u32[]{:S(2)}, u32[]{:S(2)}) collective-permute-start(bf16[32,1024]{1,0:T(8,128)(2,1)S(1)} %reduce_sum.12), channel_id=1, source_target_pairs={{0,144},{16,128},{128,16},{144,0},{1,145},{17,129},{129,17},{145,1... | collective-permute-start | bytes 196616 | tf_op jit(solution)/shard_map/ppermute | solution.py:34
  25.3 0.1 collective-permute-start.1
  25.4 1.3 %collective-permute-start = (bf16[32,1024]{1,0:T(8,128)(2,1)S(1)}, bf16[32,1024]{1,0:T(8,128)(2,1)S(1)}, u32[]{:S(2)}, u32[]{:S(2)}) collective-permute-start(bf16[32,1024]{1,0:T(8,128)(2,1)S(1)} %reduce_sum.12), channel_id=1, source_target_pairs={{0,128},{128,0},{1,129},{129,1},{2,130},{130,2},{3,131},{131,3},{4... | collective-permute-start | bytes 196616 | tf_op jit(solution)/shard_map/ppermute | solution.py:26
  26.7 2.1 %collective-permute-done.2 = bf16[32,1024]{1,0:T(8,128)(2,1)S(1)} collective-permute-done((bf16[32,1024]{1,0:T(8,128)(2,1)S(1)}, bf16[32,1024]{1,0:T(8,128)(2,1)S(1)}, u32[]{:S(2)}, u32[]{:S(2)}) %collective-permute-start.2) | collective-permute-done | bytes 65568 | tf_op jit(solution)/shard_map/ppermute | solution.py:34
  28.8 0.7 collective-permute-done.1
  29.5 0.1 collective-permute-done
  29.7 0.0 collective-permute-done.3
  29.7 0.0 collective-permute-done.4
  29.7 1.4 %collective-permute-start.7 = (bf16[4,32,1024]{2,1,0:T(8,128)(2,1)S(1)}, bf16[4,32,1024]{2,1,0:T(8,128)(2,1)S(1)}, u32[]{:S(2)}, u32[]{:S(2)}) collective-permute-start(bf16[4,32,1024]{2,1,0:T(8,128)(2,1)S(1)} %pad_maximum_fusion.refs_0_), channel_id=1, source_target_pairs={{0,2},{1,3},{2,0},{3,1},{4,6},{5,7},{6,4},{7,5},{8,10},{9,11},{10,... | collective-permute-start | bytes 786440 | tf_op jit(solution)/shard_map/ppermute | solution.py:30
  31.1 2.2 %collective-permute-start.6 = (bf16[4,32,1024]{2,1,0:T(8,128)(2,1)S(1)}, bf16[4,32,1024]{2,1,0:T(8,128)(2,1)S(1)}, u32[]{:S(2)}, u32[]{:S(2)}) collective-permute-start(bf16[4,32,1024]{2,1,0:T(8,128)(2,1)S(1)} %pad_maximum_fusion.refs_0_), channel_id=1, source_target_pairs={{0,3},{1,0},{2,1},{3,2},{4,7},{5,4},{6,5},{7,6},{8,11},{9,8},{10,9... | collective-permute-start | bytes 786440 | tf_op jit(solution)/shard_map/ppermute | solution.py:30
  33.4 0.0 collective-permute-start.5
  33.4 2.7 %collective-permute-start.8 = (bf16[4,224,128]{2,1,0:T(8,128)(2,1)S(1)}, bf16[4,224,128]{2,1,0:T(8,128)(2,1)S(1)}, u32[]{:S(2)}, u32[]{:S(2)}) collective-permute-start(bf16[4,224,128]{2,1,0:T(8,128)(2,1)S(1)} %get-tuple-element.36), channel_id=1, source_target_pairs={{0,144},{16,128},{128,16},{144,0},{1,145},{17,129},{129,17},{145,1... | collective-permute-start | bytes 688136 | tf_op jit(solution)/shard_map/ppermute | solution.py:34
  36.1 4.2 %collective-permute-done.8 = bf16[4,224,128]{2,1,0:T(8,128)(2,1)S(1)} collective-permute-done((bf16[4,224,128]{2,1,0:T(8,128)(2,1)S(1)}, bf16[4,224,128]{2,1,0:T(8,128)(2,1)S(1)}, u32[]{:S(2)}, u32[]{:S(2)}) %collective-permute-start.8) | collective-permute-done | bytes 229408 | tf_op jit(solution)/shard_map/ppermute | solution.py:34
  40.3 0.3 collective-permute-done.7.refs_3_
  40.6 0.0 collective-permute-done.6.refs_2_
  40.6 3.4 %collective-permute-done.5.refs_1_ = bf16[4,32,1024]{2,1,0:T(8,128)(2,1)S(1)} collective-permute-done((bf16[4,32,1024]{2,1,0:T(8,128)(2,1)S(1)}, bf16[4,32,1024]{2,1,0:T(8,128)(2,1)S(1)}, u32[]{:S(2)}, u32[]{:S(2)}) %collective-permute-start.5) | collective-permute-done | bytes 262176 | tf_op jit(solution)/shard_map/ppermute | solution.py:30
  43.9 1.3 %shard_map.77 = (bf16[4,112,1024]{2,1,0:T(8,128)(2,1)S(1)}, bf16[4,4,32,1024]{3,2,1,0:T(8,128)(2,1)S(1)}) custom-call(s32[16]{0:T(128)S(1)} %stack.82.place_ref._, bf16[4,32,1024]{2,1,0:T(8,128)(2,1)S(1)} %pad_maximum_fusion.refs_0_, bf16[4,32,1024]{2,1,0:T(8,128)(2,1)S(1)} %collective-permute-done.5.refs_1_, ...), custom_call_target="tpu_custom_call" | custom-call | tf_op jit(solution)/shard_map/pallas_call | solution.py:221
  45.2 0.1 collective-permute-start.9
  45.3 1.2 %shard_map.78.mine_ref = f32[4,112,1024]{2,1,0:T(8,128)S(1)} custom-call(s32[16]{0:T(128)S(1)} %stack.82.place_ref._, bf16[4,4,32,1024]{3,2,1,0:T(8,128)(2,1)S(1)} %get-tuple-element.37.whole, bf16[4,2,112,128]{3,2,1,0:T(8,128)(2,1)S(1)} %bitcast.31, bf16[4,2,112,128]{3,2,1,0:T(8,128)(2,1)S(1)} %bitcast.33, bf16[4,2,112,128]{3,2,1,0:T(8,128)(2,1)S(1)} %bitcast.35, ...), custom_call_target="tpu_custom_call" | custom-call | tf_op jit(solution)/shard_map/pallas_call | solution.py:227
  46.5 0.0 copy-start.2
  46.5 0.0 copy-start.3
  46.5 1.2 %collective-permute-done.9.came_ref = bf16[4,112,1024]{2,1,0:T(8,128)(2,1)S(1)} collective-permute-done((bf16[4,112,1024]{2,1,0:T(8,128)(2,1)S(1)}, bf16[4,112,1024]{2,1,0:T(8,128)(2,1)S(1)}, u32[]{:S(2)}, u32[]{:S(2)}) %collective-permute-start.9) | collective-permute-done | bytes 917536 | tf_op jit(solution)/shard_map/ppermute | solution.py:26
  47.8 0.7 shard_map.79
  48.5 4.0 %collective-permute-start.12 = (bf16[112,512]{1,0:T(8,128)(2,1)S(1)}, bf16[112,512]{1,0:T(8,128)(2,1)S(1)}, u32[]{:S(2)}, u32[]{:S(2)}) collective-permute-start(bf16[112,512]{1,0:T(8,128)(2,1)S(1)} %get-tuple-element.44), channel_id=1, source_target_pairs={{0,32},{32,64},{64,96},{96,0},{1,33},{33,65},{65,97},{97,1},{2,34}... | collective-permute-start | bytes 344072 | tf_op jit(solution)/shard_map/ppermute | solution.py:30
  52.4 0.0 collective-permute-start.13
  52.4 4.1 %collective-permute-start.10 = (bf16[112,512]{1,0:T(8,128)(2,1)S(1)}, bf16[112,512]{1,0:T(8,128)(2,1)S(1)}, u32[]{:S(2)}, u32[]{:S(2)}) collective-permute-start(bf16[112,512]{1,0:T(8,128)(2,1)S(1)} %get-tuple-element.40), channel_id=1, source_target_pairs={{0,32},{32,64},{64,96},{96,0},{1,33},{33,65},{65,97},{97,1},{2,34}... | collective-permute-start | bytes 344072 | tf_op jit(solution)/shard_map/ppermute | solution.py:30
  56.6 0.0 collective-permute-start.11
  56.6 1.7 %collective-permute-done.12.up_ref = bf16[112,512]{1,0:T(8,128)(2,1)S(1)} collective-permute-done((bf16[112,512]{1,0:T(8,128)(2,1)S(1)}, bf16[112,512]{1,0:T(8,128)(2,1)S(1)}, u32[]{:S(2)}, u32[]{:S(2)}) %collective-permute-start.12) | collective-permute-done | bytes 114720 | tf_op jit(solution)/shard_map/ppermute | solution.py:30
  58.2 4.5 %collective-permute-done.13.down_ref = bf16[112,512]{1,0:T(8,128)(2,1)S(1)} collective-permute-done((bf16[112,512]{1,0:T(8,128)(2,1)S(1)}, bf16[112,512]{1,0:T(8,128)(2,1)S(1)}, u32[]{:S(2)}, u32[]{:S(2)}) %collective-permute-start.13) | collective-permute-done | bytes 114720 | tf_op jit(solution)/shard_map/ppermute | solution.py:30
  62.8 0.0 copy-start.1
  62.8 0.8 collective-permute-start.14
  63.5 2.2 %collective-permute-start.15 = (bf16[112,512]{1,0:T(8,128)(2,1)S(1)}, bf16[112,512]{1,0:T(8,128)(2,1)S(1)}, u32[]{:S(2)}, u32[]{:S(2)}) collective-permute-start(bf16[112,512]{1,0:T(8,128)(2,1)S(1)} %get-tuple-element.47), channel_id=1, source_target_pairs={{0,96},{32,0},{64,32},{96,64},{1,97},{33,1},{65,33},{97,65},{2,98}... | collective-permute-start | bytes 344072 | tf_op jit(solution)/shard_map/ppermute | solution.py:30
  65.8 0.0 collective-permute-done.10.refs_1_
  65.8 0.9 collective-permute-done.11.refs_2_
  66.6 2.5 %collective-permute-done.14.refs_3_ = bf16[112,512]{1,0:T(8,128)(2,1)S(1)} collective-permute-done((bf16[112,512]{1,0:T(8,128)(2,1)S(1)}, bf16[112,512]{1,0:T(8,128)(2,1)S(1)}, u32[]{:S(2)}, u32[]{:S(2)}) %collective-permute-start.14) | collective-permute-done | bytes 114720 | tf_op jit(solution)/shard_map/ppermute | solution.py:30
  69.2 2.9 %collective-permute-done.15.refs_4_ = bf16[112,512]{1,0:T(8,128)(2,1)S(1)} collective-permute-done((bf16[112,512]{1,0:T(8,128)(2,1)S(1)}, bf16[112,512]{1,0:T(8,128)(2,1)S(1)}, u32[]{:S(2)}, u32[]{:S(2)}) %collective-permute-start.15) | collective-permute-done | bytes 114720 | tf_op jit(solution)/shard_map/ppermute | solution.py:30
  72.0 0.4 shard_map.81.refs_0_
  72.4 0.4 collective-permute-start.19
  72.8 4.9 %collective-permute-start.16 = (bf16[112,1024]{1,0:T(8,128)(2,1)S(1)}, bf16[112,1024]{1,0:T(8,128)(2,1)S(1)}, u32[]{:S(2)}, u32[]{:S(2)}) collective-permute-start(bf16[112,1024]{1,0:T(8,128)(2,1)S(1)} %shard_map.81.refs_0_), channel_id=1, source_target_pairs={{0,4},{4,0},{1,5},{5,1},{2,6},{6,2},{3,7},{7,3},{8,12},{12,8},{9,1... | collective-permute-start | bytes 688136 | tf_op jit(solution)/shard_map/ppermute | solution.py:26
  77.7 1.2 %collective-permute-start.22 = (bf16[112,1024]{1,0:T(8,128)(2,1)S(1)}, bf16[112,1024]{1,0:T(8,128)(2,1)S(1)}, u32[]{:S(2)}, u32[]{:S(2)}) collective-permute-start(bf16[112,1024]{1,0:T(8,128)(2,1)S(1)} %shard_map.81.refs_0_), channel_id=1, source_target_pairs={{0,3},{1,0},{2,1},{3,2},{4,7},{5,4},{6,5},{7,6},{8,11},{9,8},{10,9... | collective-permute-start | bytes 688136 | tf_op jit(solution)/shard_map/ppermute | solution.py:30
  79.0 0.8 collective-permute-start.21
  79.8 2.2 %collective-permute-done.19.refs_4_ = bf16[112,1024]{1,0:T(8,128)(2,1)S(1)} collective-permute-done((bf16[112,1024]{1,0:T(8,128)(2,1)S(1)}, bf16[112,1024]{1,0:T(8,128)(2,1)S(1)}, u32[]{:S(2)}, u32[]{:S(2)}) %collective-permute-start.19) | collective-permute-done | bytes 229408 | tf_op jit(solution)/shard_map/ppermute | solution.py:30
  81.9 2.4 %collective-permute-start.20 = (bf16[112,1024]{1,0:T(8,128)(2,1)S(1)}, bf16[112,1024]{1,0:T(8,128)(2,1)S(1)}, u32[]{:S(2)}, u32[]{:S(2)}) collective-permute-start(bf16[112,1024]{1,0:T(8,128)(2,1)S(1)} %collective-permute-done.19.refs_4_), channel_id=1, source_target_pairs={{0,4},{4,0},{1,5},{5,1},{2,6},{6,2},{3,7},{7,3},{8,12},{12,8},{9,1... | collective-permute-start | bytes 688136 | tf_op jit(solution)/shard_map/ppermute | solution.py:26
  84.3 0.0 collective-permute-done.16.refs_1_
  84.4 1.9 %collective-permute-start.18 = (bf16[112,1024]{1,0:T(8,128)(2,1)S(1)}, bf16[112,1024]{1,0:T(8,128)(2,1)S(1)}, u32[]{:S(2)}, u32[]{:S(2)}) collective-permute-start(bf16[112,1024]{1,0:T(8,128)(2,1)S(1)} %collective-permute-done.16.refs_1_), channel_id=1, source_target_pairs={{0,3},{1,0},{2,1},{3,2},{4,7},{5,4},{6,5},{7,6},{8,11},{9,8},{10,9... | collective-permute-start | bytes 688136 | tf_op jit(solution)/shard_map/ppermute | solution.py:30
  86.2 0.2 collective-permute-start.17
  86.4 1.0 %shard_map.82 = (f32[1,112,1024]{2,1,0:T(8,128)}, f32[1,112,1024]{2,1,0:T(8,128)}) custom-call(f32[112,1024]{1,0:T(8,128)S(1)} %get-tuple-element.39.refs_0_, bf16[112,512]{1,0:T(8,128)(2,1)S(1)} %collective-permute-done.10.refs_1_, bf16[112,512]{1,0:T(8,128)(2,1)S(1)} %collective-permute-done.11.refs_2_, ...), custom_call_target="tpu_custom_call" | custom-call | tf_op jit(solution)/shard_map/pallas_call | solution.py:251
  87.4 0.7 collective-permute-done.21.refs_2_
  88.1 2.8 %shard_map.83.refs_3_ = bf16[8,112,1024]{2,1,0:T(8,128)(2,1)} custom-call(s32[16]{0:T(128)S(1)} %stack.82.place_ref._, bf16[1024,1024]{1,0:T(8,128)(2,1)S(1)} %copy-done.1, bf16[112,1024]{1,0:T(8,128)(2,1)S(1)} %shard_map.81.refs_0_, bf16[112,1024]{1,0:T(8,128)(2,1)S(1)} %collective-permute-done.16.refs_1_, ...), custom_call_target="tpu_custom_call" | custom-call | tf_op jit(solution)/shard_map/pallas_call | solution.py:159
  90.9 0.0 collective-permute-done.20.refs_2_
  90.9 0.0 collective-permute-done.18.refs_1_
  91.0 2.5 %collective-permute-done.17.refs_0_ = bf16[112,1024]{1,0:T(8,128)(2,1)S(1)} collective-permute-done((bf16[112,1024]{1,0:T(8,128)(2,1)S(1)}, bf16[112,1024]{1,0:T(8,128)(2,1)S(1)}, u32[]{:S(2)}, u32[]{:S(2)}) %collective-permute-start.17) | collective-permute-done | bytes 229408 | tf_op jit(solution)/shard_map/ppermute | solution.py:30
  93.4 2.2 %shard_map.84 = bf16[8,112,1024]{2,1,0:T(8,128)(2,1)} custom-call(s32[16]{0:T(128)S(1)} %stack.82.place_ref._, bf16[1024,1024]{1,0:T(8,128)(2,1)S(1)} %copy-done.1, bf16[112,1024]{1,0:T(8,128)(2,1)S(1)} %collective-permute-done.17.refs_0_, bf16[112,1024]{1,0:T(8,128)(2,1)S(1)} %collective-permute-done.18.refs_1_, ...), custom_call_target="tpu_custom_call", output_to_operand_aliasing={{}: (5, {})} | custom-call | tf_op jit(solution)/shard_map/pallas_call | solution.py:159
  (8 shorter events, 0.1 us)
Async XLA Ops:
  0.6 1.0 copy-start
  0.6 10.9 %copy-start.4 = (bf16[128,1,3584]{2,0,1:T(8,128)(2,1)S(1)}, bf16[128,1,3584]{2,0,1:T(8,128)(2,1)}, u32[]{:S(2)}) copy-start(bf16[128,1,3584]{2,0,1:T(8,128)(2,1)} %param.7) | copy-start | bytes 2752516
  4.5 18.6 %all-to-all-start = ((bf16[8,32,1024]{2,1,0:T(8,128)(2,1)}), bf16[8,32,1024]{2,1,0:T(8,128)(2,1)S(1)}, u32[]{:S(2)}, u32[]{:S(2)}) async-start(bf16[8,32,1024]{2,1,0:T(8,128)(2,1)} %bitcast.17), calls=%async_computation | async-start | bytes 1048576 | tf_op jit(solution)/shard_map/all_to_all | solution.py:200
  12.4 17.3 %collective-permute-start.3 = (bf16[4,224,128]{2,1,0:T(8,128)(2,1)S(1)}, bf16[4,224,128]{2,1,0:T(8,128)(2,1)S(1)}, u32[]{:S(2)}, u32[]{:S(2)}) collective-permute-start(bf16[4,224,128]{2,1,0:T(8,128)(2,1)S(1)} %get-tuple-element.30), channel_id=1, source_target_pairs={{0,128},{128,0},{1,129},{129,1},{2,130},{130,2},{3,131},{131,3},{4... | collective-permute-start | bytes 688136 | tf_op jit(solution)/shard_map/ppermute | solution.py:26
  13.2 16.5 %collective-permute-start.4 = (bf16[4,224,128]{2,1,0:T(8,128)(2,1)S(1)}, bf16[4,224,128]{2,1,0:T(8,128)(2,1)S(1)}, u32[]{:S(2)}, u32[]{:S(2)}) collective-permute-start(bf16[4,224,128]{2,1,0:T(8,128)(2,1)S(1)} %get-tuple-element.31), channel_id=1, source_target_pairs={{0,16},{16,0},{1,17},{17,1},{2,18},{18,2},{3,19},{19,3},{4,20},{20... | collective-permute-start | bytes 688136 | tf_op jit(solution)/shard_map/ppermute | solution.py:26
  23.1 5.7 %collective-permute-start.2 = (bf16[32,1024]{1,0:T(8,128)(2,1)S(1)}, bf16[32,1024]{1,0:T(8,128)(2,1)S(1)}, u32[]{:S(2)}, u32[]{:S(2)}) collective-permute-start(bf16[32,1024]{1,0:T(8,128)(2,1)S(1)} %reduce_sum.12), channel_id=1, source_target_pairs={{0,144},{16,128},{128,16},{144,0},{1,145},{17,129},{129,17},{145,1... | collective-permute-start | bytes 196616 | tf_op jit(solution)/shard_map/ppermute | solution.py:34
  25.3 4.3 %collective-permute-start.1 = (bf16[32,1024]{1,0:T(8,128)(2,1)S(1)}, bf16[32,1024]{1,0:T(8,128)(2,1)S(1)}, u32[]{:S(2)}, u32[]{:S(2)}) collective-permute-start(bf16[32,1024]{1,0:T(8,128)(2,1)S(1)} %reduce_sum.12), channel_id=1, source_target_pairs={{0,16},{16,0},{1,17},{17,1},{2,18},{18,2},{3,19},{19,3},{4,20},{20... | collective-permute-start | bytes 196616 | tf_op jit(solution)/shard_map/ppermute | solution.py:26
  25.4 4.3 %collective-permute-start = (bf16[32,1024]{1,0:T(8,128)(2,1)S(1)}, bf16[32,1024]{1,0:T(8,128)(2,1)S(1)}, u32[]{:S(2)}, u32[]{:S(2)}) collective-permute-start(bf16[32,1024]{1,0:T(8,128)(2,1)S(1)} %reduce_sum.12), channel_id=1, source_target_pairs={{0,128},{128,0},{1,129},{129,1},{2,130},{130,2},{3,131},{131,3},{4... | collective-permute-start | bytes 196616 | tf_op jit(solution)/shard_map/ppermute | solution.py:26
  29.7 10.9 %collective-permute-start.7 = (bf16[4,32,1024]{2,1,0:T(8,128)(2,1)S(1)}, bf16[4,32,1024]{2,1,0:T(8,128)(2,1)S(1)}, u32[]{:S(2)}, u32[]{:S(2)}) collective-permute-start(bf16[4,32,1024]{2,1,0:T(8,128)(2,1)S(1)} %pad_maximum_fusion.refs_0_), channel_id=1, source_target_pairs={{0,2},{1,3},{2,0},{3,1},{4,6},{5,7},{6,4},{7,5},{8,10},{9,11},{10,... | collective-permute-start | bytes 786440 | tf_op jit(solution)/shard_map/ppermute | solution.py:30
  31.1 9.4 %collective-permute-start.6 = (bf16[4,32,1024]{2,1,0:T(8,128)(2,1)S(1)}, bf16[4,32,1024]{2,1,0:T(8,128)(2,1)S(1)}, u32[]{:S(2)}, u32[]{:S(2)}) collective-permute-start(bf16[4,32,1024]{2,1,0:T(8,128)(2,1)S(1)} %pad_maximum_fusion.refs_0_), channel_id=1, source_target_pairs={{0,3},{1,0},{2,1},{3,2},{4,7},{5,4},{6,5},{7,6},{8,11},{9,8},{10,9... | collective-permute-start | bytes 786440 | tf_op jit(solution)/shard_map/ppermute | solution.py:30
  33.4 10.6 %collective-permute-start.5 = (bf16[4,32,1024]{2,1,0:T(8,128)(2,1)S(1)}, bf16[4,32,1024]{2,1,0:T(8,128)(2,1)S(1)}, u32[]{:S(2)}, u32[]{:S(2)}) collective-permute-start(bf16[4,32,1024]{2,1,0:T(8,128)(2,1)S(1)} %pad_maximum_fusion.refs_0_), channel_id=1, source_target_pairs={{0,1},{1,2},{2,3},{3,0},{4,5},{5,6},{6,7},{7,4},{8,9},{9,10},{10,1... | collective-permute-start | bytes 786440 | tf_op jit(solution)/shard_map/ppermute | solution.py:30
  33.4 6.9 %collective-permute-start.8 = (bf16[4,224,128]{2,1,0:T(8,128)(2,1)S(1)}, bf16[4,224,128]{2,1,0:T(8,128)(2,1)S(1)}, u32[]{:S(2)}, u32[]{:S(2)}) collective-permute-start(bf16[4,224,128]{2,1,0:T(8,128)(2,1)S(1)} %get-tuple-element.36), channel_id=1, source_target_pairs={{0,144},{16,128},{128,16},{144,0},{1,145},{17,129},{129,17},{145,1... | collective-permute-start | bytes 688136 | tf_op jit(solution)/shard_map/ppermute | solution.py:34
  45.2 2.6 %collective-permute-start.9 = (bf16[4,112,1024]{2,1,0:T(8,128)(2,1)S(1)}, bf16[4,112,1024]{2,1,0:T(8,128)(2,1)S(1)}, u32[]{:S(2)}, u32[]{:S(2)}) collective-permute-start(bf16[4,112,1024]{2,1,0:T(8,128)(2,1)S(1)} %get-tuple-element.38), channel_id=1, source_target_pairs={{0,8},{8,0},{1,9},{9,1},{2,10},{10,2},{3,11},{11,3},{4,12},{12,4},... | collective-permute-start | bytes 2752520 | tf_op jit(solution)/shard_map/ppermute | solution.py:26
  46.5 25.5 %copy-start.2 = (f32[1,112,1024]{2,1,0:T(8,128)S(1)}, f32[1,112,1024]{2,1,0:T(8,128)}, u32[]{:S(2)}) copy-start(f32[1,112,1024]{2,1,0:T(8,128)} %refs_5_.3) | copy-start | bytes 1376260
  46.5 25.5 %copy-start.3 = (f32[1,112,1024]{2,1,0:T(8,128)S(1)}, f32[1,112,1024]{2,1,0:T(8,128)}, u32[]{:S(2)}) copy-start(f32[1,112,1024]{2,1,0:T(8,128)} %refs_6_.3) | copy-start | bytes 1376260
  48.5 9.8 %collective-permute-start.12 = (bf16[112,512]{1,0:T(8,128)(2,1)S(1)}, bf16[112,512]{1,0:T(8,128)(2,1)S(1)}, u32[]{:S(2)}, u32[]{:S(2)}) collective-permute-start(bf16[112,512]{1,0:T(8,128)(2,1)S(1)} %get-tuple-element.44), channel_id=1, source_target_pairs={{0,32},{32,64},{64,96},{96,0},{1,33},{33,65},{65,97},{97,1},{2,34}... | collective-permute-start | bytes 344072 | tf_op jit(solution)/shard_map/ppermute | solution.py:30
  52.4 10.3 %collective-permute-start.13 = (bf16[112,512]{1,0:T(8,128)(2,1)S(1)}, bf16[112,512]{1,0:T(8,128)(2,1)S(1)}, u32[]{:S(2)}, u32[]{:S(2)}) collective-permute-start(bf16[112,512]{1,0:T(8,128)(2,1)S(1)} %get-tuple-element.45), channel_id=1, source_target_pairs={{0,96},{32,0},{64,32},{96,64},{1,97},{33,1},{65,33},{97,65},{2,98}... | collective-permute-start | bytes 344072 | tf_op jit(solution)/shard_map/ppermute | solution.py:30
  52.4 13.4 %collective-permute-start.10 = (bf16[112,512]{1,0:T(8,128)(2,1)S(1)}, bf16[112,512]{1,0:T(8,128)(2,1)S(1)}, u32[]{:S(2)}, u32[]{:S(2)}) collective-permute-start(bf16[112,512]{1,0:T(8,128)(2,1)S(1)} %get-tuple-element.40), channel_id=1, source_target_pairs={{0,32},{32,64},{64,96},{96,0},{1,33},{33,65},{65,97},{97,1},{2,34}... | collective-permute-start | bytes 344072 | tf_op jit(solution)/shard_map/ppermute | solution.py:30
  56.6 10.1 %collective-permute-start.11 = (bf16[112,512]{1,0:T(8,128)(2,1)S(1)}, bf16[112,512]{1,0:T(8,128)(2,1)S(1)}, u32[]{:S(2)}, u32[]{:S(2)}) collective-permute-start(bf16[112,512]{1,0:T(8,128)(2,1)S(1)} %get-tuple-element.41), channel_id=1, source_target_pairs={{0,96},{32,0},{64,32},{96,64},{1,97},{33,1},{65,33},{97,65},{2,98}... | collective-permute-start | bytes 344072 | tf_op jit(solution)/shard_map/ppermute | solution.py:30
  62.8 25.4 %copy-start.1 = (bf16[1024,1024]{1,0:T(8,128)(2,1)S(1)}, bf16[1024,1024]{1,0:T(8,128)(2,1)}, u32[]{:S(2)}) copy-start(bf16[1024,1024]{1,0:T(8,128)(2,1)} %projector_ref.3) | copy-start | bytes 6291460
  62.8 6.4 %collective-permute-start.14 = (bf16[112,512]{1,0:T(8,128)(2,1)S(1)}, bf16[112,512]{1,0:T(8,128)(2,1)S(1)}, u32[]{:S(2)}, u32[]{:S(2)}) collective-permute-start(bf16[112,512]{1,0:T(8,128)(2,1)S(1)} %get-tuple-element.46), channel_id=1, source_target_pairs={{0,32},{32,64},{64,96},{96,0},{1,33},{33,65},{65,97},{97,1},{2,34}... | collective-permute-start | bytes 344072 | tf_op jit(solution)/shard_map/ppermute | solution.py:30
  63.5 8.5 %collective-permute-start.15 = (bf16[112,512]{1,0:T(8,128)(2,1)S(1)}, bf16[112,512]{1,0:T(8,128)(2,1)S(1)}, u32[]{:S(2)}, u32[]{:S(2)}) collective-permute-start(bf16[112,512]{1,0:T(8,128)(2,1)S(1)} %get-tuple-element.47), channel_id=1, source_target_pairs={{0,96},{32,0},{64,32},{96,64},{1,97},{33,1},{65,33},{97,65},{2,98}... | collective-permute-start | bytes 344072 | tf_op jit(solution)/shard_map/ppermute | solution.py:30
  72.4 9.5 %collective-permute-start.19 = (bf16[112,1024]{1,0:T(8,128)(2,1)S(1)}, bf16[112,1024]{1,0:T(8,128)(2,1)S(1)}, u32[]{:S(2)}, u32[]{:S(2)}) collective-permute-start(bf16[112,1024]{1,0:T(8,128)(2,1)S(1)} %shard_map.81.refs_0_), channel_id=1, source_target_pairs={{0,2},{1,3},{2,0},{3,1},{4,6},{5,7},{6,4},{7,5},{8,10},{9,11},{10,... | collective-permute-start | bytes 688136 | tf_op jit(solution)/shard_map/ppermute | solution.py:30
  72.8 11.5 %collective-permute-start.16 = (bf16[112,1024]{1,0:T(8,128)(2,1)S(1)}, bf16[112,1024]{1,0:T(8,128)(2,1)S(1)}, u32[]{:S(2)}, u32[]{:S(2)}) collective-permute-start(bf16[112,1024]{1,0:T(8,128)(2,1)S(1)} %shard_map.81.refs_0_), channel_id=1, source_target_pairs={{0,4},{4,0},{1,5},{5,1},{2,6},{6,2},{3,7},{7,3},{8,12},{12,8},{9,1... | collective-permute-start | bytes 688136 | tf_op jit(solution)/shard_map/ppermute | solution.py:26
  77.7 9.7 %collective-permute-start.22 = (bf16[112,1024]{1,0:T(8,128)(2,1)S(1)}, bf16[112,1024]{1,0:T(8,128)(2,1)S(1)}, u32[]{:S(2)}, u32[]{:S(2)}) collective-permute-start(bf16[112,1024]{1,0:T(8,128)(2,1)S(1)} %shard_map.81.refs_0_), channel_id=1, source_target_pairs={{0,3},{1,0},{2,1},{3,2},{4,7},{5,4},{6,5},{7,6},{8,11},{9,8},{10,9... | collective-permute-start | bytes 688136 | tf_op jit(solution)/shard_map/ppermute | solution.py:30
  79.0 9.1 %collective-permute-start.21 = (bf16[112,1024]{1,0:T(8,128)(2,1)S(1)}, bf16[112,1024]{1,0:T(8,128)(2,1)S(1)}, u32[]{:S(2)}, u32[]{:S(2)}) collective-permute-start(bf16[112,1024]{1,0:T(8,128)(2,1)S(1)} %shard_map.81.refs_0_), channel_id=1, source_target_pairs={{0,1},{1,2},{2,3},{3,0},{4,5},{5,6},{6,7},{7,4},{8,9},{9,10},{10,1... | collective-permute-start | bytes 688136 | tf_op jit(solution)/shard_map/ppermute | solution.py:30
  81.9 9.0 %collective-permute-start.20 = (bf16[112,1024]{1,0:T(8,128)(2,1)S(1)}, bf16[112,1024]{1,0:T(8,128)(2,1)S(1)}, u32[]{:S(2)}, u32[]{:S(2)}) collective-permute-start(bf16[112,1024]{1,0:T(8,128)(2,1)S(1)} %collective-permute-done.19.refs_4_), channel_id=1, source_target_pairs={{0,4},{4,0},{1,5},{5,1},{2,6},{6,2},{3,7},{7,3},{8,12},{12,8},{9,1... | collective-permute-start | bytes 688136 | tf_op jit(solution)/shard_map/ppermute | solution.py:26
  84.4 6.6 %collective-permute-start.18 = (bf16[112,1024]{1,0:T(8,128)(2,1)S(1)}, bf16[112,1024]{1,0:T(8,128)(2,1)S(1)}, u32[]{:S(2)}, u32[]{:S(2)}) collective-permute-start(bf16[112,1024]{1,0:T(8,128)(2,1)S(1)} %collective-permute-done.16.refs_1_), channel_id=1, source_target_pairs={{0,3},{1,0},{2,1},{3,2},{4,7},{5,4},{6,5},{7,6},{8,11},{9,8},{10,9... | collective-permute-start | bytes 688136 | tf_op jit(solution)/shard_map/ppermute | solution.py:30
  86.2 7.2 %collective-permute-start.17 = (bf16[112,1024]{1,0:T(8,128)(2,1)S(1)}, bf16[112,1024]{1,0:T(8,128)(2,1)S(1)}, u32[]{:S(2)}, u32[]{:S(2)}) collective-permute-start(bf16[112,1024]{1,0:T(8,128)(2,1)S(1)} %collective-permute-done.16.refs_1_), channel_id=1, source_target_pairs={{0,1},{1,2},{2,3},{3,0},{4,5},{5,6},{6,7},{7,4},{8,9},{9,10},{10,1... | collective-permute-start | bytes 688136 | tf_op jit(solution)/shard_map/ppermute | solution.py:30

commit v8 on v7

--- a/solution.py
+++ b/solution.py
@@ -84,46 +84,48 @@
     out_ref[...] = product(place_ref, place_ref[3], grads, whole)
 
 
-def split_kernel(_, mine_ref, came_ref, *outs):
-    own_ref, up_far_ref, down_far_ref, up_ref, down_ref, up_held_ref, down_held_ref = outs
-    lanes = own_ref.shape[-1] // 2
-    left, right = slice(0, lanes), slice(lanes, 2 * lanes)
-
-    def total(step, half):
-        return mine_ref[step, :, half] + came_ref[step, :, half].astype(wide)
-
-    own_ref[:, left] = total(0, left)
-    own_ref[:, right] = total(0, right)
-    up_far_ref[...] = total(2, left).astype(narrow)
-    down_far_ref[...] = total(2, right).astype(narrow)
-    up_ref[...] = total(1, right).astype(narrow)
-    down_ref[...] = total(3, left).astype(narrow)
-    up_held_ref[...] = total(1, left)
-    down_held_ref[...] = total(3, right)
-
-
-def relay_kernel(up_held_ref, down_held_ref, up_ref, down_ref, up_out_ref, down_out_ref):
-    up_out_ref[...] = (up_held_ref[...] + up_ref[...].astype(wide)).astype(narrow)
-    down_out_ref[...] = (down_held_ref[...] + down_ref[...].astype(wide)).astype(narrow)
-
-
-def moments(own_ref, up_ref, down_ref, up_sum_ref, down_sum_ref, first_ref, second_ref):
+def total(mine_ref, came_ref, step, half):
+    return mine_ref[step, :, half] + came_ref[step, :, half].astype(wide)
+
+
+def halves_of(mine_ref):
+    lanes = mine_ref.shape[-1] // 2
+    return slice(0, lanes), slice(lanes, 2 * lanes)
+
+
+def split_kernel(_, mine_ref, came_ref, up_far_ref, down_far_ref, up_ref, down_ref):
+    left, right = halves_of(mine_ref)
+    up_far_ref[...] = total(mine_ref, came_ref, 2, left).astype(narrow)
+    down_far_ref[...] = total(mine_ref, came_ref, 2, right).astype(narrow)
+    up_ref[...] = total(mine_ref, came_ref, 1, right).astype(narrow)
+    down_ref[...] = total(mine_ref, came_ref, 3, left).astype(narrow)
+
+
+def relay_kernel(mine_ref, came_ref, up_ref, down_ref, up_out_ref, down_out_ref):
+    left, right = halves_of(mine_ref)
+    up_out_ref[...] = (total(mine_ref, came_ref, 1, left) + up_ref[...].astype(wide)).astype(narrow)
+    down_sum = total(mine_ref, came_ref, 3, right) + down_ref[...].astype(wide)
+    down_out_ref[...] = down_sum.astype(narrow)
+
+
+def moments(mine_ref, came_ref, up_ref, down_ref, up_sum_ref, down_sum_ref, first_ref, second_ref):
     left = down_ref[...].astype(wide) + up_sum_ref[...].astype(wide)
     right = up_ref[...].astype(wide) + down_sum_ref[...].astype(wide)
-    gradient = own_ref[...] + jnp.concatenate([left, right], axis=1)
+    own = total(mine_ref, came_ref, 0, slice(None))
+    gradient = own + jnp.concatenate([left, right], axis=1)
     first_new = 0.9 * first_ref[0] + 0.1 * gradient
     second_new = 0.999 * second_ref[0] + 0.001 * gradient * gradient
     return first_new, second_new
 
 
 def direction_kernel(*refs):
-    first_new, second_new = moments(*refs[:7])
+    first_new, second_new = moments(*refs[:8])
     root = jnp.sqrt(second_new / bias_second) + epsilon
-    refs[7][...] = (first_new / bias_first / root).astype(narrow)
+    refs[8][...] = (first_new / bias_first / root).astype(narrow)
 
 
 def moments_kernel(*refs):
-    refs[7][0], refs[8][0] = moments(*refs[:7])
+    refs[8][0], refs[9][0] = moments(*refs[:8])
 
 
 def back_kernel(count, first, place_ref, projector_ref, *refs):
@@ -225,9 +227,7 @@
     )(place, *projected, *grads)
     came = swap(sent, "core")
     (mine,) = local(keep_kernel, [((ZH,) + one, wide)], 1 + PARTS)(place, whole, *grads)
-    own, up_far, down_far, up, down, up_held, down_held = local(
-        split_kernel, [(one, wide)] + [(part, narrow)] * 4 + [(part, wide)] * 2, 2
-    )(place, mine, came)
+    up_far, down_far, up, down = local(split_kernel, [(part, narrow)] * 4, 2)(place, mine, came)
     up_far, down_far = shift(up_far, "zh", ZH, 1), shift(down_far, "zh", ZH, 3)
     up, down = shift(up, "zh", ZH, 1), shift(down, "zh", ZH, 3)
     up_sum, down_sum = pl.pallas_call(
@@ -236,14 +236,14 @@
         in_specs=[VMEM] * 4,
         out_specs=[VMEM] * 2,
         compiler_params=pltpu.CompilerParams(vmem_limit_bytes=16 * 2**20),
-    )(up_held, down_held, up_far, down_far)
+    )(mine, came, up_far, down_far)
     up_sum, down_sum = shift(up_sum, "zh", ZH, 1), shift(down_sum, "zh", ZH, 3)
     moment = jax.ShapeDtypeStruct((1,) + one, wide)
-    sums = (own, up, down, up_sum, down_sum, first_moment, second_moment)
+    sums = (mine, came, up, down, up_sum, down_sum, first_moment, second_moment)
     direction = pl.pallas_call(
         direction_kernel,
         out_shape=jax.ShapeDtypeStruct(one, narrow),
-        in_specs=[VMEM] * 7,
+        in_specs=[VMEM] * 8,
         out_specs=VMEM,
         compiler_params=pltpu.CompilerParams(vmem_limit_bytes=16 * 2**20),
     )(*sums)
@@ -251,7 +251,7 @@
     first_new, second_new = pl.pallas_call(
         moments_kernel,
         out_shape=[moment, moment],
-        in_specs=[VMEM] * 7,
+        in_specs=[VMEM] * 8,
         out_specs=[VMEM] * 2,
         compiler_params=pltpu.CompilerParams(vmem_limit_bytes=16 * 2**20),
     )(*sums)

time: 96 us -> 96 us (level)
  no operation moved by 1% of the time
where the time goes in v8:
time: 96 us; the launch traced here: 95.8 us
  starting transfers between devices  42.4 us (44%)
  waiting for transfers between devices  37.9 us (39%)
  Pallas kernels  10.5 us (11%)
  matrix products  2.04 us (2%)
  local copies, waits for them, and re-layouts  1.91 us (2%)
  between operations  0.96 us (1%)
    ppermute x14, waiting for transfers between devices, shift(): lax.ppermute(value, axis, [(i, (i + step) % size) for i in range(size)])  21.5 us
    ppermute x14, starting transfers between devices, shift(): lax.ppermute(value, axis, [(i, (i + step) % size) for i in range(size)])  19.2 us
    ppermute x7, starting transfers between devices, swap(): return lax.ppermute(value, axis, [(0, 1), (1, 0)])  11.4 us
    all_to_all x1, waiting for transfers between devices, shards(): lax.all_to_all(jnp.broadcast_to(share, (YHI,) + share.shape[1:]).reshape(...  7.96 us
    all_to_all x1, starting transfers between devices, shards(): lax.all_to_all(jnp.broadcast_to(share, (YHI,) + share.shape[1:]).reshape(...  6.93 us
    ppermute x2, waiting for transfers between devices, exchanged(): lax.ppermute(over_both, ('ylo', 'zl'), [(i, 3 - i) for i in range(4)])  6.31 us
    pallas_call x2, Pallas kernels, back(): pl.pallas_call(functools.partial(back_kernel, count, first), out_shape=ja...  5.03 us
    ppermute x2, starting transfers between devices, exchanged(): lax.ppermute(over_both, ('ylo', 'zl'), [(i, 3 - i) for i in range(4)])  4.82 us
  transfers between devices with their start and end apart: 24, of which 16 were waited for; matrix products, arithmetic and copies ran while one was open for 0% of the time, Pallas kernels for 6%

profile of v8, /device:TPU:64, one launch (start us, length us, event | category | flops | bytes accessed | tf_op | source)
XLA Modules:
  0.0 95.8 jit_solution(4267022057687176767)
XLA Ops:
  0.6 0.0 copy-start
  0.7 0.9 copy-done
  1.6 2.0 %convolution_convert_fusion = bf16[128,1024]{1,0:T(8,128)(2,1)S(1)} fusion(bf16[128,1024]{1,0:T(8,128)(2,1)S(1)} %copy-done, bf16[1024,1024]{1,0:T(8,128)(2,1)} %projector_ref.3), kind=kOutput, calls=%fused_computation | convolution fusion | flops 268566528 | bytes 2621440 | tf_op jit(solution)/shard_map/dot_general | solution.py:199
  3.6 0.9 broadcast_in_dim.8
  4.5 6.9 %all-to-all-start = ((bf16[8,32,1024]{2,1,0:T(8,128)(2,1)}), bf16[8,32,1024]{2,1,0:T(8,128)(2,1)S(1)}, u32[]{:S(2)}, u32[]{:S(2)}) async-start(bf16[8,32,1024]{2,1,0:T(8,128)(2,1)} %bitcast.17), calls=%async_computation | async-start | bytes 1048576 | tf_op jit(solution)/shard_map/all_to_all | solution.py:202
  11.4 0.1 stack.82.place_ref._
  11.5 0.9 shard_map.76
  12.4 0.8 collective-permute-start.3
  13.2 1.9 %collective-permute-start.4 = (bf16[4,224,128]{2,1,0:T(8,128)(2,1)S(1)}, bf16[4,224,128]{2,1,0:T(8,128)(2,1)S(1)}, u32[]{:S(2)}, u32[]{:S(2)}) collective-permute-start(bf16[4,224,128]{2,1,0:T(8,128)(2,1)S(1)} %get-tuple-element.28), channel_id=1, source_target_pairs={{0,16},{16,0},{1,17},{17,1},{2,18},{18,2},{3,19},{19,3},{4,20},{20... | collective-permute-start | bytes 688136 | tf_op jit(solution)/shard_map/ppermute | solution.py:26
  15.1 8.0 %all-to-all-done = bf16[8,32,1024]{2,1,0:T(8,128)(2,1)S(1)} async-done(((bf16[8,32,1024]{2,1,0:T(8,128)(2,1)}), bf16[8,32,1024]{2,1,0:T(8,128)(2,1)S(1)}, u32[]{:S(2)}, u32[]{:S(2)}) %all-to-all-start) | async-done | bytes 524320 | tf_op jit(solution)/shard_map/all_to_all | solution.py:202
  23.1 0.1 reduce_sum.12
  23.1 2.1 %collective-permute-start.2 = (bf16[32,1024]{1,0:T(8,128)(2,1)S(1)}, bf16[32,1024]{1,0:T(8,128)(2,1)S(1)}, u32[]{:S(2)}, u32[]{:S(2)}) collective-permute-start(bf16[32,1024]{1,0:T(8,128)(2,1)S(1)} %reduce_sum.12), channel_id=1, source_target_pairs={{0,144},{16,128},{128,16},{144,0},{1,145},{17,129},{129,17},{145,1... | collective-permute-start | bytes 196616 | tf_op jit(solution)/shard_map/ppermute | solution.py:34
  25.3 0.1 collective-permute-start.1
  25.4 1.3 %collective-permute-start = (bf16[32,1024]{1,0:T(8,128)(2,1)S(1)}, bf16[32,1024]{1,0:T(8,128)(2,1)S(1)}, u32[]{:S(2)}, u32[]{:S(2)}) collective-permute-start(bf16[32,1024]{1,0:T(8,128)(2,1)S(1)} %reduce_sum.12), channel_id=1, source_target_pairs={{0,128},{128,0},{1,129},{129,1},{2,130},{130,2},{3,131},{131,3},{4... | collective-permute-start | bytes 196616 | tf_op jit(solution)/shard_map/ppermute | solution.py:26
  26.7 2.1 %collective-permute-done.2 = bf16[32,1024]{1,0:T(8,128)(2,1)S(1)} collective-permute-done((bf16[32,1024]{1,0:T(8,128)(2,1)S(1)}, bf16[32,1024]{1,0:T(8,128)(2,1)S(1)}, u32[]{:S(2)}, u32[]{:S(2)}) %collective-permute-start.2) | collective-permute-done | bytes 65568 | tf_op jit(solution)/shard_map/ppermute | solution.py:34
  28.8 0.7 collective-permute-done.1
  29.5 0.1 collective-permute-done
  29.7 0.0 collective-permute-done.3
  29.7 0.0 collective-permute-done.4
  29.7 1.4 %collective-permute-start.7 = (bf16[4,32,1024]{2,1,0:T(8,128)(2,1)S(1)}, bf16[4,32,1024]{2,1,0:T(8,128)(2,1)S(1)}, u32[]{:S(2)}, u32[]{:S(2)}) collective-permute-start(bf16[4,32,1024]{2,1,0:T(8,128)(2,1)S(1)} %pad_maximum_fusion.refs_0_), channel_id=1, source_target_pairs={{0,2},{1,3},{2,0},{3,1},{4,6},{5,7},{6,4},{7,5},{8,10},{9,11},{10,... | collective-permute-start | bytes 786440 | tf_op jit(solution)/shard_map/ppermute | solution.py:30
  31.1 2.2 %collective-permute-start.6 = (bf16[4,32,1024]{2,1,0:T(8,128)(2,1)S(1)}, bf16[4,32,1024]{2,1,0:T(8,128)(2,1)S(1)}, u32[]{:S(2)}, u32[]{:S(2)}) collective-permute-start(bf16[4,32,1024]{2,1,0:T(8,128)(2,1)S(1)} %pad_maximum_fusion.refs_0_), channel_id=1, source_target_pairs={{0,3},{1,0},{2,1},{3,2},{4,7},{5,4},{6,5},{7,6},{8,11},{9,8},{10,9... | collective-permute-start | bytes 786440 | tf_op jit(solution)/shard_map/ppermute | solution.py:30
  33.4 0.0 collective-permute-start.5
  33.4 2.7 %collective-permute-start.8 = (bf16[4,224,128]{2,1,0:T(8,128)(2,1)S(1)}, bf16[4,224,128]{2,1,0:T(8,128)(2,1)S(1)}, u32[]{:S(2)}, u32[]{:S(2)}) collective-permute-start(bf16[4,224,128]{2,1,0:T(8,128)(2,1)S(1)} %get-tuple-element.33), channel_id=1, source_target_pairs={{0,144},{16,128},{128,16},{144,0},{1,145},{17,129},{129,17},{145,1... | collective-permute-start | bytes 688136 | tf_op jit(solution)/shard_map/ppermute | solution.py:34
  36.1 4.2 %collective-permute-done.8 = bf16[4,224,128]{2,1,0:T(8,128)(2,1)S(1)} collective-permute-done((bf16[4,224,128]{2,1,0:T(8,128)(2,1)S(1)}, bf16[4,224,128]{2,1,0:T(8,128)(2,1)S(1)}, u32[]{:S(2)}, u32[]{:S(2)}) %collective-permute-start.8) | collective-permute-done | bytes 229408 | tf_op jit(solution)/shard_map/ppermute | solution.py:34
  40.3 0.3 collective-permute-done.7.refs_3_
  40.6 0.0 collective-permute-done.6.refs_2_
  40.6 3.4 %collective-permute-done.5.refs_1_ = bf16[4,32,1024]{2,1,0:T(8,128)(2,1)S(1)} collective-permute-done((bf16[4,32,1024]{2,1,0:T(8,128)(2,1)S(1)}, bf16[4,32,1024]{2,1,0:T(8,128)(2,1)S(1)}, u32[]{:S(2)}, u32[]{:S(2)}) %collective-permute-start.5) | collective-permute-done | bytes 262176 | tf_op jit(solution)/shard_map/ppermute | solution.py:30
  43.9 1.3 %shard_map.77 = (bf16[4,112,1024]{2,1,0:T(8,128)(2,1)S(1)}, bf16[4,4,32,1024]{3,2,1,0:T(8,128)(2,1)S(1)}) custom-call(s32[16]{0:T(128)S(1)} %stack.82.place_ref._, bf16[4,32,1024]{2,1,0:T(8,128)(2,1)S(1)} %pad_maximum_fusion.refs_0_, bf16[4,32,1024]{2,1,0:T(8,128)(2,1)S(1)} %collective-permute-done.5.refs_1_, ...), custom_call_target="tpu_custom_call" | custom-call | tf_op jit(solution)/shard_map/pallas_call | solution.py:223
  45.2 0.1 collective-permute-start.9
  45.3 1.2 %shard_map.78.mine_ref.refs_0_ = f32[4,112,1024]{2,1,0:T(8,128)S(1)} custom-call(s32[16]{0:T(128)S(1)} %stack.82.place_ref._, bf16[4,4,32,1024]{3,2,1,0:T(8,128)(2,1)S(1)} %get-tuple-element.34.whole, bf16[4,2,112,128]{3,2,1,0:T(8,128)(2,1)S(1)} %bitcast.31, bf16[4,2,112,128]{3,2,1,0:T(8,128)(2,1)S(1)} %bitcast.33, bf16[4,2,112,128]{3,2,1,0:T(8,128)(2,1)S(1)} %bitcast.35, ...), custom_call_target="tpu_custom_call" | custom-call | tf_op jit(solution)/shard_map/pallas_call | solution.py:229
  46.5 1.3 %collective-permute-done.9.came_ref.refs_1_ = bf16[4,112,1024]{2,1,0:T(8,128)(2,1)S(1)} collective-permute-done((bf16[4,112,1024]{2,1,0:T(8,128)(2,1)S(1)}, bf16[4,112,1024]{2,1,0:T(8,128)(2,1)S(1)}, u32[]{:S(2)}, u32[]{:S(2)}) %collective-permute-start.9) | collective-permute-done | bytes 917536 | tf_op jit(solution)/shard_map/ppermute | solution.py:26
  47.8 0.6 shard_map.79
  48.4 0.0 copy-start.2
  48.4 0.0 copy-start.3
  48.4 4.0 %collective-permute-start.12 = (bf16[112,512]{1,0:T(8,128)(2,1)S(1)}, bf16[112,512]{1,0:T(8,128)(2,1)S(1)}, u32[]{:S(2)}, u32[]{:S(2)}) collective-permute-start(bf16[112,512]{1,0:T(8,128)(2,1)S(1)} %get-tuple-element.38), channel_id=1, source_target_pairs={{0,32},{32,64},{64,96},{96,0},{1,33},{33,65},{65,97},{97,1},{2,34}... | collective-permute-start | bytes 344072 | tf_op jit(solution)/shard_map/ppermute | solution.py:30
  52.4 0.0 collective-permute-start.13
  52.4 4.1 %collective-permute-start.10 = (bf16[112,512]{1,0:T(8,128)(2,1)S(1)}, bf16[112,512]{1,0:T(8,128)(2,1)S(1)}, u32[]{:S(2)}, u32[]{:S(2)}) collective-permute-start(bf16[112,512]{1,0:T(8,128)(2,1)S(1)} %get-tuple-element.36), channel_id=1, source_target_pairs={{0,32},{32,64},{64,96},{96,0},{1,33},{33,65},{65,97},{97,1},{2,34}... | collective-permute-start | bytes 344072 | tf_op jit(solution)/shard_map/ppermute | solution.py:30
  56.5 0.0 collective-permute-start.11
  56.5 1.7 %collective-permute-done.12.up_ref = bf16[112,512]{1,0:T(8,128)(2,1)S(1)} collective-permute-done((bf16[112,512]{1,0:T(8,128)(2,1)S(1)}, bf16[112,512]{1,0:T(8,128)(2,1)S(1)}, u32[]{:S(2)}, u32[]{:S(2)}) %collective-permute-start.12) | collective-permute-done | bytes 114720 | tf_op jit(solution)/shard_map/ppermute | solution.py:30
  58.2 4.5 %collective-permute-done.13.down_ref = bf16[112,512]{1,0:T(8,128)(2,1)S(1)} collective-permute-done((bf16[112,512]{1,0:T(8,128)(2,1)S(1)}, bf16[112,512]{1,0:T(8,128)(2,1)S(1)}, u32[]{:S(2)}, u32[]{:S(2)}) %collective-permute-start.13) | collective-permute-done | bytes 114720 | tf_op jit(solution)/shard_map/ppermute | solution.py:30
  62.7 0.1 shard_map.80
  62.8 0.8 collective-permute-start.14
  63.5 2.2 %collective-permute-start.15 = (bf16[112,512]{1,0:T(8,128)(2,1)S(1)}, bf16[112,512]{1,0:T(8,128)(2,1)S(1)}, u32[]{:S(2)}, u32[]{:S(2)}) collective-permute-start(bf16[112,512]{1,0:T(8,128)(2,1)S(1)} %get-tuple-element.41), channel_id=1, source_target_pairs={{0,96},{32,0},{64,32},{96,64},{1,97},{33,1},{65,33},{97,65},{2,98}... | collective-permute-start | bytes 344072 | tf_op jit(solution)/shard_map/ppermute | solution.py:30
  65.8 0.0 collective-permute-done.10.refs_2_
  65.8 0.8 collective-permute-done.11.refs_3_
  66.6 2.6 %collective-permute-done.14.refs_4_ = bf16[112,512]{1,0:T(8,128)(2,1)S(1)} collective-permute-done((bf16[112,512]{1,0:T(8,128)(2,1)S(1)}, bf16[112,512]{1,0:T(8,128)(2,1)S(1)}, u32[]{:S(2)}, u32[]{:S(2)}) %collective-permute-start.14) | collective-permute-done | bytes 114720 | tf_op jit(solution)/shard_map/ppermute | solution.py:30
  69.2 2.9 %collective-permute-done.15.refs_5_ = bf16[112,512]{1,0:T(8,128)(2,1)S(1)} collective-permute-done((bf16[112,512]{1,0:T(8,128)(2,1)S(1)}, bf16[112,512]{1,0:T(8,128)(2,1)S(1)}, u32[]{:S(2)}, u32[]{:S(2)}) %collective-permute-start.15) | collective-permute-done | bytes 114720 | tf_op jit(solution)/shard_map/ppermute | solution.py:30
  72.0 0.4 shard_map.81.refs_0_
  72.4 0.0 copy-start.1
  72.4 0.4 collective-permute-start.19
  72.8 4.9 %collective-permute-start.16 = (bf16[112,1024]{1,0:T(8,128)(2,1)S(1)}, bf16[112,1024]{1,0:T(8,128)(2,1)S(1)}, u32[]{:S(2)}, u32[]{:S(2)}) collective-permute-start(bf16[112,1024]{1,0:T(8,128)(2,1)S(1)} %shard_map.81.refs_0_), channel_id=1, source_target_pairs={{0,4},{4,0},{1,5},{5,1},{2,6},{6,2},{3,7},{7,3},{8,12},{12,8},{9,1... | collective-permute-start | bytes 688136 | tf_op jit(solution)/shard_map/ppermute | solution.py:26
  77.7 1.2 %collective-permute-start.22 = (bf16[112,1024]{1,0:T(8,128)(2,1)S(1)}, bf16[112,1024]{1,0:T(8,128)(2,1)S(1)}, u32[]{:S(2)}, u32[]{:S(2)}) collective-permute-start(bf16[112,1024]{1,0:T(8,128)(2,1)S(1)} %shard_map.81.refs_0_), channel_id=1, source_target_pairs={{0,3},{1,0},{2,1},{3,2},{4,7},{5,4},{6,5},{7,6},{8,11},{9,8},{10,9... | collective-permute-start | bytes 688136 | tf_op jit(solution)/shard_map/ppermute | solution.py:30
  79.0 0.8 collective-permute-start.21
  79.8 2.2 %collective-permute-done.19.refs_4_ = bf16[112,1024]{1,0:T(8,128)(2,1)S(1)} collective-permute-done((bf16[112,1024]{1,0:T(8,128)(2,1)S(1)}, bf16[112,1024]{1,0:T(8,128)(2,1)S(1)}, u32[]{:S(2)}, u32[]{:S(2)}) %collective-permute-start.19) | collective-permute-done | bytes 229408 | tf_op jit(solution)/shard_map/ppermute | solution.py:30
  82.0 2.3 %collective-permute-start.20 = (bf16[112,1024]{1,0:T(8,128)(2,1)S(1)}, bf16[112,1024]{1,0:T(8,128)(2,1)S(1)}, u32[]{:S(2)}, u32[]{:S(2)}) collective-permute-start(bf16[112,1024]{1,0:T(8,128)(2,1)S(1)} %collective-permute-done.19.refs_4_), channel_id=1, source_target_pairs={{0,4},{4,0},{1,5},{5,1},{2,6},{6,2},{3,7},{7,3},{8,12},{12,8},{9,1... | collective-permute-start | bytes 688136 | tf_op jit(solution)/shard_map/ppermute | solution.py:26
  84.3 1.9 %collective-permute-start.18 = (bf16[112,1024]{1,0:T(8,128)(2,1)S(1)}, bf16[112,1024]{1,0:T(8,128)(2,1)S(1)}, u32[]{:S(2)}, u32[]{:S(2)}) collective-permute-start(bf16[112,1024]{1,0:T(8,128)(2,1)S(1)} %collective-permute-done.16.refs_1_), channel_id=1, source_target_pairs={{0,3},{1,0},{2,1},{3,2},{4,7},{5,4},{6,5},{7,6},{8,11},{9,8},{10,9... | collective-permute-start | bytes 688136 | tf_op jit(solution)/shard_map/ppermute | solution.py:30
  86.2 0.1 collective-permute-start.17
  86.3 1.1 %shard_map.82 = (f32[1,112,1024]{2,1,0:T(8,128)}, f32[1,112,1024]{2,1,0:T(8,128)}) custom-call(f32[4,112,1024]{2,1,0:T(8,128)S(1)} %shard_map.78.mine_ref.refs_0_, bf16[4,112,1024]{2,1,0:T(8,128)(2,1)S(1)} %collective-permute-done.9.came_ref.refs_1_, bf16[112,512]{1,0:T(8,128)(2,1)S(1)} %collective-permute-done.10.refs_2_, ...), custom_call_target="tpu_custom_call" | custom-call | tf_op jit(solution)/shard_map/pallas_call | solution.py:251
  87.4 0.0 collective-permute-done.22.refs_3_
  87.4 0.7 collective-permute-done.21.refs_2_
  88.1 2.8 %shard_map.83.refs_3_ = bf16[8,112,1024]{2,1,0:T(8,128)(2,1)} custom-call(s32[16]{0:T(128)S(1)} %stack.82.place_ref._, bf16[1024,1024]{1,0:T(8,128)(2,1)S(1)} %copy-done.1, bf16[112,1024]{1,0:T(8,128)(2,1)S(1)} %shard_map.81.refs_0_, bf16[112,1024]{1,0:T(8,128)(2,1)S(1)} %collective-permute-done.16.refs_1_, ...), custom_call_target="tpu_custom_call" | custom-call | tf_op jit(solution)/shard_map/pallas_call | solution.py:161
  90.9 0.0 collective-permute-done.18.refs_1_
  91.0 2.5 %collective-permute-done.17.refs_0_ = bf16[112,1024]{1,0:T(8,128)(2,1)S(1)} collective-permute-done((bf16[112,1024]{1,0:T(8,128)(2,1)S(1)}, bf16[112,1024]{1,0:T(8,128)(2,1)S(1)}, u32[]{:S(2)}, u32[]{:S(2)}) %collective-permute-start.17) | collective-permute-done | bytes 229408 | tf_op jit(solution)/shard_map/ppermute | solution.py:30
  93.4 2.2 %shard_map.84 = bf16[8,112,1024]{2,1,0:T(8,128)(2,1)} custom-call(s32[16]{0:T(128)S(1)} %stack.82.place_ref._, bf16[1024,1024]{1,0:T(8,128)(2,1)S(1)} %copy-done.1, bf16[112,1024]{1,0:T(8,128)(2,1)S(1)} %collective-permute-done.17.refs_0_, bf16[112,1024]{1,0:T(8,128)(2,1)S(1)} %collective-permute-done.18.refs_1_, ...), custom_call_target="tpu_custom_call", output_to_operand_aliasing={{}: (5, {})} | custom-call | tf_op jit(solution)/shard_map/pallas_call | solution.py:161
  (8 shorter events, 0.1 us)
Async XLA Ops:
  0.6 1.0 copy-start
  0.6 10.9 %copy-start.4 = (bf16[128,1,3584]{2,0,1:T(8,128)(2,1)S(1)}, bf16[128,1,3584]{2,0,1:T(8,128)(2,1)}, u32[]{:S(2)}) copy-start(bf16[128,1,3584]{2,0,1:T(8,128)(2,1)} %param.7) | copy-start | bytes 2752516
  4.5 18.6 %all-to-all-start = ((bf16[8,32,1024]{2,1,0:T(8,128)(2,1)}), bf16[8,32,1024]{2,1,0:T(8,128)(2,1)S(1)}, u32[]{:S(2)}, u32[]{:S(2)}) async-start(bf16[8,32,1024]{2,1,0:T(8,128)(2,1)} %bitcast.17), calls=%async_computation | async-start | bytes 1048576 | tf_op jit(solution)/shard_map/all_to_all | solution.py:202
  12.4 17.3 %collective-permute-start.3 = (bf16[4,224,128]{2,1,0:T(8,128)(2,1)S(1)}, bf16[4,224,128]{2,1,0:T(8,128)(2,1)S(1)}, u32[]{:S(2)}, u32[]{:S(2)}) collective-permute-start(bf16[4,224,128]{2,1,0:T(8,128)(2,1)S(1)} %get-tuple-element.27), channel_id=1, source_target_pairs={{0,128},{128,0},{1,129},{129,1},{2,130},{130,2},{3,131},{131,3},{4... | collective-permute-start | bytes 688136 | tf_op jit(solution)/shard_map/ppermute | solution.py:26
  13.2 16.5 %collective-permute-start.4 = (bf16[4,224,128]{2,1,0:T(8,128)(2,1)S(1)}, bf16[4,224,128]{2,1,0:T(8,128)(2,1)S(1)}, u32[]{:S(2)}, u32[]{:S(2)}) collective-permute-start(bf16[4,224,128]{2,1,0:T(8,128)(2,1)S(1)} %get-tuple-element.28), channel_id=1, source_target_pairs={{0,16},{16,0},{1,17},{17,1},{2,18},{18,2},{3,19},{19,3},{4,20},{20... | collective-permute-start | bytes 688136 | tf_op jit(solution)/shard_map/ppermute | solution.py:26
  23.1 5.7 %collective-permute-start.2 = (bf16[32,1024]{1,0:T(8,128)(2,1)S(1)}, bf16[32,1024]{1,0:T(8,128)(2,1)S(1)}, u32[]{:S(2)}, u32[]{:S(2)}) collective-permute-start(bf16[32,1024]{1,0:T(8,128)(2,1)S(1)} %reduce_sum.12), channel_id=1, source_target_pairs={{0,144},{16,128},{128,16},{144,0},{1,145},{17,129},{129,17},{145,1... | collective-permute-start | bytes 196616 | tf_op jit(solution)/shard_map/ppermute | solution.py:34
  25.3 4.3 %collective-permute-start.1 = (bf16[32,1024]{1,0:T(8,128)(2,1)S(1)}, bf16[32,1024]{1,0:T(8,128)(2,1)S(1)}, u32[]{:S(2)}, u32[]{:S(2)}) collective-permute-start(bf16[32,1024]{1,0:T(8,128)(2,1)S(1)} %reduce_sum.12), channel_id=1, source_target_pairs={{0,16},{16,0},{1,17},{17,1},{2,18},{18,2},{3,19},{19,3},{4,20},{20... | collective-permute-start | bytes 196616 | tf_op jit(solution)/shard_map/ppermute | solution.py:26
  25.4 4.3 %collective-permute-start = (bf16[32,1024]{1,0:T(8,128)(2,1)S(1)}, bf16[32,1024]{1,0:T(8,128)(2,1)S(1)}, u32[]{:S(2)}, u32[]{:S(2)}) collective-permute-start(bf16[32,1024]{1,0:T(8,128)(2,1)S(1)} %reduce_sum.12), channel_id=1, source_target_pairs={{0,128},{128,0},{1,129},{129,1},{2,130},{130,2},{3,131},{131,3},{4... | collective-permute-start | bytes 196616 | tf_op jit(solution)/shard_map/ppermute | solution.py:26
  29.7 10.9 %collective-permute-start.7 = (bf16[4,32,1024]{2,1,0:T(8,128)(2,1)S(1)}, bf16[4,32,1024]{2,1,0:T(8,128)(2,1)S(1)}, u32[]{:S(2)}, u32[]{:S(2)}) collective-permute-start(bf16[4,32,1024]{2,1,0:T(8,128)(2,1)S(1)} %pad_maximum_fusion.refs_0_), channel_id=1, source_target_pairs={{0,2},{1,3},{2,0},{3,1},{4,6},{5,7},{6,4},{7,5},{8,10},{9,11},{10,... | collective-permute-start | bytes 786440 | tf_op jit(solution)/shard_map/ppermute | solution.py:30
  31.1 9.4 %collective-permute-start.6 = (bf16[4,32,1024]{2,1,0:T(8,128)(2,1)S(1)}, bf16[4,32,1024]{2,1,0:T(8,128)(2,1)S(1)}, u32[]{:S(2)}, u32[]{:S(2)}) collective-permute-start(bf16[4,32,1024]{2,1,0:T(8,128)(2,1)S(1)} %pad_maximum_fusion.refs_0_), channel_id=1, source_target_pairs={{0,3},{1,0},{2,1},{3,2},{4,7},{5,4},{6,5},{7,6},{8,11},{9,8},{10,9... | collective-permute-start | bytes 786440 | tf_op jit(solution)/shard_map/ppermute | solution.py:30
  33.4 10.6 %collective-permute-start.5 = (bf16[4,32,1024]{2,1,0:T(8,128)(2,1)S(1)}, bf16[4,32,1024]{2,1,0:T(8,128)(2,1)S(1)}, u32[]{:S(2)}, u32[]{:S(2)}) collective-permute-start(bf16[4,32,1024]{2,1,0:T(8,128)(2,1)S(1)} %pad_maximum_fusion.refs_0_), channel_id=1, source_target_pairs={{0,1},{1,2},{2,3},{3,0},{4,5},{5,6},{6,7},{7,4},{8,9},{9,10},{10,1... | collective-permute-start | bytes 786440 | tf_op jit(solution)/shard_map/ppermute | solution.py:30
  33.4 6.9 %collective-permute-start.8 = (bf16[4,224,128]{2,1,0:T(8,128)(2,1)S(1)}, bf16[4,224,128]{2,1,0:T(8,128)(2,1)S(1)}, u32[]{:S(2)}, u32[]{:S(2)}) collective-permute-start(bf16[4,224,128]{2,1,0:T(8,128)(2,1)S(1)} %get-tuple-element.33), channel_id=1, source_target_pairs={{0,144},{16,128},{128,16},{144,0},{1,145},{17,129},{129,17},{145,1... | collective-permute-start | bytes 688136 | tf_op jit(solution)/shard_map/ppermute | solution.py:34
  45.2 2.6 %collective-permute-start.9 = (bf16[4,112,1024]{2,1,0:T(8,128)(2,1)S(1)}, bf16[4,112,1024]{2,1,0:T(8,128)(2,1)S(1)}, u32[]{:S(2)}, u32[]{:S(2)}) collective-permute-start(bf16[4,112,1024]{2,1,0:T(8,128)(2,1)S(1)} %get-tuple-element.35), channel_id=1, source_target_pairs={{0,8},{8,0},{1,9},{9,1},{2,10},{10,2},{3,11},{11,3},{4,12},{12,4},... | collective-permute-start | bytes 2752520 | tf_op jit(solution)/shard_map/ppermute | solution.py:26
  48.4 23.6 %copy-start.2 = (f32[1,112,1024]{2,1,0:T(8,128)S(1)}, f32[1,112,1024]{2,1,0:T(8,128)}, u32[]{:S(2)}) copy-start(f32[1,112,1024]{2,1,0:T(8,128)} %refs_6_.3) | copy-start | bytes 1376260
  48.4 23.6 %copy-start.3 = (f32[1,112,1024]{2,1,0:T(8,128)S(1)}, f32[1,112,1024]{2,1,0:T(8,128)}, u32[]{:S(2)}) copy-start(f32[1,112,1024]{2,1,0:T(8,128)} %refs_7_.3) | copy-start | bytes 1376260
  48.4 9.8 %collective-permute-start.12 = (bf16[112,512]{1,0:T(8,128)(2,1)S(1)}, bf16[112,512]{1,0:T(8,128)(2,1)S(1)}, u32[]{:S(2)}, u32[]{:S(2)}) collective-permute-start(bf16[112,512]{1,0:T(8,128)(2,1)S(1)} %get-tuple-element.38), channel_id=1, source_target_pairs={{0,32},{32,64},{64,96},{96,0},{1,33},{33,65},{65,97},{97,1},{2,34}... | collective-permute-start | bytes 344072 | tf_op jit(solution)/shard_map/ppermute | solution.py:30
  52.4 10.3 %collective-permute-start.13 = (bf16[112,512]{1,0:T(8,128)(2,1)S(1)}, bf16[112,512]{1,0:T(8,128)(2,1)S(1)}, u32[]{:S(2)}, u32[]{:S(2)}) collective-permute-start(bf16[112,512]{1,0:T(8,128)(2,1)S(1)} %get-tuple-element.39), channel_id=1, source_target_pairs={{0,96},{32,0},{64,32},{96,64},{1,97},{33,1},{65,33},{97,65},{2,98}... | collective-permute-start | bytes 344072 | tf_op jit(solution)/shard_map/ppermute | solution.py:30
  52.4 13.4 %collective-permute-start.10 = (bf16[112,512]{1,0:T(8,128)(2,1)S(1)}, bf16[112,512]{1,0:T(8,128)(2,1)S(1)}, u32[]{:S(2)}, u32[]{:S(2)}) collective-permute-start(bf16[112,512]{1,0:T(8,128)(2,1)S(1)} %get-tuple-element.36), channel_id=1, source_target_pairs={{0,32},{32,64},{64,96},{96,0},{1,33},{33,65},{65,97},{97,1},{2,34}... | collective-permute-start | bytes 344072 | tf_op jit(solution)/shard_map/ppermute | solution.py:30
  56.5 10.1 %collective-permute-start.11 = (bf16[112,512]{1,0:T(8,128)(2,1)S(1)}, bf16[112,512]{1,0:T(8,128)(2,1)S(1)}, u32[]{:S(2)}, u32[]{:S(2)}) collective-permute-start(bf16[112,512]{1,0:T(8,128)(2,1)S(1)} %get-tuple-element.37), channel_id=1, source_target_pairs={{0,96},{32,0},{64,32},{96,64},{1,97},{33,1},{65,33},{97,65},{2,98}... | collective-permute-start | bytes 344072 | tf_op jit(solution)/shard_map/ppermute | solution.py:30
  62.8 6.4 %collective-permute-start.14 = (bf16[112,512]{1,0:T(8,128)(2,1)S(1)}, bf16[112,512]{1,0:T(8,128)(2,1)S(1)}, u32[]{:S(2)}, u32[]{:S(2)}) collective-permute-start(bf16[112,512]{1,0:T(8,128)(2,1)S(1)} %get-tuple-element.40), channel_id=1, source_target_pairs={{0,32},{32,64},{64,96},{96,0},{1,33},{33,65},{65,97},{97,1},{2,34}... | collective-permute-start | bytes 344072 | tf_op jit(solution)/shard_map/ppermute | solution.py:30
  63.5 8.5 %collective-permute-start.15 = (bf16[112,512]{1,0:T(8,128)(2,1)S(1)}, bf16[112,512]{1,0:T(8,128)(2,1)S(1)}, u32[]{:S(2)}, u32[]{:S(2)}) collective-permute-start(bf16[112,512]{1,0:T(8,128)(2,1)S(1)} %get-tuple-element.41), channel_id=1, source_target_pairs={{0,96},{32,0},{64,32},{96,64},{1,97},{33,1},{65,33},{97,65},{2,98}... | collective-permute-start | bytes 344072 | tf_op jit(solution)/shard_map/ppermute | solution.py:30
  72.4 15.7 %copy-start.1 = (bf16[1024,1024]{1,0:T(8,128)(2,1)S(1)}, bf16[1024,1024]{1,0:T(8,128)(2,1)}, u32[]{:S(2)}) copy-start(bf16[1024,1024]{1,0:T(8,128)(2,1)} %projector_ref.3) | copy-start | bytes 6291460
  72.4 9.6 %collective-permute-start.19 = (bf16[112,1024]{1,0:T(8,128)(2,1)S(1)}, bf16[112,1024]{1,0:T(8,128)(2,1)S(1)}, u32[]{:S(2)}, u32[]{:S(2)}) collective-permute-start(bf16[112,1024]{1,0:T(8,128)(2,1)S(1)} %shard_map.81.refs_0_), channel_id=1, source_target_pairs={{0,2},{1,3},{2,0},{3,1},{4,6},{5,7},{6,4},{7,5},{8,10},{9,11},{10,... | collective-permute-start | bytes 688136 | tf_op jit(solution)/shard_map/ppermute | solution.py:30
  72.8 11.5 %collective-permute-start.16 = (bf16[112,1024]{1,0:T(8,128)(2,1)S(1)}, bf16[112,1024]{1,0:T(8,128)(2,1)S(1)}, u32[]{:S(2)}, u32[]{:S(2)}) collective-permute-start(bf16[112,1024]{1,0:T(8,128)(2,1)S(1)} %shard_map.81.refs_0_), channel_id=1, source_target_pairs={{0,4},{4,0},{1,5},{5,1},{2,6},{6,2},{3,7},{7,3},{8,12},{12,8},{9,1... | collective-permute-start | bytes 688136 | tf_op jit(solution)/shard_map/ppermute | solution.py:26
  77.7 9.7 %collective-permute-start.22 = (bf16[112,1024]{1,0:T(8,128)(2,1)S(1)}, bf16[112,1024]{1,0:T(8,128)(2,1)S(1)}, u32[]{:S(2)}, u32[]{:S(2)}) collective-permute-start(bf16[112,1024]{1,0:T(8,128)(2,1)S(1)} %shard_map.81.refs_0_), channel_id=1, source_target_pairs={{0,3},{1,0},{2,1},{3,2},{4,7},{5,4},{6,5},{7,6},{8,11},{9,8},{10,9... | collective-permute-start | bytes 688136 | tf_op jit(solution)/shard_map/ppermute | solution.py:30
  79.0 9.1 %collective-permute-start.21 = (bf16[112,1024]{1,0:T(8,128)(2,1)S(1)}, bf16[112,1024]{1,0:T(8,128)(2,1)S(1)}, u32[]{:S(2)}, u32[]{:S(2)}) collective-permute-start(bf16[112,1024]{1,0:T(8,128)(2,1)S(1)} %shard_map.81.refs_0_), channel_id=1, source_target_pairs={{0,1},{1,2},{2,3},{3,0},{4,5},{5,6},{6,7},{7,4},{8,9},{9,10},{10,1... | collective-permute-start | bytes 688136 | tf_op jit(solution)/shard_map/ppermute | solution.py:30
  82.0 8.9 %collective-permute-start.20 = (bf16[112,1024]{1,0:T(8,128)(2,1)S(1)}, bf16[112,1024]{1,0:T(8,128)(2,1)S(1)}, u32[]{:S(2)}, u32[]{:S(2)}) collective-permute-start(bf16[112,1024]{1,0:T(8,128)(2,1)S(1)} %collective-permute-done.19.refs_4_), channel_id=1, source_target_pairs={{0,4},{4,0},{1,5},{5,1},{2,6},{6,2},{3,7},{7,3},{8,12},{12,8},{9,1... | collective-permute-start | bytes 688136 | tf_op jit(solution)/shard_map/ppermute | solution.py:26
  84.3 6.6 %collective-permute-start.18 = (bf16[112,1024]{1,0:T(8,128)(2,1)S(1)}, bf16[112,1024]{1,0:T(8,128)(2,1)S(1)}, u32[]{:S(2)}, u32[]{:S(2)}) collective-permute-start(bf16[112,1024]{1,0:T(8,128)(2,1)S(1)} %collective-permute-done.16.refs_1_), channel_id=1, source_target_pairs={{0,3},{1,0},{2,1},{3,2},{4,7},{5,4},{6,5},{7,6},{8,11},{9,8},{10,9... | collective-permute-start | bytes 688136 | tf_op jit(solution)/shard_map/ppermute | solution.py:30
  86.2 7.2 %collective-permute-start.17 = (bf16[112,1024]{1,0:T(8,128)(2,1)S(1)}, bf16[112,1024]{1,0:T(8,128)(2,1)S(1)}, u32[]{:S(2)}, u32[]{:S(2)}) collective-permute-start(bf16[112,1024]{1,0:T(8,128)(2,1)S(1)} %collective-permute-done.16.refs_1_), channel_id=1, source_target_pairs={{0,1},{1,2},{2,3},{3,0},{4,5},{5,6},{6,7},{7,4},{8,9},{9,10},{10,1... | collective-permute-start | bytes 688136 | tf_op jit(solution)/shard_map/ppermute | solution.py:30
